TPU v7x, 256 devices: a whole 4x4x8 slice. The times are simulated.
256 devices in a mesh: dp: 16 (over z_lo, y, core), tensor: 16 (over z_hi, x).
Axes of the slice: x: 4, y: 4, z: 8 (z_hi: 4, z_lo: 2; z = z_hi * 2 + z_lo), core: 2. Of those that a mesh axis runs over, the one named last changes fastest.
Arguments:
- query: bfloat16 [16384, 8192], P('dp', 'tensor'), may hold values from -144 to 144
- key_value: bfloat16 [2, 16384, 1024], P(None, 'dp'), may hold values from -6 to 6
- residual: bfloat16 [16384, 4096], P('dp', 'tensor'), may hold values from -2.7 to 2.7
- out_weight: bfloat16 [8192, 4096], P('tensor'), may hold values from -0.09375 to 0.09375
- norm_gain: bfloat16 [4096], replicated, may hold values from 0.099609375 to 1.8984375
- doc_ids: int32 [16, 1024], replicated, may hold values from 0 to 15, as said below
Outputs:
- hidden: bfloat16 [16384, 4096], P('dp', 'tensor')
- normed: bfloat16 [16384, 4096], P('dp', 'tensor')
Inputs may be any that keep to these rules, and one draw needn't show every extreme that they name: `doc_ids`: numbers start at 0 in each row and never fall along it; every sequence has a length that is a multiple of 64; in every draw some row holds a single sequence of 1024 tokens and some row holds only sequences of 64 tokens.
All inputs are finite; a program needn't handle non-finite values.
Results may differ from a plain program's by a relative error of at most 0.017.
Values may be sent and summed in bfloat16 or wider, within the bound.
No kernel may reach another device: no remote copies, remote signals or barrier semaphores. Data moves between devices by JAX's collectives and lax.ppermute only.
A program may use at most 64 MiB of HBM per device.

v0:
```python
import math

import jax
import jax.numpy as jnp
from jax import lax
from jax.sharding import PartitionSpec as P

D = 4096
HEADS = 64
KVH = 8
HD = 128
BLK = 256


MASK_FILL = -1e30
EPSILON = 1e-06


def partner_2(block, axis, apart):
    count = lax.axis_size(axis)
    route = []
    for low in range(count):
        high = low | 1 << apart
        if high != low and high < count:
            route += [(low, high), (high, low)]
    return lax.ppermute(block, axis, route)


def block_starts(doc_row):
    block_count = doc_row.shape[0] // BLK
    lead_docs = doc_row.reshape(block_count, BLK)[:, 0]
    starts = jnp.sum((doc_row[None, :] < lead_docs[:, None]).astype(jnp.int32), axis=1)
    return starts // BLK


def plan_blocks(packed, capacity):
    group_count, row_total = packed.shape
    block_count = row_total // BLK
    positions = jnp.arange(row_total, dtype=jnp.int32)[None, :]
    earlier = jnp.concatenate([jnp.full((group_count, 1), -1, jnp.int32), packed[:, :-1]], axis=1)
    boundary = jnp.where(packed != earlier, positions, 0)
    doc_start = lax.cummax(boundary, axis=1)
    depth = positions - doc_start + 1
    block_cost = jnp.sum(depth.reshape(group_count, block_count, BLK), axis=2)
    group_load = jnp.sum(block_cost, axis=1)
    group_ids = jnp.arange(group_count, dtype=jnp.int32)
    block_ids = jnp.arange(block_count, dtype=jnp.int32)
    destination = jnp.broadcast_to(group_ids[:, None], (group_count, block_count))
    still_kept = jnp.ones((group_count, block_count), dtype=bool)
    for bit_index in range(group_count.bit_length() - 1):
        partner = jnp.bitwise_xor(group_ids, 1 << bit_index)
        load_gap = group_load - group_load[partner]
        rank_score = jnp.where(still_kept, block_cost * block_count + block_ids[None, :], -1)
        sorted_score, sorted_ids = lax.top_k(rank_score, block_count)
        available = sorted_score >= 0
        sorted_cost = jnp.where(available, sorted_score // block_count, 0)
        running = jnp.cumsum(sorted_cost, axis=1)
        fitting = jnp.sum(
            (available & (2 * running <= load_gap[:, None])).astype(jnp.int32), axis=1
        )
        hand_count = jnp.minimum(jnp.maximum(fitting, 1), capacity)
        hand_count = jnp.minimum(hand_count, jnp.sum(available.astype(jnp.int32), axis=1))
        hand_count = jnp.where(load_gap > 0, hand_count, 0)
        chosen_sorted = block_ids[None, :] < hand_count[:, None]
        chosen = jnp.any(
            (sorted_ids[:, :, None] == block_ids[None, None, :]) & chosen_sorted[:, :, None], axis=1
        )
        moved = jnp.sum(jnp.where(chosen, block_cost, 0), axis=1)
        destination = jnp.where(chosen, partner[:, None], destination)
        still_kept = still_kept & jnp.logical_not(chosen)
        group_load = group_load - moved + moved[partner]
    return destination


def pick_slots(selected, capacity):
    order_rank = jnp.cumsum(selected.astype(jnp.int32)) - 1
    block_ids = jnp.arange(selected.shape[0], dtype=jnp.int32)
    matches = selected[None, :] & (
        order_rank[None, :] == jnp.arange(capacity, dtype=jnp.int32)[:, None]
    )
    slot_blocks = jnp.sum(jnp.where(matches, block_ids[None, :], 0), axis=1)
    return (slot_blocks, jnp.any(matches, axis=1))


def attend_block(q_rows, q_docs, q_pos, pairs, pair_docs, first_block, last_block):
    rows_here = q_rows.shape[0]
    head_dim = pairs.shape[1] // 2
    head_count = q_rows.shape[1] // head_dim
    q_heads = q_rows.reshape(rows_here, head_count, head_dim)
    score_scale = 1.0 / math.sqrt(head_dim)

    def visit_tile(tile_index, carry):
        run_peak, run_total, run_sum = carry
        key_tile = lax.dynamic_slice_in_dim(pairs, tile_index * rows_here, rows_here, 0)
        key_docs = lax.dynamic_slice_in_dim(pair_docs, tile_index * rows_here, rows_here, 0)
        key_pos = tile_index * rows_here + jnp.arange(rows_here, dtype=jnp.int32)
        scores = (
            jnp.einsum(
                "qhd,kd->hqk", q_heads, key_tile[:, :head_dim], preferred_element_type=jnp.float32
            )
            * score_scale
        )
        allowed = (q_docs[:, None] == key_docs[None, :]) & (key_pos[None, :] <= q_pos[:, None])
        scores = jnp.where(allowed[None], scores, MASK_FILL)
        new_peak = jnp.maximum(run_peak, jnp.max(scores, axis=2))
        weights = jnp.where(allowed[None], jnp.exp(scores - new_peak[:, :, None]), 0.0)
        factor = jnp.exp(run_peak - new_peak)
        run_total = run_total * factor + jnp.sum(weights, axis=2)
        run_sum = run_sum * factor[:, :, None] + jnp.einsum(
            "hqk,kd->hqd",
            weights.astype(jnp.bfloat16),
            key_tile[:, head_dim:],
            preferred_element_type=jnp.float32,
        )
        return (new_peak, run_total, run_sum)

    start_state = (
        jnp.full((head_count, rows_here), MASK_FILL, jnp.float32),
        jnp.zeros((head_count, rows_here), jnp.float32),
        jnp.zeros((head_count, rows_here, head_dim), jnp.float32),
    )
    run_peak, run_total, run_sum = lax.fori_loop(
        first_block, last_block + 1, visit_tile, start_state
    )
    run_total = jnp.where(run_total > 0.0, run_total, 1.0)
    result = (run_sum / run_total[:, :, None]).astype(jnp.bfloat16)
    return result.transpose(1, 0, 2).reshape(rows_here, head_count * head_dim)


def body(query, key_value, residual, out_weight, norm_gain, doc_ids):
    row_count, columns = query.shape
    block_count = row_count // BLK
    capacity = max(1, block_count // 4)
    heads_here = columns // HD
    tensor_index = lax.axis_index("tensor")
    group_index = lax.axis_index("dp")
    kv_column = tensor_index * heads_here // (HEADS // KVH) * HD
    own_pairs = jnp.concatenate(
        [
            lax.dynamic_slice_in_dim(key_value[0], kv_column, HD, 1),
            lax.dynamic_slice_in_dim(key_value[1], kv_column, HD, 1),
        ],
        axis=1,
    )
    own_docs = doc_ids[group_index]
    own_first = block_starts(own_docs)
    query_blocks = query.reshape(block_count, BLK, columns)
    offsets = jnp.arange(BLK, dtype=jnp.int32)
    block_dest = plan_blocks(doc_ids, capacity)
    own_dest = block_dest[group_index]
    stays_home = own_dest == group_index
    outputs = []
    for block_index in range(block_count):
        last_block = jnp.where(stays_home[block_index], block_index, own_first[block_index] - 1)
        outputs.append(
            attend_block(
                query_blocks[block_index],
                own_docs[block_index * BLK : (block_index + 1) * BLK],
                block_index * BLK + offsets,
                own_pairs,
                own_docs,
                own_first[block_index],
                last_block,
            )
        )
    attention = jnp.stack(outputs)
    for bit_index in range(lax.axis_size("dp").bit_length() - 1):
        partner = jnp.bitwise_xor(group_index, 1 << bit_index)
        send_blocks, send_valid = pick_slots(own_dest == partner, capacity)
        take_blocks, take_valid = pick_slots(block_dest[partner] == group_index, capacity)
        sent_rows = jnp.take(query_blocks, send_blocks, axis=0).reshape(capacity * BLK, columns)
        guest_rows, guest_pairs = partner_2((sent_rows, own_pairs), "dp", bit_index)
        guest_docs = doc_ids[partner]
        guest_first = block_starts(guest_docs)
        slot_index = 0
        slot_block = take_blocks[slot_index]
        first_block = guest_first[slot_block]
        last_block = jnp.where(take_valid[slot_index], slot_block, first_block - 1)
        answers = [
            attend_block(
                guest_rows,
                lax.dynamic_slice_in_dim(guest_docs, slot_block * BLK, BLK, 0),
                slot_block * BLK + offsets,
                guest_pairs,
                guest_docs,
                first_block,
                last_block,
            )
        ]
        returned = partner_2(jnp.stack(answers), "dp", bit_index)
        slot_index = 0
        landing = (
            jnp.arange(block_count, dtype=jnp.int32) == send_blocks[slot_index]
        ) & send_valid[slot_index]
        attention = jnp.where(landing[:, None, None], returned[slot_index][None], attention)
    attn_rows = attention.reshape(row_count, columns)
    feature_count = residual.shape[1]
    partial_value = jnp.dot(attn_rows, out_weight, preferred_element_type=jnp.float32)
    mixed = lax.psum_scatter(
        partial_value.astype(jnp.bfloat16), "tensor", scatter_dimension=1, tiled=True
    ).astype(jnp.float32)
    hidden = (residual.astype(jnp.float32) + mixed).astype(jnp.bfloat16)
    widened = hidden.astype(jnp.float32)
    squares = lax.psum(jnp.sum(widened * widened, axis=1), "tensor")
    gain_part = lax.dynamic_slice_in_dim(norm_gain, tensor_index * feature_count, feature_count, 0)
    normed = (
        widened * lax.rsqrt(squares / D + EPSILON)[:, None] * gain_part.astype(jnp.float32)
    ).astype(jnp.bfloat16)
    return (hidden, normed)


def solution(mesh):
    placed = (
        P("dp", "tensor"),
        P(None, "dp", None),
        P("dp", "tensor"),
        P("tensor", None),
        P(),
        P(),
    )
    return jax.shard_map(
        body,
        mesh=mesh,
        in_specs=placed,
        out_specs=(P("dp", "tensor"), P("dp", "tensor")),
        check_vma=False,
    )
```

profile of v0, /device:TPU:16, one launch (start us, length us, event | category | flops | bytes accessed | tf_op | source)
XLA Modules:
  0.0 378.7 jit_solution(2411701644651987344)
XLA Ops:
  8.4 4.5 %reduce-window.18 = s32[16,8,128]{2,1,0:T(8,128)S(1)} reduce-window(s32[16,8,128]{2,1,0:T(8,128)S(1)} %bitcast.287, s32[]{:T(128)} %constant.347.clone.1), window={size=1x1x128 pad=0_0x0_0x127_0}, to_apply=%region_0.1 | reduce-window | flops 2080768 | bytes 131076 | tf_op jit(solution)/shard_map/reduce-window
  20.0 1.2 select_reduce_fusion.5
  30.6 1.9 collective-permute-start.1
  32.5 4.0 %fusion.182 = (bf16[1,1024,1024]{2,1,0:T(8,128)(2,1)S(1)}, bf16[1,1024,1024]{2,1,0:T(8,128)(2,1)}) fusion(bf16[2,1024,1024]{2,1,0:T(8,128)(2,1)} %param.25), kind=kLoop, calls=%fused_computation.415 | loop fusion | bytes 8388608 | tf_op jit(solution)/shard_map/slice | solution.py:140
  38.5 2.1 collective-permute-start.4
  48.5 1.6 fusion.149
  56.8 5.8 %while.125 = (s32[]{:T(128)}, f32[4,256]{1,0:T(4,128)S(1)}, f32[4,256]{1,0:T(4,128)S(1)}, f32[4,256,128]{2,1,0:T(8,128)S(1)}, s32[]{:T(128)}, /*index=5*/s32[256...) while((s32[]{:T(128)}, f32[4,256]{1,0:T(4,128)S(1)}, ...), condition=%wide.region_76.78_spmd.clone, body=%wide.region_73.77_spmd.clone.sunk | while | flops 137038080 | bytes 4921555 | solution.py:122
  58.2 1.2 fusion.249
  59.6 1.3 convolution_add_fusion.20
  64.4 5.8 %while.126 = (s32[]{:T(128)}, f32[4,256]{1,0:T(4,128)S(1)}, f32[4,256]{1,0:T(4,128)S(1)}, f32[4,256,128]{2,1,0:T(8,128)S(1)}, s32[]{:T(128)}, /*index=5*/s32[256...) while((s32[]{:T(128)}, f32[4,256]{1,0:T(4,128)S(1)}, ...), condition=%wide.region_80.82_spmd.clone, body=%wide.region_77.81_spmd.clone.sunk | while | flops 137038336 | bytes 4923603 | solution.py:122
  65.8 1.2 fusion.253
  67.2 1.3 convolution_add_fusion.21
  94.9 1.2 compare_and_fusion.10
  96.2 1.1 pad_maximum_fusion
  97.3 6.9 %collective-permute-start.3 = (bf16[1024,256]{1,0:T(8,128)(2,1)}, bf16[1024,256]{1,0:T(8,128)(2,1)}, u32[]{:S(2)}, u32[]{:S(2)}) collective-permute-start(bf16[1024,256]{1,0:T(8,128)(2,1)} %pad_maximum_fusion.1), channel_id=1, source_target_pairs={{0,64},{64,0},{16,80},{80,16},{32,96},{96,32},{48,112},{112,48},{1... | collective-permute-start | bytes 1572872 | tf_op jit(solution)/shard_map/ppermute | solution.py:26
  105.5 21.5 %collective-permute-start.6 = (bf16[1024,256]{1,0:T(8,128)(2,1)}, bf16[1024,256]{1,0:T(8,128)(2,1)}, u32[]{:S(2)}, u32[]{:S(2)}) collective-permute-start(bf16[1024,256]{1,0:T(8,128)(2,1)} %pad_maximum_fusion.1), channel_id=1, source_target_pairs={{0,32},{32,0},{16,48},{48,16},{64,96},{96,64},{80,112},{112,80},{1... | collective-permute-start | bytes 1572872 | tf_op jit(solution)/shard_map/ppermute | solution.py:26
  131.0 10.9 %while.121 = (s32[]{:T(128)}, f32[4,256]{1,0:T(4,128)S(1)}, f32[4,256]{1,0:T(4,128)S(1)}, f32[4,256,128]{2,1,0:T(8,128)S(1)}, s32[]{:T(128)}, /*index=5*/s32[256...) while((s32[]{:T(128)}, f32[4,256]{1,0:T(4,128)S(1)}, ...), condition=%wide.region_38.40_spmd.clone, body=%wide.region_35.39_spmd.clone.sunk | while | flops 137038336 | bytes 4923615 | solution.py:122
  132.4 1.2 fusion.232
  133.8 1.3 convolution_add_fusion.16
  137.5 1.2 fusion.232
  139.0 1.3 convolution_add_fusion.16
  144.6 13.6 %collective-permute-start.5 = (bf16[1,256,512]{1,2,0:T(8,128)(2,1)}, bf16[1,256,512]{1,2,0:T(8,128)(2,1)}, u32[]{:S(2)}, u32[]{:S(2)}) collective-permute-start(bf16[1,256,512]{1,2,0:T(8,128)(2,1)} %bitcast.31), channel_id=1, source_target_pairs={{0,64},{64,0},{16,80},{80,16},{32,96},{96,32},{48,112},{112,48},{1... | collective-permute-start | bytes 786440 | tf_op jit(solution)/shard_map/ppermute | solution.py:26
  159.9 8.3 %collective-permute-start.8 = (bf16[1,256,512]{1,2,0:T(8,128)(2,1)}, bf16[1,256,512]{1,2,0:T(8,128)(2,1)}, u32[]{:S(2)}, u32[]{:S(2)}) collective-permute-start(bf16[1,256,512]{1,2,0:T(8,128)(2,1)} %bitcast.43), channel_id=1, source_target_pairs={{0,32},{32,0},{16,48},{48,16},{64,96},{96,64},{80,112},{112,80},{1... | collective-permute-start | bytes 786440 | tf_op jit(solution)/shard_map/ppermute | solution.py:26
  168.2 12.8 %while.124 = (s32[]{:T(128)}, f32[4,256]{1,0:T(4,128)S(1)}, f32[4,256]{1,0:T(4,128)S(1)}, f32[4,256,128]{2,1,0:T(8,128)S(1)}, s32[]{:T(128)}, /*index=5*/s32[256...) while((s32[]{:T(128)}, f32[4,256]{1,0:T(4,128)S(1)}, ...), condition=%wide.region_71.73_spmd.clone, body=%wide.region_68.72_spmd.clone.sunk | while | flops 137038336 | bytes 4923615 | solution.py:122
  181.3 1.3 compare_and_fusion.9
  184.0 1.3 compare_and_fusion.8
  186.1 1.2 compare_and_fusion.7
  187.4 1.1 copy.157
  192.0 8.9 %convolution_convert_fusion = bf16[1024,4096]{1,0:T(8,128)(2,1)} fusion(bf16[1024,512]{1,0:T(8,128)(2,1)S(1)} %fusion.102, bf16[512,4096]{1,0:T(8,128)(2,1)} %param.27), kind=kOutput, calls=%fused_computation.167 | convolution fusion | flops 4299161600 | bytes 13631488 | tf_op jit(solution)/shard_map/dot_general | solution.py:198
  201.7 125.3 %reduce-scatter.2.cloned.1.call-done = bf16[1024,256]{1,0:T(8,128)(2,1)} async-done(((bf16[1024,4096]{1,0:T(8,128)(2,1)}), bf16[1024,256]{1,0:T(8,128)(2,1)}) %reduce-scatter.2.cloned.1.call-update) | async-done | bytes 524304 | tf_op jit(solution)/shard_map/reduce_scatter | solution.py:199
  327.1 1.3 fusion.97
  328.4 42.4 %psum.7 = f32[1024]{0:T(1024)S(1)} all-reduce(f32[1024]{0:T(1024)S(1)} %get-tuple-element.1148), channel_id=1, replica_groups=mesh['dp'=16,'tensor'=16] {'tensor'}, use_global_device_ids=true, to_apply=%region_91.93 | all-reduce | flops 1024 | bytes 8192 | tf_op jit(solution)/shard_map/psum | solution.py:204
  (305 shorter events, 52.9 us)
Async XLA Ops:
  7.2 22.4 %copy-start = (bf16[1024,512]{1,0:T(8,128)(2,1)S(1)}, bf16[1024,512]{1,0:T(8,128)(2,1)}, u32[]{:S(2)}) copy-start(bf16[1024,512]{1,0:T(8,128)(2,1)} %param.24) | copy-start | bytes 3145732
  7.2 319.9 %reduce-scatter.2.cloned.1.call-start = ((), (), s32[]{:S(2)}) async-start(), calls=%async_computation.1 | async-start | bytes 8912896 | tf_op jit(solution)/shard_map/reduce_scatter | solution.py:199
  30.6 66.7 %collective-permute-start.1 = (bf16[256,512]{1,0:T(8,128)(2,1)}, bf16[256,512]{1,0:T(8,128)(2,1)}, u32[]{:S(2)}, u32[]{:S(2)}) collective-permute-start(bf16[256,512]{1,0:T(8,128)(2,1)} %get-tuple-element.1224), channel_id=1, source_target_pairs={{0,128},{128,0},{16,144},{144,16},{32,160},{160,32},{48,176},{176,... | collective-permute-start | bytes 786440 | tf_op jit(solution)/shard_map/ppermute | solution.py:26
  38.4 92.5 %collective-permute-start = (bf16[1024,256]{1,0:T(8,128)(2,1)}, bf16[1024,256]{1,0:T(8,128)(2,1)}, u32[]{:S(2)}, u32[]{:S(2)}) collective-permute-start(bf16[1024,256]{1,0:T(8,128)(2,1)} %pad_maximum_fusion.1), channel_id=1, source_target_pairs={{0,128},{128,0},{16,144},{144,16},{32,160},{160,32},{48,176},{176,... | collective-permute-start | bytes 1572872 | tf_op jit(solution)/shard_map/ppermute | solution.py:26
  38.5 67.0 %collective-permute-start.4 = (bf16[256,512]{1,0:T(8,128)(2,1)}, bf16[256,512]{1,0:T(8,128)(2,1)}, u32[]{:S(2)}, u32[]{:S(2)}) collective-permute-start(bf16[256,512]{1,0:T(8,128)(2,1)} %get-tuple-element.1227), channel_id=1, source_target_pairs={{0,64},{64,0},{16,80},{80,16},{32,96},{96,32},{48,112},{112,48},{1... | collective-permute-start | bytes 786440 | tf_op jit(solution)/shard_map/ppermute | solution.py:26
  40.6 87.7 %collective-permute-start.7 = (bf16[256,512]{1,0:T(8,128)(2,1)}, bf16[256,512]{1,0:T(8,128)(2,1)}, u32[]{:S(2)}, u32[]{:S(2)}) collective-permute-start(bf16[256,512]{1,0:T(8,128)(2,1)} %get-tuple-element.1226), channel_id=1, source_target_pairs={{0,32},{32,0},{16,48},{48,16},{64,96},{96,64},{80,112},{112,80},{1... | collective-permute-start | bytes 786440 | tf_op jit(solution)/shard_map/ppermute | solution.py:26
  41.0 88.6 %collective-permute-start.10 = (bf16[256,512]{1,0:T(8,128)(2,1)}, bf16[256,512]{1,0:T(8,128)(2,1)}, u32[]{:S(2)}, u32[]{:S(2)}) collective-permute-start(bf16[256,512]{1,0:T(8,128)(2,1)} %get-tuple-element.1225), channel_id=1, source_target_pairs={{0,16},{16,0},{32,48},{48,32},{64,80},{80,64},{96,112},{112,96},{1... | collective-permute-start | bytes 786440 | tf_op jit(solution)/shard_map/ppermute | solution.py:26
  75.2 6.4 %copy-start.6 = (s32[4]{0:T(128)S(1)}, s32[4]{0:T(128)}, u32[]{:S(2)}) copy-start(s32[4]{0:T(128)} %and_select_fusion.4) | copy-start | bytes 52
  75.3 9.6 %copy-start.8 = (s32[4]{0:T(128)S(1)}, s32[4]{0:T(128)}, u32[]{:S(2)}) copy-start(s32[4]{0:T(128)} %and_select_fusion.3) | copy-start | bytes 52
  75.3 12.7 %copy-start.7 = (s32[4]{0:T(128)S(1)}, s32[4]{0:T(128)}, u32[]{:S(2)}) copy-start(s32[4]{0:T(128)} %and_select_fusion.2) | copy-start | bytes 52
  75.3 18.3 %copy-start.5 = (pred[1,4]{0,1:T(4,128)(4,1)S(1)}, pred[1,4]{0,1:T(4,128)(4,1)}, u32[]{:S(2)}) copy-start(pred[1,4]{0,1:T(4,128)(4,1)} %get-tuple-element.1284) | copy-start | bytes 16
  75.3 18.9 %copy-start.4 = (pred[1,4]{0,1:T(4,128)(4,1)S(1)}, pred[1,4]{0,1:T(4,128)(4,1)}, u32[]{:S(2)}) copy-start(pred[1,4]{0,1:T(4,128)(4,1)} %get-tuple-element.1179) | copy-start | bytes 16
  97.3 45.6 %collective-permute-start.3 = (bf16[1024,256]{1,0:T(8,128)(2,1)}, bf16[1024,256]{1,0:T(8,128)(2,1)}, u32[]{:S(2)}, u32[]{:S(2)}) collective-permute-start(bf16[1024,256]{1,0:T(8,128)(2,1)} %pad_maximum_fusion.1), channel_id=1, source_target_pairs={{0,64},{64,0},{16,80},{80,16},{32,96},{96,32},{48,112},{112,48},{1... | collective-permute-start | bytes 1572872 | tf_op jit(solution)/shard_map/ppermute | solution.py:26
  105.5 52.7 %collective-permute-start.6 = (bf16[1024,256]{1,0:T(8,128)(2,1)}, bf16[1024,256]{1,0:T(8,128)(2,1)}, u32[]{:S(2)}, u32[]{:S(2)}) collective-permute-start(bf16[1024,256]{1,0:T(8,128)(2,1)} %pad_maximum_fusion.1), channel_id=1, source_target_pairs={{0,32},{32,0},{16,48},{48,16},{64,96},{96,64},{80,112},{112,80},{1... | collective-permute-start | bytes 1572872 | tf_op jit(solution)/shard_map/ppermute | solution.py:26
  128.3 39.9 %collective-permute-start.9 = (bf16[1024,256]{1,0:T(8,128)(2,1)}, bf16[1024,256]{1,0:T(8,128)(2,1)S(1)}, u32[]{:S(2)}, u32[]{:S(2)}) collective-permute-start(bf16[1024,256]{1,0:T(8,128)(2,1)} %pad_maximum_fusion.1), channel_id=1, source_target_pairs={{0,16},{16,0},{32,48},{48,32},{64,80},{80,64},{96,112},{112,96},{1... | collective-permute-start | bytes 1572872 | tf_op jit(solution)/shard_map/ppermute | solution.py:26
  142.9 44.5 %collective-permute-start.2 = (bf16[1,256,512]{1,2,0:T(8,128)(2,1)}, bf16[1,256,512]{1,2,0:T(8,128)(2,1)}, u32[]{:S(2)}, u32[]{:S(2)}) collective-permute-start(bf16[1,256,512]{1,2,0:T(8,128)(2,1)} %bitcast.19), channel_id=1, source_target_pairs={{0,128},{128,0},{16,144},{144,16},{32,160},{160,32},{48,176},{176,... | collective-permute-start | bytes 786440 | tf_op jit(solution)/shard_map/ppermute | solution.py:26
  144.6 43.9 %collective-permute-start.5 = (bf16[1,256,512]{1,2,0:T(8,128)(2,1)}, bf16[1,256,512]{1,2,0:T(8,128)(2,1)}, u32[]{:S(2)}, u32[]{:S(2)}) collective-permute-start(bf16[1,256,512]{1,2,0:T(8,128)(2,1)} %bitcast.31), channel_id=1, source_target_pairs={{0,64},{64,0},{16,80},{80,16},{32,96},{96,32},{48,112},{112,48},{1... | collective-permute-start | bytes 786440 | tf_op jit(solution)/shard_map/ppermute | solution.py:26
  159.9 29.8 %collective-permute-start.8 = (bf16[1,256,512]{1,2,0:T(8,128)(2,1)}, bf16[1,256,512]{1,2,0:T(8,128)(2,1)}, u32[]{:S(2)}, u32[]{:S(2)}) collective-permute-start(bf16[1,256,512]{1,2,0:T(8,128)(2,1)} %bitcast.43), channel_id=1, source_target_pairs={{0,32},{32,0},{16,48},{48,16},{64,96},{96,64},{80,112},{112,80},{1... | collective-permute-start | bytes 786440 | tf_op jit(solution)/shard_map/ppermute | solution.py:26
  168.2 14.5 %copy-start.1 = (bf16[4,256,512]{1,2,0:T(8,128)(2,1)S(1)}, bf16[4,256,512]{1,2,0:T(8,128)(2,1)}, u32[]{:S(2)}) copy-start(bf16[4,256,512]{1,2,0:T(8,128)(2,1)} %pad_maximum_fusion) | copy-start | bytes 3145732
  181.2 9.5 %collective-permute-start.11 = (bf16[1,256,512]{1,2,0:T(8,128)(2,1)S(1)}, bf16[1,256,512]{1,2,0:T(8,128)(2,1)S(1)}, u32[]{:S(2)}, u32[]{:S(2)}) collective-permute-start(bf16[1,256,512]{1,2,0:T(8,128)(2,1)S(1)} %bitcast.285), channel_id=1, source_target_pairs={{0,16},{16,0},{32,48},{48,32},{64,80},{80,64},{96,112},{112,96},{1... | collective-permute-start | bytes 786440 | tf_op jit(solution)/shard_map/ppermute | solution.py:26
  200.9 126.2 %copy-start.3 = (bf16[1024,256]{1,0:T(8,128)(2,1)S(1)}, bf16[1024,256]{1,0:T(8,128)(2,1)}, u32[]{:S(2)}) copy-start(bf16[1024,256]{1,0:T(8,128)(2,1)} %param.26) | copy-start | bytes 1572868
  328.4 43.5 %copy-start.2 = (bf16[1024,256]{1,0:T(8,128)(2,1)}, bf16[1024,256]{1,0:T(8,128)(2,1)S(1)}, u32[]{:S(2)}) copy-start(bf16[1024,256]{1,0:T(8,128)(2,1)S(1)} %get-tuple-element.1149) | copy-start | bytes 1572868
Sparse Core Ops, SparseCore 0:
  201.0 125.9 reduce-scatter.1
where the time goes:
time: 378 us; the launch traced here: 379 us
  waiting for transfers between devices  125 us (33%)
  starting transfers between devices  55 us (15%)
  between operations  45.3 us (12%)
  blocking collectives  42.4 us (11%)
  other arithmetic  36.3 us (10%)
  local copies, waits for them, and re-layouts  30.5 us (8%)
  loops' own time  22.2 us (6%)
  matrix products  21.5 us (6%)
    reduce_scatter x1, waiting for transfers between devices, body(): lax.psum_scatter(partial_value.astype(jnp.bfloat16), 'tensor', scatter_di...  125 us
    ppermute x12, starting transfers between devices, partner_2(): return lax.ppermute(block, axis, route)  55 us
    psum x1, blocking collectives, body(): squares = lax.psum(jnp.sum(widened * widened, axis=1), 'tensor')  42.4 us
    another operation x8, loops' own time, attend_block(): lax.fori_loop(first_block, last_block + 1, visit_tile, start_state)  22.2 us
    dot_general x1, matrix products, body(): jnp.dot(attn_rows, out_weight, preferred_element_type=jnp.float32)  8.89 us
  transfers between devices with their start and end apart: 13, of which 1 were waited for; matrix products, arithmetic and copies ran while one was open for 16% of the time, Pallas kernels for 0%

commit v1 on v0

v1 whole, which is shorter than its diff:
```python
import functools, math

import jax
import jax.numpy as jnp
from jax import lax
from jax.experimental import pallas as pl
from jax.experimental.pallas import tpu as pltpu
from jax.sharding import PartitionSpec as P

D = 4096
HEADS = 64
KVH = 8
HD = 128
SUB = 256
X = 4
Z = 4
MASK_FILL = -1e30
EPSILON = 1e-06
PLAN = {"B": (0, 448, "x", 1, True), "A": (448, 256, "z", 1, True), "C": (704, 320, "x", -1, False)}
ORDER = ("1B", "1A", "1C", "2B", "2A", "2C", "3B", "3A", "3C", "FB", "FC", "FA")
GATES = {("C", 1, "back"): "3B", ("A", 2, 0): "FB"}
COST = pl.CostEstimate(flops=1, bytes_accessed=1, transcendentals=0)
LONG = pl.CostEstimate(flops=200_000_000_000, bytes_accessed=1, transcendentals=0)
PROJECT_VMEM = 36 << 20
OTHER_VMEM = 16 << 20


def ring_pairs(axis, step):
    pairs = []
    for z in range(Z):
        for x in range(X):
            to = z * X + (x + step) % X if axis == "x" else (z + step) % Z * X + x
            pairs.append((z * X + x, to))
    return pairs


def shift(value, axis, step):
    return lax.ppermute(value, "tensor", ring_pairs(axis, step))


def place_of(axis, where):
    return where[3] if axis == "x" else where[2]


def attend_rows(first, rows, docs, q_ref, q_first, kv_ref):
    factor = math.log2(math.e) / math.sqrt(HD)
    q_docs = jnp.broadcast_to(docs[:, first : first + rows], (128, rows)).T[:, :1]
    tiles = [(start, min(SUB, first - start)) for start in range(0, first, SUB)] + [(first, rows)]
    masks = []
    for start, width in tiles:
        mask = q_docs == docs[:, start : start + width]
        if start == first:
            here = (rows, width)
            mask = mask & (lax.broadcasted_iota(jnp.int32, here, 1) <= lax.broadcasted_iota(jnp.int32, here, 0))
        masks.append(mask)
    heads = []
    for head in range(q_ref.shape[1] // HD):
        q = q_ref[q_first : q_first + rows, head * HD : (head + 1) * HD]
        scores = []
        peak = None
        for (start, width), mask in zip(tiles, masks):
            keys = kv_ref[0, start : start + width, :]
            score = lax.dot_general(q, keys, (((1,), (1,)), ((), ())), preferred_element_type=jnp.float32)
            score = jnp.where(mask, score, MASK_FILL)
            top = jnp.max(score, axis=1, keepdims=True)
            peak = top if peak is None else jnp.maximum(peak, top)
            scores.append(score)
        offset = peak * factor
        total = 0.0
        summed = 0.0
        for (start, width), score in zip(tiles, scores):
            weight = jnp.exp2(score * factor - offset)
            total = total + jnp.sum(weight, axis=1, keepdims=True)
            summed = summed + jnp.dot(
                weight.astype(jnp.bfloat16), kv_ref[1, start : start + width, :], preferred_element_type=jnp.float32
            )
        heads.append((summed / total).astype(jnp.bfloat16))
    return jnp.concatenate(heads, axis=1)


def project_kernel(first, rows, axis, where_ref, docs_hbm, q_hbm, kv_hbm, w_hbm, token_ref, *rest):
    outs, (token_out, docs_ref, q_ref, kv_ref, w_ref, attn_ref, sems) = rest[:-7], rest[-7:]
    keys = kv_ref.shape[1]
    column = pl.ds(pl.multiple_of(where_ref[0] * HD, HD), HD)
    fetches = [
        pltpu.make_async_copy(docs_hbm, docs_ref, sems.at[0]),
        pltpu.make_async_copy(q_hbm.at[pl.ds(first, rows), :], q_ref, sems.at[1]),
        pltpu.make_async_copy(kv_hbm.at[:, pl.ds(0, keys), column], kv_ref, sems.at[2]),
        pltpu.make_async_copy(w_hbm, w_ref, sems.at[3]),
    ]
    for fetch in fetches:
        fetch.start()
    token_out[...] = jnp.zeros_like(token_out)
    for fetch in fetches[:3]:
        fetch.wait()
    docs = docs_ref[pl.ds(where_ref[1], 1), :]
    for at in range(0, rows, SUB):
        size = min(SUB, rows - at)
        attn_ref[at : at + size, :] = attend_rows(first + at, size, docs, q_ref, at, kv_ref)
    fetches[3].wait()
    attn = attn_ref[...]
    wide = w_ref.shape[1] // (X * Z)
    for step in (2, 3, 1, 0):
        if axis == "x":
            place = lax.rem(where_ref[3] + step, X)
            for z in range(Z):
                cols = pl.ds(pl.multiple_of((z * X + place) * wide, wide), wide)
                outs[step][:, z * wide : (z + 1) * wide] = jnp.dot(
                    attn, w_ref[:, cols], preferred_element_type=jnp.float32
                ).astype(jnp.bfloat16)
        else:
            place = lax.rem(where_ref[2] + step, Z)
            cols = pl.ds(pl.multiple_of(place * (X * wide), X * wide), X * wide)
            outs[step][...] = jnp.dot(attn, w_ref[:, cols], preferred_element_type=jnp.float32).astype(jnp.bfloat16)


TOKEN = jax.ShapeDtypeStruct((8, 128), jnp.float32)
TOKEN_SPEC = pl.BlockSpec((8, 128), lambda i, s: (0, 0))


def project(first, rows, axis, where, docs, query, key_value, out_weight, token):
    cols = query.shape[1]
    keys = first + rows
    docs, query, key_value, out_weight = [
        pltpu.with_memory_space_constraint(a, pltpu.HBM) for a in (docs, query, key_value, out_weight)
    ]
    count = 4
    wide = out_weight.shape[1] // count
    *blocks, token = pl.pallas_call(
        functools.partial(project_kernel, first, rows, axis),
        out_shape=[jax.ShapeDtypeStruct((rows, wide), jnp.bfloat16)] * count + [TOKEN],
        grid_spec=pltpu.PrefetchScalarGridSpec(
            num_scalar_prefetch=1,
            grid=(1,),
            in_specs=[pl.BlockSpec(memory_space=pltpu.HBM)] * 4 + [pl.BlockSpec(memory_space=pl.ANY)],
            out_specs=[pl.BlockSpec((rows, wide), lambda i, s: (0, 0))] * count + [TOKEN_SPEC],
            scratch_shapes=[
                pltpu.VMEM(docs.shape, jnp.int32),
                pltpu.VMEM((rows, cols), jnp.bfloat16),
                pltpu.VMEM((2, keys, HD), jnp.bfloat16),
                pltpu.VMEM(out_weight.shape, jnp.bfloat16),
                pltpu.VMEM((rows, cols), jnp.bfloat16),
                pltpu.SemaphoreType.DMA((4,)),
            ],
        ),
        compiler_params=pltpu.CompilerParams(vmem_limit_bytes=PROJECT_VMEM),
        cost_estimate=COST,
        name="project_%d" % first,
    )(where, docs, query, key_value, out_weight, token)
    return blocks, token


def add_kernel(token_ref, a_ref, b_ref, out_ref, token_out):
    token_out[...] = jnp.zeros_like(token_out)
    out_ref[...] = (a_ref[...].astype(jnp.float32) + b_ref[...].astype(jnp.float32)).astype(jnp.bfloat16)


def add(a, b, cost, token):
    whole = pl.BlockSpec(a.shape, lambda i: (0, 0))
    return pl.pallas_call(
        add_kernel,
        out_shape=[jax.ShapeDtypeStruct(a.shape, jnp.bfloat16), TOKEN],
        grid=(1,),
        in_specs=[pl.BlockSpec(memory_space=pl.ANY), whole, whole],
        out_specs=[whole, pl.BlockSpec((8, 128), lambda i: (0, 0))],
        compiler_params=pltpu.CompilerParams(vmem_limit_bytes=OTHER_VMEM),
        cost_estimate=cost,
        name="add",
    )(token, a, b)


def merge_kernel(axis, wide, together, where_ref, token_ref, *refs):
    ins, outs = refs[:3], refs[3:]
    outs[-1][...] = jnp.zeros_like(outs[-1])
    for step in range(4):
        if together:
            cols = pl.ds(step * wide, wide)
        elif axis == "x":
            cols = pl.ds(pl.multiple_of(lax.rem(where_ref[3] + step, X) * wide, wide), wide)
        else:
            cols = pl.ds(pl.multiple_of(lax.rem(where_ref[2] + step, Z) * wide, wide), wide)
        total = ins[0][:, cols].astype(jnp.float32)
        for ref in ins[1:]:
            total = total + ref[:, cols].astype(jnp.float32)
        if together:
            outs[0][step] = total.astype(jnp.bfloat16)
        else:
            outs[step][...] = total.astype(jnp.bfloat16)


def merge(axis, where, total, others, together, cost, token):
    rows, cols = total.shape
    wide = cols // 4
    whole = pl.BlockSpec((rows, cols), lambda i, s: (0, 0))
    shapes = [(4, rows, wide)] if together else [(rows, wide)] * 4
    *blocks, token = pl.pallas_call(
        functools.partial(merge_kernel, axis, wide, together),
        out_shape=[jax.ShapeDtypeStruct(shape, jnp.bfloat16) for shape in shapes] + [TOKEN],
        grid_spec=pltpu.PrefetchScalarGridSpec(
            num_scalar_prefetch=1,
            grid=(1,),
            in_specs=[pl.BlockSpec(memory_space=pl.ANY)] + [whole] * (1 + len(others)),
            out_specs=[pl.BlockSpec(shape, lambda i, s, n=len(shape): (0,) * n) for shape in shapes] + [TOKEN_SPEC],
        ),
        compiler_params=pltpu.CompilerParams(vmem_limit_bytes=OTHER_VMEM),
        cost_estimate=cost,
        name="merge",
    )(where, token, total, *others)
    return blocks, token


def final_kernel(token_ref, residual_ref, *rest):
    others, (hidden_ref, squares_ref, token_out) = rest[:-3], rest[-3:]
    token_out[...] = jnp.zeros_like(token_out)
    parts = [others[0][i] for i in range(4)] if len(others) == 1 else [ref[...] for ref in others]
    mixed = parts[0].astype(jnp.float32)
    for part in parts[1:]:
        mixed = mixed + part.astype(jnp.float32)
    hidden = (residual_ref[...].astype(jnp.float32) + mixed).astype(jnp.bfloat16)
    hidden_ref[...] = hidden
    widened = hidden.astype(jnp.float32)
    squares_ref[...] = jnp.sum(widened * widened, axis=1, keepdims=True)


def final(first, residual, blocks, token):
    rows, cols = blocks[0].shape[-2:]
    whole = pl.BlockSpec((rows, cols), lambda i: (0, 0))
    return pl.pallas_call(
        final_kernel,
        out_shape=[
            jax.ShapeDtypeStruct((rows, cols), jnp.bfloat16),
            jax.ShapeDtypeStruct((rows, 1), jnp.float32),
            TOKEN,
        ],
        grid=(1,),
        in_specs=[pl.BlockSpec(memory_space=pl.ANY)]
        + [pl.BlockSpec((pl.Element(rows), pl.Element(cols)), lambda i: (first, 0))]
        + [pl.BlockSpec(b.shape, lambda i, n=b.ndim: (0,) * n) for b in blocks],
        out_specs=[whole, pl.BlockSpec((rows, 1), lambda i: (0, 0)), pl.BlockSpec((8, 128), lambda i: (0, 0))],
        compiler_params=pltpu.CompilerParams(vmem_limit_bytes=OTHER_VMEM),
        cost_estimate=COST,
        name="final",
    )(token, residual, *blocks)


def swap(value, axis):
    if axis == "x":
        groups = [[z * X + x for x in range(X)] for z in range(Z)]
    else:
        groups = [[z * X + x for z in range(Z)] for x in range(X)]
    return lax.all_to_all(value, "tensor", split_axis=0, concat_axis=0, axis_index_groups=groups, tiled=True)


class Sender:
    def __init__(self):
        self.tokens = {}
        self.held = {}
        self.results = {}

    def send(self, name, value, axis, way):
        gate = GATES.get(name)
        if gate is None or gate in self.tokens:
            if gate is not None:
                value, _ = lax.optimization_barrier((value, self.tokens[gate]))
            self.results[name] = shift(value, axis, way) if way else swap(value, axis)
        else:
            self.held[name] = (value, axis, way)

    def passed(self, step, token):
        self.tokens[step] = token
        for name in list(self.held):
            if GATES[name] == step:
                self.send(name, *self.held.pop(name))

    def take(self, *names):
        return [self.results[name] for name in names]


def body(query, key_value, residual, out_weight, norm_gain, doc_ids):
    tensor_index = lax.axis_index("tensor")
    group_index = lax.axis_index("dp")
    heads_here = query.shape[1] // HD
    kv_head = tensor_index * heads_here // (HEADS // KVH)
    where = jnp.stack([kv_head, group_index, tensor_index // X, tensor_index % X]).astype(jnp.int32)
    feature_count = residual.shape[1]
    token = where
    state = {}
    sender = Sender()
    for step, chunk in ORDER:
        first, rows, axis, way, together = PLAN[chunk]
        other = "z" if axis == "x" else "x"
        if step == "1":
            blocks, token = project(first, rows, axis, where, doc_ids, query, key_value, out_weight, token)
            near, far, back = (blocks[1], blocks[2], blocks[3]) if way > 0 else (blocks[3], blocks[2], blocks[1])
            sender.send((chunk, 1, "far"), far, axis, way)
            sender.send((chunk, 1, "back"), back, axis, -way)
            state[chunk] = (near, blocks[0])
        elif step == "2":
            near, own = state[chunk]
            if chunk == "B":
                near, _ = lax.optimization_barrier((near, *sender.take((chunk, 1, "back"))))
            summed, token = add(near, *sender.take((chunk, 1, "far")), LONG if chunk == "A" else COST, token)
            state[chunk] = own
            sender.send((chunk, 1, "near"), summed, axis, way)
        elif step == "3":
            others = sender.take((chunk, 1, "near"), (chunk, 1, "back"))
            blocks, token = merge(other, where, state[chunk], others, together, LONG if chunk == "A" else COST, token)
            if together:
                sender.send((chunk, 2, 0), blocks[0], other, 0)
            else:
                for i in (1, 3, 2):
                    sender.send((chunk, 2, i), blocks[i], other, i)
            state[chunk] = blocks[0]
        else:
            if together:
                blocks = sender.take((chunk, 2, 0))
            else:
                blocks = [state[chunk], *sender.take((chunk, 2, 1), (chunk, 2, 3), (chunk, 2, 2))]
            hidden, squares, token = final(first, residual, blocks, token)
            state[chunk] = (first, hidden, squares)
        sender.passed(step + chunk, token)
    done = sorted(state.values(), key=lambda entry: entry[0])
    hidden = jnp.concatenate([h for _, h, _ in done], axis=0)
    squares = jnp.concatenate([s for _, _, s in done], axis=0)[:, 0]
    widened = hidden.astype(jnp.float32)
    spread = jnp.broadcast_to(squares[None], (X * Z, squares.shape[0]))
    squares = jnp.sum(lax.all_to_all(spread, "tensor", split_axis=0, concat_axis=0, tiled=True), axis=0)
    gain_part = lax.dynamic_slice_in_dim(norm_gain, tensor_index * feature_count, feature_count, 0)
    normed = (
        widened * lax.rsqrt(squares / D + EPSILON)[:, None] * gain_part.astype(jnp.float32)
    ).astype(jnp.bfloat16)
    return (hidden, normed)


def solution(mesh):
    placed = (P("dp", "tensor"), P(None, "dp", None), P("dp", "tensor"), P("tensor", None), P(), P())
    return jax.shard_map(
        body, mesh=mesh, in_specs=placed, out_specs=(P("dp", "tensor"), P("dp", "tensor")), check_vma=False
    )
```

time: 378 us -> 134 us (0.35)
  waiting for transfers between devices: 125 us -> 44.7 us
  between operations: 45.3 us -> 0.77 us
  blocking collectives: 42.4 us -> 0 us
  Pallas kernels: 0 us -> 35.6 us
  other arithmetic: 36.3 us -> 1.97 us
  local copies, waits for them, and re-layouts: 30.5 us -> 1.69 us
  loops' own time: 22.2 us -> 0 us
  matrix products: 21.5 us -> 0 us
  starting transfers between devices: 55 us -> 49.2 us
    reduce_scatter x1 -> x0, waiting for transfers between devices: 125 us -> none  [body(): lax.psum_scatter(partial_value.astype(jnp.bfloat16), 'tensor', scatter_di...]
    psum x1 -> x0, blocking collectives: 42.4 us -> none  [body(): squares = lax.psum(jnp.sum(widened * widened, axis=1), 'tensor')]
    pallas_call x0 -> x12, Pallas kernels: none -> 35.6 us  [the longest x3 22.2 us: project(): pl.pallas_call(functools.partial(project_kernel, first, rows, axis), out_...]
    ppermute x12, waiting for transfers between devices: 0.03 us -> 31.4 us  [shift(): return lax.ppermute(value, 'tensor', ring_pairs(axis, step))]
    another operation x8 -> x0, loops' own time: 22.2 us -> none  [attend_block(): lax.fori_loop(first_block, last_block + 1, visit_tile, start_state)]
    dot_general x15 -> x0, matrix products: 21.5 us -> none  [the longest x1 8.89 us: body(): jnp.dot(attn_rows, out_weight, preferred_element_type=jnp.float32)]
    ppermute x12, starting transfers between devices: 55 us -> 34.1 us  [shift(): return lax.ppermute(value, 'tensor', ring_pairs(axis, step))]
    all_to_all x0 -> x3, starting transfers between devices: none -> 15.1 us  [the longest x2 9.69 us: swap(): lax.all_to_all(value, 'tensor', split_axis=0, concat_axis=0, axis_index_g...]
  transfers between devices with their start and end apart: 13 -> 15, of which waited for: 1 -> 9; matrix products, arithmetic and copies ran while one was open for 16% -> 1% of each run, Pallas kernels for 0% -> 21%
where the time goes in v1:
time: 134 us
  starting transfers between devices  49.2 us (37%)
  waiting for transfers between devices  44.7 us (33%)
  Pallas kernels  35.6 us (27%)
  other arithmetic  1.97 us (1%)
  local copies, waits for them, and re-layouts  1.69 us (1%)
    ppermute x12, starting transfers between devices, shift(): return lax.ppermute(value, 'tensor', ring_pairs(axis, step))  34.1 us
    ppermute x12, waiting for transfers between devices, shift(): return lax.ppermute(value, 'tensor', ring_pairs(axis, step))  31.4 us
    pallas_call x3, Pallas kernels, project(): pl.pallas_call(functools.partial(project_kernel, first, rows, axis), out_...  22.2 us
    all_to_all x1, waiting for transfers between devices, body(): lax.all_to_all(spread, 'tensor', split_axis=0, concat_axis=0, tiled=True)  10.1 us
    all_to_all x2, starting transfers between devices, swap(): lax.all_to_all(value, 'tensor', split_axis=0, concat_axis=0, axis_index_g...  9.69 us
    pallas_call x3, Pallas kernels, merge(): pl.pallas_call(functools.partial(merge_kernel, axis, wide, together), out...  7.64 us
    all_to_all x1, starting transfers between devices, body(): lax.all_to_all(spread, 'tensor', split_axis=0, concat_axis=0, tiled=True)  5.44 us
    pallas_call x3, Pallas kernels, add(): pl.pallas_call(add_kernel, out_shape=[jax.ShapeDtypeStruct(a.shape, jnp.b...  3.39 us
  transfers between devices with their start and end apart: 15, of which 9 were waited for; matrix products, arithmetic and copies ran while one was open for 1% of the time, Pallas kernels for 21%

profile of v1, /device:TPU:16, one launch (start us, length us, event | category | flops | bytes accessed | tf_op | source)
XLA Modules:
  0.0 134.0 jit_solution(15628145345223965176)
XLA Ops:
  0.7 5.9 %project_0.1 = (bf16[448,1024]{1,0:T(8,128)(2,1)S(1)}, bf16[448,1024]{1,0:T(8,128)(2,1)S(1)}, bf16[448,1024]{1,0:T(8,128)(2,1)S(1)}, bf16[448,1024]{1,0:T(8,128)(2,1)S(1)}, f32[8,128]{1,0:T(8,128)S(1)}) custom-call(s32[4]{0:T(128)S(1)} %pad_add_fusion.where_ref.token_ref, s32[16,1024]{1,0:T(8,128)} %docs_hbm.5, bf16[1024,512]{1,0:T(8,128)(2,1)} %q_hbm.5, ...), custom_call_target="tpu_custom_call" | custom-call | flops 1 | bytes 1 | tf_op jit(solution)/shard_map/project_0/pallas_call | solution.py:129
  6.7 2.9 %collective-permute-start = (bf16[448,1024]{1,0:T(8,128)(2,1)S(1)}, bf16[448,1024]{1,0:T(8,128)(2,1)S(1)}, u32[]{:S(2)}, u32[]{:S(2)}) collective-permute-start(bf16[448,1024]{1,0:T(8,128)(2,1)S(1)} %get-tuple-element.47), channel_id=1, source_target_pairs={{0,3},{1,0},{2,1},{3,2},{4,7},{5,4},{6,5},{7,6},{8,11},{9,8},{10,9... | collective-permute-start | bytes 2752520 | tf_op jit(solution)/shard_map/ppermute | solution.py:38
  9.5 6.7 %project_448.1 = (bf16[256,1024]{1,0:T(8,128)(2,1)S(1)}, bf16[256,1024]{1,0:T(8,128)(2,1)S(1)}, bf16[256,1024]{1,0:T(8,128)(2,1)S(1)}, bf16[256,1024]{1,0:T(8,128)(2,1)}, f32[8,128]{1,0:T(8,128)S(1)}) custom-call(s32[4]{0:T(128)S(1)} %pad_add_fusion.where_ref.token_ref, s32[16,1024]{1,0:T(8,128)} %docs_hbm.5, bf16[1024,512]{1,0:T(8,128)(2,1)} %q_hbm.5, ...), custom_call_target="tpu_custom_call" | custom-call | flops 1 | bytes 1 | tf_op jit(solution)/shard_map/project_448/pallas_call | solution.py:129
  16.2 3.3 %collective-permute-start.2 = (bf16[256,1024]{1,0:T(8,128)(2,1)S(1)}, bf16[256,1024]{1,0:T(8,128)(2,1)S(1)}, u32[]{:S(2)}, u32[]{:S(2)}) collective-permute-start(bf16[256,1024]{1,0:T(8,128)(2,1)S(1)} %get-tuple-element.52), channel_id=1, source_target_pairs={{0,4},{1,5},{2,6},{3,7},{4,8},{5,9},{6,10},{7,11},{8,12},{9,13},{1... | collective-permute-start | bytes 1572872 | tf_op jit(solution)/shard_map/ppermute | solution.py:38
  19.5 3.3 %collective-permute-start.6 = (bf16[256,1024]{1,0:T(8,128)(2,1)}, bf16[256,1024]{1,0:T(8,128)(2,1)}, u32[]{:S(2)}, u32[]{:S(2)}) collective-permute-start(bf16[256,1024]{1,0:T(8,128)(2,1)} %get-tuple-element.62), channel_id=1, source_target_pairs={{0,12},{1,13},{2,14},{3,15},{4,0},{5,1},{6,2},{7,3},{8,4},{9,5},{1... | collective-permute-start | bytes 1572872 | tf_op jit(solution)/shard_map/ppermute | solution.py:38
  22.8 9.7 %project_704.1 = (bf16[320,1024]{1,0:T(8,128)(2,1)S(1)}, bf16[320,1024]{1,0:T(8,128)(2,1)}, bf16[320,1024]{1,0:T(8,128)(2,1)}, bf16[320,1024]{1,0:T(8,128)(2,1)S(1)}, f32[8,128]{1,0:T(8,128)S(1)}) custom-call(s32[4]{0:T(128)S(1)} %pad_add_fusion.where_ref.token_ref, s32[16,1024]{1,0:T(8,128)} %docs_hbm.5, bf16[1024,512]{1,0:T(8,128)(2,1)} %q_hbm.5, ...), custom_call_target="tpu_custom_call" | custom-call | flops 1 | bytes 1 | tf_op jit(solution)/shard_map/project_704/pallas_call | solution.py:129
  32.5 3.3 %collective-permute-start.3 = (bf16[320,1024]{1,0:T(8,128)(2,1)}, bf16[320,1024]{1,0:T(8,128)(2,1)}, u32[]{:S(2)}, u32[]{:S(2)}) collective-permute-start(bf16[320,1024]{1,0:T(8,128)(2,1)} %get-tuple-element.55), channel_id=1, source_target_pairs={{0,3},{1,0},{2,1},{3,2},{4,7},{5,4},{6,5},{7,6},{8,11},{9,8},{10,9... | collective-permute-start | bytes 1966088 | tf_op jit(solution)/shard_map/ppermute | solution.py:38
  35.9 1.2 add.34
  37.0 1.5 %collective-permute-done.2.b_ref = bf16[256,1024]{1,0:T(8,128)(2,1)S(1)} collective-permute-done((bf16[256,1024]{1,0:T(8,128)(2,1)S(1)}, bf16[256,1024]{1,0:T(8,128)(2,1)S(1)}, u32[]{:S(2)}, u32[]{:S(2)}) %collective-permute-start.2) | collective-permute-done | bytes 524320 | tf_op jit(solution)/shard_map/ppermute | solution.py:38
  38.7 7.6 %collective-permute-start.5 = (bf16[256,1024]{1,0:T(8,128)(2,1)S(1)}, bf16[256,1024]{1,0:T(8,128)(2,1)S(1)}, u32[]{:S(2)}, u32[]{:S(2)}) collective-permute-start(bf16[256,1024]{1,0:T(8,128)(2,1)S(1)} %get-tuple-element.61), channel_id=1, source_target_pairs={{0,4},{1,5},{2,6},{3,7},{4,8},{5,9},{6,10},{7,11},{8,12},{9,13},{1... | collective-permute-start | bytes 1572872 | tf_op jit(solution)/shard_map/ppermute | solution.py:38
  46.3 3.0 %collective-permute-done.3.b_ref = bf16[320,1024]{1,0:T(8,128)(2,1)} collective-permute-done((bf16[320,1024]{1,0:T(8,128)(2,1)}, bf16[320,1024]{1,0:T(8,128)(2,1)}, u32[]{:S(2)}, u32[]{:S(2)}) %collective-permute-start.3) | collective-permute-done | bytes 655392 | tf_op jit(solution)/shard_map/ppermute | solution.py:38
  49.3 2.1 %add.36 = (bf16[320,1024]{1,0:T(8,128)(2,1)}, f32[8,128]{1,0:T(8,128)S(1)}) custom-call(f32[8,128]{1,0:T(8,128)S(1)} %get-tuple-element.53.token_ref, bf16[320,1024]{1,0:T(8,128)(2,1)S(1)} %get-tuple-element.54.a_ref, bf16[320,1024]{1,0:T(8,128)(2,1)} %collective-permute-done.3.b_ref), custom_call_target="tpu_custom_call" | custom-call | flops 1 | bytes 1 | tf_op jit(solution)/shard_map/add/pallas_call | solution.py:160
  51.4 3.7 %collective-permute-start.7 = (bf16[320,1024]{1,0:T(8,128)(2,1)}, bf16[320,1024]{1,0:T(8,128)(2,1)}, u32[]{:S(2)}, u32[]{:S(2)}) collective-permute-start(bf16[320,1024]{1,0:T(8,128)(2,1)} %get-tuple-element.65), channel_id=1, source_target_pairs={{0,3},{1,0},{2,1},{3,2},{4,7},{5,4},{6,5},{7,6},{8,11},{9,8},{10,9... | collective-permute-start | bytes 1966088 | tf_op jit(solution)/shard_map/ppermute | solution.py:38
  55.1 4.4 %collective-permute-done.4.refs_1_ = bf16[448,1024]{1,0:T(8,128)(2,1)} collective-permute-done((bf16[448,1024]{1,0:T(8,128)(2,1)}, bf16[448,1024]{1,0:T(8,128)(2,1)}, u32[]{:S(2)}, u32[]{:S(2)}) %collective-permute-start.4) | collective-permute-done | bytes 917536 | tf_op jit(solution)/shard_map/ppermute | solution.py:38
  59.5 3.0 %merge.3 = (bf16[4,448,256]{2,1,0:T(8,128)(2,1)}, f32[8,128]{1,0:T(8,128)S(1)}) custom-call(s32[4]{0:T(128)S(1)} %pad_add_fusion.where_ref.token_ref, f32[8,128]{1,0:T(8,128)S(1)} %get-tuple-element.56.token_ref, bf16[448,1024]{1,0:T(8,128)(2,1)S(1)} %get-tuple-element.57.refs_0_, bf16[448,1024]{1,0:T(8,128)(2,1)} %collective-permute-done.4.refs_1_, ...), custom_call_target="tpu_custom_call" | custom-call | flops 1 | bytes 1 | tf_op jit(solution)/shard_map/merge/pallas_call | solution.py:196
  62.5 5.7 %all-to-all-start = ((bf16[4,448,256]{2,1,0:T(8,128)(2,1)}), bf16[4,448,256]{2,1,0:T(8,128)(2,1)}, u32[]{:S(2)}, u32[]{:S(2)}) async-start(bf16[4,448,256]{2,1,0:T(8,128)(2,1)} %get-tuple-element.69), calls=%async_computation | async-start | bytes 1835008 | tf_op jit(solution)/shard_map/all_to_all | solution.py:251
  68.3 0.9 collective-permute-done.5.refs_1_
  69.8 2.6 %merge.4 = (bf16[4,256,256]{2,1,0:T(8,128)(2,1)}, f32[8,128]{1,0:T(8,128)S(1)}) custom-call(s32[4]{0:T(128)S(1)} %copy-done.2, f32[8,128]{1,0:T(8,128)S(1)} %get-tuple-element.59.token_ref, bf16[256,1024]{1,0:T(8,128)(2,1)S(1)} %get-tuple-element.60.refs_0_, bf16[256,1024]{1,0:T(8,128)(2,1)S(1)} %collective-permute-done.5.refs_1_, ...), custom_call_target="tpu_custom_call" | custom-call | flops 199999995904 | bytes 1 | tf_op jit(solution)/shard_map/merge/pallas_call | solution.py:196
  72.4 11.2 %collective-permute-done.8.refs_2_ = bf16[320,1024]{1,0:T(8,128)(2,1)} collective-permute-done((bf16[320,1024]{1,0:T(8,128)(2,1)}, bf16[320,1024]{1,0:T(8,128)(2,1)}, u32[]{:S(2)}, u32[]{:S(2)}) %collective-permute-start.8) | collective-permute-done | bytes 655392 | tf_op jit(solution)/shard_map/ppermute | solution.py:38
  83.7 2.1 %merge.5 = (bf16[320,256]{1,0:T(8,128)(2,1)S(1)}, bf16[320,256]{1,0:T(8,128)(2,1)S(1)}, bf16[320,256]{1,0:T(8,128)(2,1)S(1)}, bf16[320,256]{1,0:T(8,128)(2,1)S(1)}, f32[8,128]{1,0:T(8,128)S(1)}) custom-call(s32[4]{0:T(128)S(1)} %copy-done.2, f32[8,128]{1,0:T(8,128)S(1)} %get-tuple-element.63.token_ref, bf16[320,1024]{1,0:T(8,128)(2,1)S(1)} %get-tuple-element.64.refs_0_, ...), custom_call_target="tpu_custom_call" | custom-call | flops 1 | bytes 1 | tf_op jit(solution)/shard_map/merge/pallas_call | solution.py:196
  85.7 3.2 %all-to-all-done.rest_0_ = bf16[4,448,256]{2,1,0:T(8,128)(2,1)} async-done(((bf16[4,448,256]{2,1,0:T(8,128)(2,1)}), bf16[4,448,256]{2,1,0:T(8,128)(2,1)}, u32[]{:S(2)}, u32[]{:S(2)}) %all-to-all-start) | async-done | bytes 917536 | tf_op jit(solution)/shard_map/all_to_all | solution.py:251
  89.0 1.4 %final.3 = (bf16[448,256]{1,0:T(8,128)(2,1)S(1)}, f32[448,1]{1,0:T(8,128)S(1)}, f32[8,128]{1,0:T(8,128)S(1)}) custom-call(f32[8,128]{1,0:T(8,128)S(1)} %get-tuple-element.68.token_ref, bf16[1024,256]{1,0:T(8,128)(2,1)S(1)} %copy-done, bf16[4,448,256]{2,1,0:T(8,128)(2,1)} %all-to-all-done.rest_0_), custom_call_target="tpu_custom_call" | custom-call | flops 1 | bytes 1 | tf_op jit(solution)/shard_map/final/pallas_call | solution.py:228
  90.4 3.9 %all-to-all-start.1 = ((bf16[4,256,256]{2,1,0:T(8,128)(2,1)}), bf16[4,256,256]{2,1,0:T(8,128)(2,1)S(1)}, u32[]{:S(2)}, u32[]{:S(2)}) async-start(bf16[4,256,256]{2,1,0:T(8,128)(2,1)} %get-tuple-element.78), calls=%async_computation.1 | async-start | bytes 1048576 | tf_op jit(solution)/shard_map/all_to_all | solution.py:251
  94.4 3.7 %collective-permute-start.9 = (bf16[320,256]{1,0:T(8,128)(2,1)S(1)}, bf16[320,256]{1,0:T(8,128)(2,1)S(1)}, u32[]{:S(2)}, u32[]{:S(2)}) collective-permute-start(bf16[320,256]{1,0:T(8,128)(2,1)S(1)} %get-tuple-element.73), channel_id=1, source_target_pairs={{0,4},{1,5},{2,6},{3,7},{4,8},{5,9},{6,10},{7,11},{8,12},{9,13},{1... | collective-permute-start | bytes 491528 | tf_op jit(solution)/shard_map/ppermute | solution.py:38
  98.1 3.9 %collective-permute-start.10 = (bf16[320,256]{1,0:T(8,128)(2,1)S(1)}, bf16[320,256]{1,0:T(8,128)(2,1)S(1)}, u32[]{:S(2)}, u32[]{:S(2)}) collective-permute-start(bf16[320,256]{1,0:T(8,128)(2,1)S(1)} %get-tuple-element.74), channel_id=1, source_target_pairs={{0,12},{1,13},{2,14},{3,15},{4,0},{5,1},{6,2},{7,3},{8,4},{9,5},{1... | collective-permute-start | bytes 491528 | tf_op jit(solution)/shard_map/ppermute | solution.py:38
  102.0 2.4 %collective-permute-start.11 = (bf16[320,256]{1,0:T(8,128)(2,1)S(1)}, bf16[320,256]{1,0:T(8,128)(2,1)S(1)}, u32[]{:S(2)}, u32[]{:S(2)}) collective-permute-start(bf16[320,256]{1,0:T(8,128)(2,1)S(1)} %get-tuple-element.75), channel_id=1, source_target_pairs={{0,8},{1,9},{2,10},{3,11},{4,12},{5,13},{6,14},{7,15},{8,0},{9,1},... | collective-permute-start | bytes 491528 | tf_op jit(solution)/shard_map/ppermute | solution.py:38
  104.3 0.8 dynamic-slice_convert_fusion
  105.1 1.8 %collective-permute-done.9.rest_1_ = bf16[320,256]{1,0:T(8,128)(2,1)S(1)} collective-permute-done((bf16[320,256]{1,0:T(8,128)(2,1)S(1)}, bf16[320,256]{1,0:T(8,128)(2,1)S(1)}, u32[]{:S(2)}, u32[]{:S(2)}) %collective-permute-start.9) | collective-permute-done | bytes 163872 | tf_op jit(solution)/shard_map/ppermute | solution.py:38
  106.9 8.4 %collective-permute-done.11.rest_3_ = bf16[320,256]{1,0:T(8,128)(2,1)S(1)} collective-permute-done((bf16[320,256]{1,0:T(8,128)(2,1)S(1)}, bf16[320,256]{1,0:T(8,128)(2,1)S(1)}, u32[]{:S(2)}, u32[]{:S(2)}) %collective-permute-start.11) | collective-permute-done | bytes 163872 | tf_op jit(solution)/shard_map/ppermute | solution.py:38
  117.3 5.4 %all-to-all-start.2 = ((f32[16,1,1024]{2,1,0:T(1,128)}), f32[16,1,1024]{2,1,0:T(1,128)S(1)}, u32[]{:S(2)}, u32[]{:S(2)}) async-start(f32[16,1,1024]{2,1,0:T(1,128)} %broadcast_in_dim.10), calls=%async_computation.2 | async-start | bytes 131072 | tf_op jit(solution)/shard_map/all_to_all | solution.py:327
  122.8 10.1 %all-to-all-done.2 = f32[16,1,1024]{2,1,0:T(1,128)S(1)} async-done(((f32[16,1,1024]{2,1,0:T(1,128)}), f32[16,1,1024]{2,1,0:T(1,128)S(1)}, u32[]{:S(2)}, u32[]{:S(2)}) %all-to-all-start.2) | async-done | bytes 65568 | tf_op jit(solution)/shard_map/all_to_all | solution.py:327
  133.0 1.0 multiply_convert_fusion
  (31 shorter events, 3.0 us)
Async XLA Ops:
  0.7 58.8 %copy-start.1 = (s32[4]{0:T(128)}, s32[4]{0:T(128)S(1)}, u32[]{:S(2)}) copy-start(s32[4]{0:T(128)S(1)} %pad_add_fusion.where_ref.token_ref) | copy-start | bytes 52
  6.7 29.2 %collective-permute-start = (bf16[448,1024]{1,0:T(8,128)(2,1)S(1)}, bf16[448,1024]{1,0:T(8,128)(2,1)S(1)}, u32[]{:S(2)}, u32[]{:S(2)}) collective-permute-start(bf16[448,1024]{1,0:T(8,128)(2,1)S(1)} %get-tuple-element.47), channel_id=1, source_target_pairs={{0,3},{1,0},{2,1},{3,2},{4,7},{5,4},{6,5},{7,6},{8,11},{9,8},{10,9... | collective-permute-start | bytes 2752520 | tf_op jit(solution)/shard_map/ppermute | solution.py:38
  9.5 26.3 %collective-permute-start.1 = (bf16[448,1024]{1,0:T(8,128)(2,1)S(1)}, bf16[448,1024]{1,0:T(8,128)(2,1)S(1)}, u32[]{:S(2)}, u32[]{:S(2)}) collective-permute-start(bf16[448,1024]{1,0:T(8,128)(2,1)S(1)} %get-tuple-element.49), channel_id=1, source_target_pairs={{0,1},{1,2},{2,3},{3,0},{4,5},{5,6},{6,7},{7,4},{8,9},{9,10},{10,1... | collective-permute-start | bytes 2752520 | tf_op jit(solution)/shard_map/ppermute | solution.py:38
  16.2 22.4 %collective-permute-start.2 = (bf16[256,1024]{1,0:T(8,128)(2,1)S(1)}, bf16[256,1024]{1,0:T(8,128)(2,1)S(1)}, u32[]{:S(2)}, u32[]{:S(2)}) collective-permute-start(bf16[256,1024]{1,0:T(8,128)(2,1)S(1)} %get-tuple-element.52), channel_id=1, source_target_pairs={{0,4},{1,5},{2,6},{3,7},{4,8},{5,9},{6,10},{7,11},{8,12},{9,13},{1... | collective-permute-start | bytes 1572872 | tf_op jit(solution)/shard_map/ppermute | solution.py:38
  19.5 48.7 %collective-permute-start.6 = (bf16[256,1024]{1,0:T(8,128)(2,1)}, bf16[256,1024]{1,0:T(8,128)(2,1)}, u32[]{:S(2)}, u32[]{:S(2)}) collective-permute-start(bf16[256,1024]{1,0:T(8,128)(2,1)} %get-tuple-element.62), channel_id=1, source_target_pairs={{0,12},{1,13},{2,14},{3,15},{4,0},{5,1},{6,2},{7,3},{8,4},{9,5},{1... | collective-permute-start | bytes 1572872 | tf_op jit(solution)/shard_map/ppermute | solution.py:38
  32.5 16.8 %collective-permute-start.3 = (bf16[320,1024]{1,0:T(8,128)(2,1)}, bf16[320,1024]{1,0:T(8,128)(2,1)}, u32[]{:S(2)}, u32[]{:S(2)}) collective-permute-start(bf16[320,1024]{1,0:T(8,128)(2,1)} %get-tuple-element.55), channel_id=1, source_target_pairs={{0,3},{1,0},{2,1},{3,2},{4,7},{5,4},{6,5},{7,6},{8,11},{9,8},{10,9... | collective-permute-start | bytes 1966088 | tf_op jit(solution)/shard_map/ppermute | solution.py:38
  37.0 22.5 %collective-permute-start.4 = (bf16[448,1024]{1,0:T(8,128)(2,1)}, bf16[448,1024]{1,0:T(8,128)(2,1)}, u32[]{:S(2)}, u32[]{:S(2)}) collective-permute-start(bf16[448,1024]{1,0:T(8,128)(2,1)} %get-tuple-element.58), channel_id=1, source_target_pairs={{0,1},{1,2},{2,3},{3,0},{4,5},{5,6},{6,7},{7,4},{8,9},{9,10},{10,1... | collective-permute-start | bytes 2752520 | tf_op jit(solution)/shard_map/ppermute | solution.py:38
  38.7 30.5 %collective-permute-start.5 = (bf16[256,1024]{1,0:T(8,128)(2,1)S(1)}, bf16[256,1024]{1,0:T(8,128)(2,1)S(1)}, u32[]{:S(2)}, u32[]{:S(2)}) collective-permute-start(bf16[256,1024]{1,0:T(8,128)(2,1)S(1)} %get-tuple-element.61), channel_id=1, source_target_pairs={{0,4},{1,5},{2,6},{3,7},{4,8},{5,9},{6,10},{7,11},{8,12},{9,13},{1... | collective-permute-start | bytes 1572872 | tf_op jit(solution)/shard_map/ppermute | solution.py:38
  51.4 21.0 %collective-permute-start.7 = (bf16[320,1024]{1,0:T(8,128)(2,1)}, bf16[320,1024]{1,0:T(8,128)(2,1)}, u32[]{:S(2)}, u32[]{:S(2)}) collective-permute-start(bf16[320,1024]{1,0:T(8,128)(2,1)} %get-tuple-element.65), channel_id=1, source_target_pairs={{0,3},{1,0},{2,1},{3,2},{4,7},{5,4},{6,5},{7,6},{8,11},{9,8},{10,9... | collective-permute-start | bytes 1966088 | tf_op jit(solution)/shard_map/ppermute | solution.py:38
  62.5 26.4 %all-to-all-start = ((bf16[4,448,256]{2,1,0:T(8,128)(2,1)}), bf16[4,448,256]{2,1,0:T(8,128)(2,1)}, u32[]{:S(2)}, u32[]{:S(2)}) async-start(bf16[4,448,256]{2,1,0:T(8,128)(2,1)} %get-tuple-element.69), calls=%async_computation | async-start | bytes 1835008 | tf_op jit(solution)/shard_map/all_to_all | solution.py:251
  68.3 15.4 %collective-permute-start.8 = (bf16[320,1024]{1,0:T(8,128)(2,1)}, bf16[320,1024]{1,0:T(8,128)(2,1)}, u32[]{:S(2)}, u32[]{:S(2)}) collective-permute-start(bf16[320,1024]{1,0:T(8,128)(2,1)} %get-tuple-element.67), channel_id=1, source_target_pairs={{0,1},{1,2},{2,3},{3,0},{4,5},{5,6},{6,7},{7,4},{8,9},{9,10},{10,1... | collective-permute-start | bytes 1966088 | tf_op jit(solution)/shard_map/ppermute | solution.py:38
  69.2 0.7 copy-start.2
  69.8 19.1 %copy-start = (bf16[1024,256]{1,0:T(8,128)(2,1)S(1)}, bf16[1024,256]{1,0:T(8,128)(2,1)}, u32[]{:S(2)}) copy-start(bf16[1024,256]{1,0:T(8,128)(2,1)} %residual_ref.5) | copy-start | bytes 1572868
  90.4 25.4 %all-to-all-start.1 = ((bf16[4,256,256]{2,1,0:T(8,128)(2,1)}), bf16[4,256,256]{2,1,0:T(8,128)(2,1)S(1)}, u32[]{:S(2)}, u32[]{:S(2)}) async-start(bf16[4,256,256]{2,1,0:T(8,128)(2,1)} %get-tuple-element.78), calls=%async_computation.1 | async-start | bytes 1048576 | tf_op jit(solution)/shard_map/all_to_all | solution.py:251
  94.4 12.6 %collective-permute-start.9 = (bf16[320,256]{1,0:T(8,128)(2,1)S(1)}, bf16[320,256]{1,0:T(8,128)(2,1)S(1)}, u32[]{:S(2)}, u32[]{:S(2)}) collective-permute-start(bf16[320,256]{1,0:T(8,128)(2,1)S(1)} %get-tuple-element.73), channel_id=1, source_target_pairs={{0,4},{1,5},{2,6},{3,7},{4,8},{5,9},{6,10},{7,11},{8,12},{9,13},{1... | collective-permute-start | bytes 491528 | tf_op jit(solution)/shard_map/ppermute | solution.py:38
  98.1 8.8 %collective-permute-start.10 = (bf16[320,256]{1,0:T(8,128)(2,1)S(1)}, bf16[320,256]{1,0:T(8,128)(2,1)S(1)}, u32[]{:S(2)}, u32[]{:S(2)}) collective-permute-start(bf16[320,256]{1,0:T(8,128)(2,1)S(1)} %get-tuple-element.74), channel_id=1, source_target_pairs={{0,12},{1,13},{2,14},{3,15},{4,0},{5,1},{6,2},{7,3},{8,4},{9,5},{1... | collective-permute-start | bytes 491528 | tf_op jit(solution)/shard_map/ppermute | solution.py:38
  102.0 13.3 %collective-permute-start.11 = (bf16[320,256]{1,0:T(8,128)(2,1)S(1)}, bf16[320,256]{1,0:T(8,128)(2,1)S(1)}, u32[]{:S(2)}, u32[]{:S(2)}) collective-permute-start(bf16[320,256]{1,0:T(8,128)(2,1)S(1)} %get-tuple-element.75), channel_id=1, source_target_pairs={{0,8},{1,9},{2,10},{3,11},{4,12},{5,13},{6,14},{7,15},{8,0},{9,1},... | collective-permute-start | bytes 491528 | tf_op jit(solution)/shard_map/ppermute | solution.py:38
  117.3 15.6 %all-to-all-start.2 = ((f32[16,1,1024]{2,1,0:T(1,128)}), f32[16,1,1024]{2,1,0:T(1,128)S(1)}, u32[]{:S(2)}, u32[]{:S(2)}) async-start(f32[16,1,1024]{2,1,0:T(1,128)} %broadcast_in_dim.10), calls=%async_computation.2 | async-start | bytes 131072 | tf_op jit(solution)/shard_map/all_to_all | solution.py:327
  122.8 11.2 %copy-start.3 = (bf16[1024,256]{1,0:T(8,128)(2,1)}, bf16[1024,256]{1,0:T(8,128)(2,1)S(1)}, u32[]{:S(2)}) copy-start(bf16[1024,256]{1,0:T(8,128)(2,1)S(1)} %constant_dynamic-update-slice_fusion) | copy-start | bytes 1572868

commit v2 on v1

v2 whole, which is shorter than its diff:
```python
import functools
import math

import jax
import jax.numpy as jnp
from jax import lax
from jax.experimental import pallas as pl
from jax.experimental.pallas import tpu as pltpu
from jax.sharding import PartitionSpec as P

D = 4096
HEADS = 64
KVH = 8
HD = 128
SUB = 256
X = 4
Z = 4
WIDE = 256
MASK_FILL = -1e30
EPSILON = 1e-06
PLAN = {"B": (0, 400, "x", 1, True), "A": (400, 224, "z", 1, False), "C": (624, 400, "x", -1, False)}
ORDER = ("1B", "1A", "1C", "2B", "2A", "2C", "3B", "3A", "3C", "FB", "FA", "FC")
GATES = {("C", 1, "back"): "2C", ("A", 2, 1): "3C", ("A", 2, 2): "3C", ("A", 2, 3): "3C"}
COST = pl.CostEstimate(flops=1, bytes_accessed=1, transcendentals=0)
LONG = pl.CostEstimate(flops=200_000_000_000, bytes_accessed=1, transcendentals=0)
ATTEND_VMEM = 36 << 20
OTHER_VMEM = 16 << 20
TOKEN = jax.ShapeDtypeStruct((8, 128), jnp.float32)
ANY = pl.BlockSpec(memory_space=pl.ANY)
OWN, NEAR, FAR, BACK = 0, 1, 2, 3


def ring_pairs(axis, step):
    pairs = []
    for z in range(Z):
        for x in range(X):
            to = z * X + (x + step) % X if axis == "x" else (z + step) % Z * X + x
            pairs.append((z * X + x, to))
    return pairs


def shift(value, axis, step):
    return lax.ppermute(value, "tensor", ring_pairs(axis, step))


def swap(value, axis):
    if axis == "x":
        groups = [[z * X + x for x in range(X)] for z in range(Z)]
    else:
        groups = [[z * X + x for z in range(Z)] for x in range(X)]
    return lax.all_to_all(value, "tensor", split_axis=0, concat_axis=0, axis_index_groups=groups, tiled=True)


def full(shape):
    return pl.BlockSpec(shape, lambda i, s: (0,) * len(shape))


def call(kernel, name, cost, vmem, where, inputs, in_specs, out_shapes, scratch=()):
    return pl.pallas_call(
        kernel,
        out_shape=out_shapes,
        grid_spec=pltpu.PrefetchScalarGridSpec(
            num_scalar_prefetch=1,
            grid=(1,),
            in_specs=in_specs,
            out_specs=[full(o.shape) for o in out_shapes],
            scratch_shapes=list(scratch),
        ),
        compiler_params=pltpu.CompilerParams(vmem_limit_bytes=vmem),
        cost_estimate=cost,
        name=name,
    )(where, *inputs)


def columns_of(where_ref, axis, way, block):
    size = X if axis == "x" else Z
    steps = block if way > 0 else (size - block) % size
    place = lax.rem(where_ref[3 if axis == "x" else 2] + steps, size)
    if axis == "x":
        return [(pl.multiple_of((z * X + place) * WIDE, WIDE), WIDE, z * WIDE) for z in range(Z)]
    return [(pl.multiple_of(place * (X * WIDE), X * WIDE), X * WIDE, 0)]


def attend_rows(first, rows, docs, q_ref, q_first, kv_ref):
    factor = math.log2(math.e) / math.sqrt(HD)
    q_docs = jnp.broadcast_to(docs[:, first : first + rows], (128, rows)).T[:, :1]
    tiles = [(start, min(SUB, first + rows - start)) for start in range(0, first + rows, SUB)]
    masks = []
    for start, width in tiles:
        mask = q_docs == docs[:, start : start + width]
        if start + width > first:
            here = (rows, width)
            ahead = lax.broadcasted_iota(jnp.int32, here, 1) - lax.broadcasted_iota(jnp.int32, here, 0)
            mask = mask & (ahead <= first - start)
        masks.append(mask)
    heads = []
    for head in range(q_ref.shape[1] // HD):
        q = q_ref[q_first : q_first + rows, head * HD : (head + 1) * HD]
        scores = []
        peak = None
        for (start, width), mask in zip(tiles, masks):
            keys = kv_ref[0, start : start + width, :]
            score = lax.dot_general(q, keys, (((1,), (1,)), ((), ())), preferred_element_type=jnp.float32)
            score = jnp.where(mask, score, MASK_FILL)
            top = jnp.max(score, axis=1, keepdims=True)
            peak = top if peak is None else jnp.maximum(peak, top)
            scores.append(score)
        offset = peak * factor
        total = 0.0
        summed = 0.0
        for (start, width), score in zip(tiles, scores):
            weight = jnp.exp2(score * factor - offset)
            total = total + jnp.sum(weight, axis=1, keepdims=True)
            summed = summed + jnp.dot(
                weight.astype(jnp.bfloat16), kv_ref[1, start : start + width, :], preferred_element_type=jnp.float32
            )
        heads.append((summed / total).astype(jnp.bfloat16))
    return jnp.concatenate(heads, axis=1)


def attend_kernel(first, rows, axis, way, inside, where_ref, token_ref, docs_hbm, q_hbm, kv_hbm, w_any, *rest):
    attn_ref, far_ref, back_ref, token_out, docs_ref, q_ref, kv_ref, sems, *more = rest
    keys = kv_ref.shape[1]
    column = pl.ds(pl.multiple_of(where_ref[0] * HD, HD), HD)
    fetches = [
        pltpu.make_async_copy(docs_hbm, docs_ref, sems.at[0]),
        pltpu.make_async_copy(q_hbm.at[pl.ds(first, rows), :], q_ref, sems.at[1]),
        pltpu.make_async_copy(kv_hbm.at[:, pl.ds(0, keys), column], kv_ref, sems.at[2]),
    ]
    for fetch in fetches:
        fetch.start()
    pieces = [columns_of(where_ref, axis, way, block) for block in (FAR, BACK)]
    later = [[], []]
    if not inside:
        w_ref, w_sems = more
        for slot in range(2):
            for i, (start, size, offset) in enumerate(pieces[slot]):
                later[slot].append(
                    pltpu.make_async_copy(
                        w_any.at[:, pl.ds(start, size)], w_ref.at[slot, :, offset : offset + size], w_sems.at[slot, i]
                    )
                )
                later[slot][-1].start()
    token_out[...] = jnp.zeros_like(token_out)
    for fetch in fetches:
        fetch.wait()
    docs = docs_ref[pl.ds(where_ref[1], 1), :]
    for at in range(0, rows, SUB):
        size = min(SUB, rows - at)
        attn_ref[at : at + size, :] = attend_rows(first + at, size, docs, q_ref, at, kv_ref)
    attn = attn_ref[...]
    for slot, out_ref in enumerate((far_ref, back_ref)):
        for fetch in later[slot]:
            fetch.wait()
        for start, size, offset in pieces[slot]:
            weight = w_any[:, pl.ds(start, size)] if inside else w_ref[slot, :, offset : offset + size]
            out_ref[:, offset : offset + size] = jnp.dot(attn, weight, preferred_element_type=jnp.float32).astype(
                jnp.bfloat16
            )


def attend(first, rows, axis, way, inside, where, docs, query, key_value, out_weight, token):
    cols = query.shape[1]
    keys = first + rows
    wide = out_weight.shape[1] // 4
    docs, query, key_value = [pltpu.with_memory_space_constraint(a, pltpu.HBM) for a in (docs, query, key_value)]
    out_weight = pltpu.with_memory_space_constraint(out_weight, pltpu.VMEM if inside else pltpu.HBM)
    scratch = [
        pltpu.VMEM(docs.shape, jnp.int32),
        pltpu.VMEM((rows, cols), jnp.bfloat16),
        pltpu.VMEM((2, keys, HD), jnp.bfloat16),
        pltpu.SemaphoreType.DMA((3,)),
    ]
    if not inside:
        scratch += [pltpu.VMEM((2, cols, wide), jnp.bfloat16), pltpu.SemaphoreType.DMA((2, 4))]
    return call(
        functools.partial(attend_kernel, first, rows, axis, way, inside),
        "attend_%d" % first,
        COST,
        ATTEND_VMEM,
        where,
        (token, docs, query, key_value, out_weight),
        [ANY] * 4 + [pl.BlockSpec(memory_space=pltpu.VMEM) if inside else ANY],
        [jax.ShapeDtypeStruct((rows, cols), jnp.bfloat16)]
        + [jax.ShapeDtypeStruct((rows, wide), jnp.bfloat16)] * 2
        + [TOKEN],
        scratch,
    )


def near_kernel(axis, way, where_ref, token_ref, w_ref, attn_ref, passed_ref, out_ref, own_ref, token_out):
    token_out[...] = jnp.zeros_like(token_out)
    for block in (NEAR, OWN):
        for start, size, offset in columns_of(where_ref, axis, way, block):
            total = jnp.dot(attn_ref[...], w_ref[:, pl.ds(start, size)], preferred_element_type=jnp.float32)
            if block == NEAR:
                total = total + passed_ref[:, offset : offset + size].astype(jnp.float32)
                out_ref[:, offset : offset + size] = total.astype(jnp.bfloat16)
            else:
                own_ref[:, offset : offset + size] = total.astype(jnp.bfloat16)


def near(axis, way, cost, where, out_weight, attn, passed, token):
    return call(
        functools.partial(near_kernel, axis, way),
        "near",
        cost,
        OTHER_VMEM,
        where,
        (token, pltpu.with_memory_space_constraint(out_weight, pltpu.VMEM), attn, passed),
        [ANY, pl.BlockSpec(memory_space=pltpu.VMEM), full(attn.shape), full(passed.shape)],
        [jax.ShapeDtypeStruct(passed.shape, jnp.bfloat16)] * 2 + [TOKEN],
    )


def merge_kernel(axis, together, where_ref, token_ref, own_ref, ahead_ref, behind_ref, *outs):
    outs[-1][...] = jnp.zeros_like(outs[-1])
    for step in range(4):
        place = step if together else lax.rem(where_ref[2 if axis == "x" else 3] + step, 4)
        cols = pl.ds(pl.multiple_of(place * WIDE, WIDE), WIDE)
        total = own_ref[:, cols].astype(jnp.float32)
        for ref in (ahead_ref, behind_ref):
            total = total + ref[:, cols].astype(jnp.float32)
        if together:
            outs[0][step] = total.astype(jnp.bfloat16)
        else:
            outs[step][...] = total.astype(jnp.bfloat16)


def merge(axis, together, cost, where, own, ahead, behind, token):
    rows = own.shape[0]
    if together:
        blocks = [jax.ShapeDtypeStruct((4, rows, WIDE), jnp.bfloat16)]
    else:
        blocks = [jax.ShapeDtypeStruct((rows, WIDE), jnp.bfloat16)] * 4
    return call(
        functools.partial(merge_kernel, axis, together),
        "merge",
        cost,
        OTHER_VMEM,
        where,
        (token, own, ahead, behind),
        [ANY] + [full(own.shape)] * 3,
        blocks + [TOKEN],
    )


def final_kernel(where_ref, token_ref, residual_ref, parts_ref, *rest):
    others, (hidden_ref, squares_ref, token_out) = rest[:-3], rest[-3:]
    token_out[...] = jnp.zeros_like(token_out)
    if others:
        mixed = parts_ref[...].astype(jnp.float32)
        for ref in others:
            mixed = mixed + ref[...].astype(jnp.float32)
    else:
        mixed = parts_ref[0].astype(jnp.float32)
        for i in range(1, 4):
            mixed = mixed + parts_ref[i].astype(jnp.float32)
    hidden = (residual_ref[...].astype(jnp.float32) + mixed).astype(jnp.bfloat16)
    hidden_ref[...] = hidden
    widened = hidden.astype(jnp.float32)
    squares_ref[...] = jnp.sum(widened * widened, axis=1, keepdims=True)


def final(first, where, residual, parts, others, token):
    rows, cols = parts.shape[-2:]
    return call(
        final_kernel,
        "final",
        COST,
        OTHER_VMEM,
        where,
        (token, pltpu.with_memory_space_constraint(residual, pltpu.HBM), parts, *others),
        [ANY, pl.BlockSpec((pl.Element(rows), pl.Element(cols)), lambda i, s: (first, 0))]
        + [full(a.shape) for a in (parts, *others)],
        [jax.ShapeDtypeStruct((rows, cols), jnp.bfloat16), jax.ShapeDtypeStruct((rows, 1), jnp.float32), TOKEN],
    )


class Sender:
    def __init__(self):
        self.tokens = {}
        self.held = {}
        self.results = {}

    def send(self, name, value, axis, way):
        gate = GATES.get(name)
        if gate is None or gate in self.tokens:
            if gate is not None:
                value, _ = lax.optimization_barrier((value, self.tokens[gate]))
            self.results[name] = shift(value, axis, way) if way else swap(value, axis)
        else:
            self.held[name] = (value, axis, way)

    def passed(self, step, token):
        self.tokens[step] = token
        for name in list(self.held):
            if GATES[name] == step:
                self.send(name, *self.held.pop(name))

    def take(self, *names):
        return [self.results[name] for name in names]


def body(query, key_value, residual, out_weight, norm_gain, doc_ids):
    tensor_index = lax.axis_index("tensor")
    group_index = lax.axis_index("dp")
    heads_here = query.shape[1] // HD
    kv_head = tensor_index * heads_here // (HEADS // KVH)
    where = jnp.stack([kv_head, group_index, tensor_index // X, tensor_index % X]).astype(jnp.int32)
    feature_count = residual.shape[1]
    token = where
    state = {}
    sender = Sender()
    for step, chunk in ORDER:
        first, rows, axis, way, together = PLAN[chunk]
        other = "z" if axis == "x" else "x"
        cost = LONG if chunk == "A" else COST
        if step == "1":
            inside = token is not where
            attn, far, back, token = attend(
                first, rows, axis, way, inside, where, doc_ids, query, key_value, out_weight, token
            )
            sender.send((chunk, 1, "far"), far, axis, way)
            sender.send((chunk, 1, "back"), back, axis, -way)
            state[chunk] = attn
        elif step == "2":
            attn = state[chunk]
            if chunk == "B":
                attn, _ = lax.optimization_barrier((attn, *sender.take((chunk, 1, "back"))))
            passed = sender.take((chunk, 1, "far"))
            summed, state[chunk], token = near(axis, way, cost, where, out_weight, attn, *passed, token)
            sender.send((chunk, 1, "near"), summed, axis, way)
        elif step == "3":
            others = sender.take((chunk, 1, "near"), (chunk, 1, "back"))
            *blocks, token = merge(axis, together, cost, where, state[chunk], *others, token)
            if together:
                sender.send((chunk, 2, 0), blocks[0], other, 0)
            else:
                for i in (1, 3, 2):
                    sender.send((chunk, 2, i), blocks[i], other, i)
            state[chunk] = blocks[0]
        else:
            if together:
                parts, others = *sender.take((chunk, 2, 0)), []
            else:
                parts, others = state[chunk], sender.take((chunk, 2, 1), (chunk, 2, 3), (chunk, 2, 2))
            hidden, squares, token = final(first, where, residual, parts, others, token)
            state[chunk] = (first, hidden, squares)
        sender.passed(step + chunk, token)
    done = sorted(state.values(), key=lambda entry: entry[0])
    hidden = jnp.concatenate([h for _, h, _ in done], axis=0)
    squares = jnp.concatenate([s for _, _, s in done], axis=0)[:, 0]
    widened = hidden.astype(jnp.float32)
    spread = jnp.tile(squares.reshape(8, -1), (X * Z, 1))
    spread = lax.all_to_all(spread, "tensor", split_axis=0, concat_axis=0, tiled=True)
    squares = jnp.sum(spread.reshape(X * Z, -1), axis=0)
    gain_part = lax.dynamic_slice_in_dim(norm_gain, tensor_index * feature_count, feature_count, 0)
    normed = (
        widened * lax.rsqrt(squares / D + EPSILON)[:, None] * gain_part.astype(jnp.float32)
    ).astype(jnp.bfloat16)
    return (hidden, normed)


def solution(mesh):
    placed = (P("dp", "tensor"), P(None, "dp", None), P("dp", "tensor"), P("tensor", None), P(), P())
    return jax.shard_map(
        body, mesh=mesh, in_specs=placed, out_specs=(P("dp", "tensor"), P("dp", "tensor")), check_vma=False
    )
```

time: 134 us -> 123 us (0.918)
  waiting for transfers between devices: 44.7 us -> 30.2 us
  starting transfers between devices: 49.2 us -> 52 us
    ppermute x12 -> x15, waiting for transfers between devices: 31.4 us -> 20.2 us  [shift(): return lax.ppermute(value, 'tensor', ring_pairs(axis, step))]
    ppermute x12 -> x15, starting transfers between devices: 34.1 us -> 37.8 us  [shift(): return lax.ppermute(value, 'tensor', ring_pairs(axis, step))]
    all_to_all x2 -> x1, starting transfers between devices: 9.69 us -> 6.41 us  [swap(): lax.all_to_all(value, 'tensor', split_axis=0, concat_axis=0, axis_index_g...]
    all_to_all x2 -> x1, waiting for transfers between devices: 3.22 us -> 0.01 us  [swap(): lax.all_to_all(value, 'tensor', split_axis=0, concat_axis=0, axis_index_g...]
    all_to_all x1, starting transfers between devices: 5.44 us -> 7.87 us  [body(): lax.all_to_all(spread, 'tensor', split_axis=0, concat_axis=0, tiled=True)]
  transfers between devices with their start and end apart: 15 -> 17, of which waited for: 9 -> 9; matrix products, arithmetic and copies ran while one was open for 1% -> 1% of each run, Pallas kernels for 21% -> 24%
where the time goes in v2:
time: 123 us; the launch traced here: 122 us
  starting transfers between devices  52 us (42%)
  Pallas kernels  36.5 us (30%)
  waiting for transfers between devices  30.2 us (25%)
  other arithmetic  1.95 us (2%)
    ppermute x15, starting transfers between devices, shift(): return lax.ppermute(value, 'tensor', ring_pairs(axis, step))  37.8 us
    pallas_call x12, Pallas kernels, call(): pl.pallas_call(kernel, out_shape=out_shapes, grid_spec=pltpu.PrefetchScal...  36.5 us
    ppermute x15, waiting for transfers between devices, shift(): return lax.ppermute(value, 'tensor', ring_pairs(axis, step))  20.2 us
    all_to_all x1, waiting for transfers between devices, body(): lax.all_to_all(spread, 'tensor', split_axis=0, concat_axis=0, tiled=True)  10 us
    all_to_all x1, starting transfers between devices, body(): lax.all_to_all(spread, 'tensor', split_axis=0, concat_axis=0, tiled=True)  7.87 us
    all_to_all x1, starting transfers between devices, swap(): lax.all_to_all(value, 'tensor', split_axis=0, concat_axis=0, axis_index_g...  6.41 us
  transfers between devices with their start and end apart: 17, of which 9 were waited for; matrix products, arithmetic and copies ran while one was open for 1% of the time, Pallas kernels for 24%

profile of v2, /device:TPU:16, one launch (start us, length us, event | category | flops | bytes accessed | tf_op | source)
XLA Modules:
  0.0 122.5 jit_solution(5567148177427803467)
XLA Ops:
  0.7 5.2 %attend_0.1 = (bf16[400,512]{1,0:T(8,128)(2,1)S(1)}, bf16[400,1024]{1,0:T(8,128)(2,1)S(1)}, bf16[400,1024]{1,0:T(8,128)(2,1)S(1)}, f32[8,128]{1,0:T(8,128)S(1)}) custom-call(s32[4]{0:T(128)S(1)} %pad_add_fusion.where_ref.token_ref, s32[4]{0:T(128)S(1)} %pad_add_fusion.where_ref.token_ref, s32[16,1024]{1,0:T(8,128)} %docs_hbm.5, bf16[1024,512]{1,0:T(8,128)(2,1)} %q_hbm.5, ...), custom_call_target="tpu_custom_call" | custom-call | flops 1 | bytes 1 | tf_op jit(solution)/shard_map/attend_0/pallas_call | solution.py:59
  6.0 2.8 %collective-permute-start = (bf16[400,1024]{1,0:T(8,128)(2,1)S(1)}, bf16[400,1024]{1,0:T(8,128)(2,1)S(1)}, u32[]{:S(2)}, u32[]{:S(2)}) collective-permute-start(bf16[400,1024]{1,0:T(8,128)(2,1)S(1)} %get-tuple-element.52), channel_id=1, source_target_pairs={{0,3},{1,0},{2,1},{3,2},{4,7},{5,4},{6,5},{7,6},{8,11},{9,8},{10,9... | collective-permute-start | bytes 2457608 | tf_op jit(solution)/shard_map/ppermute | solution.py:43
  8.8 4.7 %attend_400.1 = (bf16[224,512]{1,0:T(8,128)(2,1)S(1)}, bf16[224,1024]{1,0:T(8,128)(2,1)S(1)}, bf16[224,1024]{1,0:T(8,128)(2,1)}, f32[8,128]{1,0:T(8,128)S(1)}) custom-call(s32[4]{0:T(128)S(1)} %pad_add_fusion.where_ref.token_ref, f32[8,128]{1,0:T(8,128)S(1)} %get-tuple-element.48.token_ref, s32[16,1024]{1,0:T(8,128)} %docs_hbm.5, bf16[1024,512]{1,0:T(8,128)(2,1)} %q_hbm.5, ...), custom_call_target="tpu_custom_call" | custom-call | flops 1 | bytes 1 | tf_op jit(solution)/shard_map/attend_400/pallas_call | solution.py:59
  13.5 3.3 %collective-permute-start.2 = (bf16[224,1024]{1,0:T(8,128)(2,1)S(1)}, bf16[224,1024]{1,0:T(8,128)(2,1)S(1)}, u32[]{:S(2)}, u32[]{:S(2)}) collective-permute-start(bf16[224,1024]{1,0:T(8,128)(2,1)S(1)} %get-tuple-element.57), channel_id=1, source_target_pairs={{0,4},{1,5},{2,6},{3,7},{4,8},{5,9},{6,10},{7,11},{8,12},{9,13},{1... | collective-permute-start | bytes 1376264 | tf_op jit(solution)/shard_map/ppermute | solution.py:43
  16.8 7.2 %attend_624.1 = (bf16[400,512]{1,0:T(8,128)(2,1)S(1)}, bf16[400,1024]{1,0:T(8,128)(2,1)}, bf16[400,1024]{1,0:T(8,128)(2,1)}, f32[8,128]{1,0:T(8,128)S(1)}) custom-call(s32[4]{0:T(128)S(1)} %pad_add_fusion.where_ref.token_ref, f32[8,128]{1,0:T(8,128)S(1)} %get-tuple-element.49.token_ref, s32[16,1024]{1,0:T(8,128)} %docs_hbm.5, bf16[1024,512]{1,0:T(8,128)(2,1)} %q_hbm.5, ...), custom_call_target="tpu_custom_call" | custom-call | flops 1 | bytes 1 | tf_op jit(solution)/shard_map/attend_624/pallas_call | solution.py:59
  24.1 3.3 %collective-permute-start.3 = (bf16[400,1024]{1,0:T(8,128)(2,1)}, bf16[400,1024]{1,0:T(8,128)(2,1)}, u32[]{:S(2)}, u32[]{:S(2)}) collective-permute-start(bf16[400,1024]{1,0:T(8,128)(2,1)} %get-tuple-element.60), channel_id=1, source_target_pairs={{0,3},{1,0},{2,1},{3,2},{4,7},{5,4},{6,5},{7,6},{8,11},{9,8},{10,9... | collective-permute-start | bytes 2457608 | tf_op jit(solution)/shard_map/ppermute | solution.py:43
  27.4 3.0 %collective-permute-start.6 = (bf16[224,1024]{1,0:T(8,128)(2,1)}, bf16[224,1024]{1,0:T(8,128)(2,1)}, u32[]{:S(2)}, u32[]{:S(2)}) collective-permute-start(bf16[224,1024]{1,0:T(8,128)(2,1)} %get-tuple-element.67), channel_id=1, source_target_pairs={{0,12},{1,13},{2,14},{3,15},{4,0},{5,1},{6,2},{7,3},{8,4},{9,5},{1... | collective-permute-start | bytes 1376264 | tf_op jit(solution)/shard_map/ppermute | solution.py:43
  30.4 2.1 %near.3 = (bf16[400,1024]{1,0:T(8,128)(2,1)}, bf16[400,1024]{1,0:T(8,128)(2,1)S(1)}, f32[8,128]{1,0:T(8,128)S(1)}) custom-call(s32[4]{0:T(128)S(1)} %pad_add_fusion.where_ref.token_ref, f32[8,128]{1,0:T(8,128)S(1)} %get-tuple-element.50.token_ref, bf16[512,4096]{1,0:T(8,128)(2,1)S(1)} %copy-done, bf16[400,512]{1,0:T(8,128)(2,1)S(1)} %get-tuple-element.53.attn_ref, ...), custom_call_target="tpu_custom_call" | custom-call | flops 1 | bytes 1 | tf_op jit(solution)/shard_map/near/pallas_call | solution.py:59
  33.5 1.2 near.4
  34.7 7.1 %collective-permute-start.5 = (bf16[224,1024]{1,0:T(8,128)(2,1)S(1)}, bf16[224,1024]{1,0:T(8,128)(2,1)S(1)}, u32[]{:S(2)}, u32[]{:S(2)}) collective-permute-start(bf16[224,1024]{1,0:T(8,128)(2,1)S(1)} %get-tuple-element.66), channel_id=1, source_target_pairs={{0,4},{1,5},{2,6},{3,7},{4,8},{5,9},{6,10},{7,11},{8,12},{9,13},{1... | collective-permute-start | bytes 1376264 | tf_op jit(solution)/shard_map/ppermute | solution.py:43
  41.8 2.5 %collective-permute-done.3.passed_ref = bf16[400,1024]{1,0:T(8,128)(2,1)} collective-permute-done((bf16[400,1024]{1,0:T(8,128)(2,1)}, bf16[400,1024]{1,0:T(8,128)(2,1)}, u32[]{:S(2)}, u32[]{:S(2)}) %collective-permute-start.3) | collective-permute-done | bytes 819232 | tf_op jit(solution)/shard_map/ppermute | solution.py:43
  44.3 3.3 %near.5 = (bf16[400,1024]{1,0:T(8,128)(2,1)}, bf16[400,1024]{1,0:T(8,128)(2,1)S(1)}, f32[8,128]{1,0:T(8,128)S(1)}) custom-call(s32[4]{0:T(128)S(1)} %pad_add_fusion.where_ref.token_ref, f32[8,128]{1,0:T(8,128)S(1)} %get-tuple-element.58.token_ref, bf16[512,4096]{1,0:T(8,128)(2,1)S(1)} %copy-done, bf16[400,512]{1,0:T(8,128)(2,1)S(1)} %get-tuple-element.59.attn_ref, ...), custom_call_target="tpu_custom_call" | custom-call | flops 1 | bytes 1 | tf_op jit(solution)/shard_map/near/pallas_call | solution.py:59
  48.4 2.9 %collective-permute-start.7 = (bf16[400,1024]{1,0:T(8,128)(2,1)}, bf16[400,1024]{1,0:T(8,128)(2,1)}, u32[]{:S(2)}, u32[]{:S(2)}) collective-permute-start(bf16[400,1024]{1,0:T(8,128)(2,1)} %get-tuple-element.70), channel_id=1, source_target_pairs={{0,3},{1,0},{2,1},{3,2},{4,7},{5,4},{6,5},{7,6},{8,11},{9,8},{10,9... | collective-permute-start | bytes 2457608 | tf_op jit(solution)/shard_map/ppermute | solution.py:43
  51.3 3.9 %collective-permute-done.4.ahead_ref = bf16[400,1024]{1,0:T(8,128)(2,1)} collective-permute-done((bf16[400,1024]{1,0:T(8,128)(2,1)}, bf16[400,1024]{1,0:T(8,128)(2,1)}, u32[]{:S(2)}, u32[]{:S(2)}) %collective-permute-start.4) | collective-permute-done | bytes 819232 | tf_op jit(solution)/shard_map/ppermute | solution.py:43
  55.2 2.9 %merge.3 = (bf16[4,400,256]{2,1,0:T(8,128)(2,1)}, f32[8,128]{1,0:T(8,128)S(1)}) custom-call(s32[4]{0:T(128)S(1)} %pad_add_fusion.where_ref.token_ref, f32[8,128]{1,0:T(8,128)S(1)} %get-tuple-element.61.token_ref, bf16[400,1024]{1,0:T(8,128)(2,1)S(1)} %get-tuple-element.62.own_ref, bf16[400,1024]{1,0:T(8,128)(2,1)} %collective-permute-done.4.ahead_ref, ...), custom_call_target="tpu_custom_call" | custom-call | flops 1 | bytes 1 | tf_op jit(solution)/shard_map/merge/pallas_call | solution.py:59
  58.1 6.4 %all-to-all-start = ((bf16[4,400,256]{2,1,0:T(8,128)(2,1)}), bf16[4,400,256]{2,1,0:T(8,128)(2,1)}, u32[]{:S(2)}, u32[]{:S(2)}) async-start(bf16[4,400,256]{2,1,0:T(8,128)(2,1)} %get-tuple-element.74), calls=%async_computation | async-start | bytes 1638400 | tf_op jit(solution)/shard_map/all_to_all | solution.py:51
  64.5 1.7 %merge.4 = (bf16[224,256]{1,0:T(8,128)(2,1)S(1)}, bf16[224,256]{1,0:T(8,128)(2,1)S(1)}, bf16[224,256]{1,0:T(8,128)(2,1)S(1)}, bf16[224,256]{1,0:T(8,128)(2,1)S(1)}, f32[8,128]{1,0:T(8,128)S(1)}) custom-call(s32[4]{0:T(128)S(1)} %pad_add_fusion.where_ref.token_ref, f32[8,128]{1,0:T(8,128)S(1)} %get-tuple-element.64.token_ref, ...), custom_call_target="tpu_custom_call" | custom-call | flops 199999995904 | bytes 1 | tf_op jit(solution)/shard_map/merge/pallas_call | solution.py:59
  66.3 4.2 %collective-permute-done.8.behind_ref = bf16[400,1024]{1,0:T(8,128)(2,1)} collective-permute-done((bf16[400,1024]{1,0:T(8,128)(2,1)}, bf16[400,1024]{1,0:T(8,128)(2,1)}, u32[]{:S(2)}, u32[]{:S(2)}) %collective-permute-start.8) | collective-permute-done | bytes 819232 | tf_op jit(solution)/shard_map/ppermute | solution.py:43
  70.5 2.3 %merge.5 = (bf16[400,256]{1,0:T(8,128)(2,1)S(1)}, bf16[400,256]{1,0:T(8,128)(2,1)S(1)}, bf16[400,256]{1,0:T(8,128)(2,1)S(1)}, bf16[400,256]{1,0:T(8,128)(2,1)S(1)}, f32[8,128]{1,0:T(8,128)S(1)}) custom-call(s32[4]{0:T(128)S(1)} %pad_add_fusion.where_ref.token_ref, f32[8,128]{1,0:T(8,128)S(1)} %get-tuple-element.68.token_ref, ...), custom_call_target="tpu_custom_call" | custom-call | flops 1 | bytes 1 | tf_op jit(solution)/shard_map/merge/pallas_call | solution.py:59
  73.4 4.5 %collective-permute-start.12 = (bf16[400,256]{1,0:T(8,128)(2,1)S(1)}, bf16[400,256]{1,0:T(8,128)(2,1)S(1)}, u32[]{:S(2)}, u32[]{:S(2)}) collective-permute-start(bf16[400,256]{1,0:T(8,128)(2,1)S(1)} %get-tuple-element.87), channel_id=1, source_target_pairs={{0,4},{1,5},{2,6},{3,7},{4,8},{5,9},{6,10},{7,11},{8,12},{9,13},{1... | collective-permute-start | bytes 614408 | tf_op jit(solution)/shard_map/ppermute | solution.py:43
  77.8 2.3 %collective-permute-start.13 = (bf16[400,256]{1,0:T(8,128)(2,1)S(1)}, bf16[400,256]{1,0:T(8,128)(2,1)S(1)}, u32[]{:S(2)}, u32[]{:S(2)}) collective-permute-start(bf16[400,256]{1,0:T(8,128)(2,1)S(1)} %get-tuple-element.88), channel_id=1, source_target_pairs={{0,12},{1,13},{2,14},{3,15},{4,0},{5,1},{6,2},{7,3},{8,4},{9,5},{1... | collective-permute-start | bytes 614408 | tf_op jit(solution)/shard_map/ppermute | solution.py:43
  80.2 5.0 %collective-permute-start.14 = (bf16[400,256]{1,0:T(8,128)(2,1)S(1)}, bf16[400,256]{1,0:T(8,128)(2,1)S(1)}, u32[]{:S(2)}, u32[]{:S(2)}) collective-permute-start(bf16[400,256]{1,0:T(8,128)(2,1)S(1)} %get-tuple-element.89), channel_id=1, source_target_pairs={{0,8},{1,9},{2,10},{3,11},{4,12},{5,13},{6,14},{7,15},{8,0},{9,1},... | collective-permute-start | bytes 614408 | tf_op jit(solution)/shard_map/ppermute | solution.py:43
  86.1 1.1 collective-permute-start.9
  88.0 2.0 %final.3 = (bf16[400,256]{1,0:T(8,128)(2,1)S(1)}, f32[400,1]{1,0:T(8,128)S(1)}, f32[8,128]{1,0:T(8,128)S(1)}) custom-call(s32[4]{0:T(128)S(1)} %pad_add_fusion.where_ref.token_ref, f32[8,128]{1,0:T(8,128)S(1)} %get-tuple-element.73.token_ref, bf16[1024,256]{1,0:T(8,128)(2,1)} %residual_ref.5, bf16[4,400,256]{2,1,0:T(8,128)(2,1)} %all-to-all-done.parts_ref), custom_call_target="tpu_custom_call" | custom-call | flops 1 | bytes 1 | tf_op jit(solution)/shard_map/final/pallas_call | solution.py:59
  90.1 2.1 %collective-permute-done.9.rest_0_ = bf16[224,256]{1,0:T(8,128)(2,1)S(1)} collective-permute-done((bf16[224,256]{1,0:T(8,128)(2,1)S(1)}, bf16[224,256]{1,0:T(8,128)(2,1)S(1)}, u32[]{:S(2)}, u32[]{:S(2)}) %collective-permute-start.9) | collective-permute-done | bytes 114720 | tf_op jit(solution)/shard_map/ppermute | solution.py:43
  92.1 1.6 %final.4 = (bf16[224,256]{1,0:T(8,128)(2,1)S(1)}, f32[224,1]{1,0:T(8,128)S(1)}, f32[8,128]{1,0:T(8,128)S(1)}) custom-call(s32[4]{0:T(128)S(1)} %pad_add_fusion.where_ref.token_ref, f32[8,128]{1,0:T(8,128)S(1)} %get-tuple-element.76.token_ref, bf16[1024,256]{1,0:T(8,128)(2,1)} %residual_ref.5, bf16[224,256]{1,0:T(8,128)(2,1)S(1)} %get-tuple-element.77.parts_ref, ...), custom_call_target="tpu_custom_call" | custom-call | flops 1 | bytes 1 | tf_op jit(solution)/shard_map/final/pallas_call | solution.py:59
  93.7 1.5 %collective-permute-done.12.rest_0_ = bf16[400,256]{1,0:T(8,128)(2,1)S(1)} collective-permute-done((bf16[400,256]{1,0:T(8,128)(2,1)S(1)}, bf16[400,256]{1,0:T(8,128)(2,1)S(1)}, u32[]{:S(2)}, u32[]{:S(2)}) %collective-permute-start.12) | collective-permute-done | bytes 204832 | tf_op jit(solution)/shard_map/ppermute | solution.py:43
  95.2 1.6 %collective-permute-done.13.rest_1_ = bf16[400,256]{1,0:T(8,128)(2,1)S(1)} collective-permute-done((bf16[400,256]{1,0:T(8,128)(2,1)S(1)}, bf16[400,256]{1,0:T(8,128)(2,1)S(1)}, u32[]{:S(2)}, u32[]{:S(2)}) %collective-permute-start.13) | collective-permute-done | bytes 204832 | tf_op jit(solution)/shard_map/ppermute | solution.py:43
  96.9 3.3 %collective-permute-done.14.rest_2_ = bf16[400,256]{1,0:T(8,128)(2,1)S(1)} collective-permute-done((bf16[400,256]{1,0:T(8,128)(2,1)S(1)}, bf16[400,256]{1,0:T(8,128)(2,1)S(1)}, u32[]{:S(2)}, u32[]{:S(2)}) %collective-permute-start.14) | collective-permute-done | bytes 204832 | tf_op jit(solution)/shard_map/ppermute | solution.py:43
  100.1 2.2 %final.5 = (bf16[400,256]{1,0:T(8,128)(2,1)S(1)}, f32[400,1]{1,0:T(8,128)S(1)}, f32[8,128]{1,0:T(8,128)}) custom-call(s32[4]{0:T(128)S(1)} %pad_add_fusion.where_ref.token_ref, f32[8,128]{1,0:T(8,128)S(1)} %get-tuple-element.85.token_ref, bf16[1024,256]{1,0:T(8,128)(2,1)} %residual_ref.5, bf16[400,256]{1,0:T(8,128)(2,1)S(1)} %get-tuple-element.86.parts_ref, ...), custom_call_target="tpu_custom_call" | custom-call | flops 1 | bytes 1 | tf_op jit(solution)/shard_map/final/pallas_call | solution.py:59
  103.4 7.9 %all-to-all-start.1 = ((f32[16,8,128]{2,1,0:T(8,128)}), f32[16,8,128]{2,1,0:T(8,128)S(1)}, u32[]{:S(2)}, u32[]{:S(2)}) async-start(f32[16,8,128]{2,1,0:T(8,128)} %tile.9), calls=%async_computation.1 | async-start | bytes 131072 | tf_op jit(solution)/shard_map/all_to_all | solution.py:356
  111.4 10.0 %all-to-all-done.1 = f32[16,8,128]{2,1,0:T(8,128)S(1)} async-done(((f32[16,8,128]{2,1,0:T(8,128)}), f32[16,8,128]{2,1,0:T(8,128)S(1)}, u32[]{:S(2)}, u32[]{:S(2)}) %all-to-all-start.1) | async-done | bytes 65568 | tf_op jit(solution)/shard_map/all_to_all | solution.py:356
  (31 shorter events, 6.2 us)
Async XLA Ops:
  0.7 8.1 %copy-start = (bf16[512,4096]{1,0:T(8,128)(2,1)S(1)}, bf16[512,4096]{1,0:T(8,128)(2,1)}, u32[]{:S(2)}) copy-start(bf16[512,4096]{1,0:T(8,128)(2,1)} %w_ref.5) | copy-start | bytes 12582916
  6.0 24.4 %collective-permute-start = (bf16[400,1024]{1,0:T(8,128)(2,1)S(1)}, bf16[400,1024]{1,0:T(8,128)(2,1)S(1)}, u32[]{:S(2)}, u32[]{:S(2)}) collective-permute-start(bf16[400,1024]{1,0:T(8,128)(2,1)S(1)} %get-tuple-element.52), channel_id=1, source_target_pairs={{0,3},{1,0},{2,1},{3,2},{4,7},{5,4},{6,5},{7,6},{8,11},{9,8},{10,9... | collective-permute-start | bytes 2457608 | tf_op jit(solution)/shard_map/ppermute | solution.py:43
  8.8 21.6 %collective-permute-start.1 = (bf16[400,1024]{1,0:T(8,128)(2,1)S(1)}, bf16[400,1024]{1,0:T(8,128)(2,1)S(1)}, u32[]{:S(2)}, u32[]{:S(2)}) collective-permute-start(bf16[400,1024]{1,0:T(8,128)(2,1)S(1)} %get-tuple-element.54), channel_id=1, source_target_pairs={{0,1},{1,2},{2,3},{3,0},{4,5},{5,6},{6,7},{7,4},{8,9},{9,10},{10,1... | collective-permute-start | bytes 2457608 | tf_op jit(solution)/shard_map/ppermute | solution.py:43
  13.5 20.0 %collective-permute-start.2 = (bf16[224,1024]{1,0:T(8,128)(2,1)S(1)}, bf16[224,1024]{1,0:T(8,128)(2,1)S(1)}, u32[]{:S(2)}, u32[]{:S(2)}) collective-permute-start(bf16[224,1024]{1,0:T(8,128)(2,1)S(1)} %get-tuple-element.57), channel_id=1, source_target_pairs={{0,4},{1,5},{2,6},{3,7},{4,8},{5,9},{6,10},{7,11},{8,12},{9,13},{1... | collective-permute-start | bytes 1376264 | tf_op jit(solution)/shard_map/ppermute | solution.py:43
  24.1 20.3 %collective-permute-start.3 = (bf16[400,1024]{1,0:T(8,128)(2,1)}, bf16[400,1024]{1,0:T(8,128)(2,1)}, u32[]{:S(2)}, u32[]{:S(2)}) collective-permute-start(bf16[400,1024]{1,0:T(8,128)(2,1)} %get-tuple-element.60), channel_id=1, source_target_pairs={{0,3},{1,0},{2,1},{3,2},{4,7},{5,4},{6,5},{7,6},{8,11},{9,8},{10,9... | collective-permute-start | bytes 2457608 | tf_op jit(solution)/shard_map/ppermute | solution.py:43
  27.4 37.2 %collective-permute-start.6 = (bf16[224,1024]{1,0:T(8,128)(2,1)}, bf16[224,1024]{1,0:T(8,128)(2,1)}, u32[]{:S(2)}, u32[]{:S(2)}) collective-permute-start(bf16[224,1024]{1,0:T(8,128)(2,1)} %get-tuple-element.67), channel_id=1, source_target_pairs={{0,12},{1,13},{2,14},{3,15},{4,0},{5,1},{6,2},{7,3},{8,4},{9,5},{1... | collective-permute-start | bytes 1376264 | tf_op jit(solution)/shard_map/ppermute | solution.py:43
  32.5 22.7 %collective-permute-start.4 = (bf16[400,1024]{1,0:T(8,128)(2,1)}, bf16[400,1024]{1,0:T(8,128)(2,1)}, u32[]{:S(2)}, u32[]{:S(2)}) collective-permute-start(bf16[400,1024]{1,0:T(8,128)(2,1)} %get-tuple-element.63), channel_id=1, source_target_pairs={{0,1},{1,2},{2,3},{3,0},{4,5},{5,6},{6,7},{7,4},{8,9},{9,10},{10,1... | collective-permute-start | bytes 2457608 | tf_op jit(solution)/shard_map/ppermute | solution.py:43
  34.7 29.8 %collective-permute-start.5 = (bf16[224,1024]{1,0:T(8,128)(2,1)S(1)}, bf16[224,1024]{1,0:T(8,128)(2,1)S(1)}, u32[]{:S(2)}, u32[]{:S(2)}) collective-permute-start(bf16[224,1024]{1,0:T(8,128)(2,1)S(1)} %get-tuple-element.66), channel_id=1, source_target_pairs={{0,4},{1,5},{2,6},{3,7},{4,8},{5,9},{6,10},{7,11},{8,12},{9,13},{1... | collective-permute-start | bytes 1376264 | tf_op jit(solution)/shard_map/ppermute | solution.py:43
  47.6 22.9 %collective-permute-start.8 = (bf16[400,1024]{1,0:T(8,128)(2,1)}, bf16[400,1024]{1,0:T(8,128)(2,1)}, u32[]{:S(2)}, u32[]{:S(2)}) collective-permute-start(bf16[400,1024]{1,0:T(8,128)(2,1)} %get-tuple-element.72), channel_id=1, source_target_pairs={{0,1},{1,2},{2,3},{3,0},{4,5},{5,6},{6,7},{7,4},{8,9},{9,10},{10,1... | collective-permute-start | bytes 2457608 | tf_op jit(solution)/shard_map/ppermute | solution.py:43
  48.4 22.1 %collective-permute-start.7 = (bf16[400,1024]{1,0:T(8,128)(2,1)}, bf16[400,1024]{1,0:T(8,128)(2,1)}, u32[]{:S(2)}, u32[]{:S(2)}) collective-permute-start(bf16[400,1024]{1,0:T(8,128)(2,1)} %get-tuple-element.70), channel_id=1, source_target_pairs={{0,3},{1,0},{2,1},{3,2},{4,7},{5,4},{6,5},{7,6},{8,11},{9,8},{10,9... | collective-permute-start | bytes 2457608 | tf_op jit(solution)/shard_map/ppermute | solution.py:43
  58.1 29.9 %all-to-all-start = ((bf16[4,400,256]{2,1,0:T(8,128)(2,1)}), bf16[4,400,256]{2,1,0:T(8,128)(2,1)}, u32[]{:S(2)}, u32[]{:S(2)}) async-start(bf16[4,400,256]{2,1,0:T(8,128)(2,1)} %get-tuple-element.74), calls=%async_computation | async-start | bytes 1638400 | tf_op jit(solution)/shard_map/all_to_all | solution.py:51
  72.8 13.3 %collective-permute-start.11 = (bf16[224,256]{1,0:T(8,128)(2,1)S(1)}, bf16[224,256]{1,0:T(8,128)(2,1)S(1)}, u32[]{:S(2)}, u32[]{:S(2)}) collective-permute-start(bf16[224,256]{1,0:T(8,128)(2,1)S(1)} %get-tuple-element.83), channel_id=1, source_target_pairs={{0,2},{1,3},{2,0},{3,1},{4,6},{5,7},{6,4},{7,5},{8,10},{9,11},{10,... | collective-permute-start | bytes 344072 | tf_op jit(solution)/shard_map/ppermute | solution.py:43
  73.4 21.9 %collective-permute-start.12 = (bf16[400,256]{1,0:T(8,128)(2,1)S(1)}, bf16[400,256]{1,0:T(8,128)(2,1)S(1)}, u32[]{:S(2)}, u32[]{:S(2)}) collective-permute-start(bf16[400,256]{1,0:T(8,128)(2,1)S(1)} %get-tuple-element.87), channel_id=1, source_target_pairs={{0,4},{1,5},{2,6},{3,7},{4,8},{5,9},{6,10},{7,11},{8,12},{9,13},{1... | collective-permute-start | bytes 614408 | tf_op jit(solution)/shard_map/ppermute | solution.py:43
  77.8 19.0 %collective-permute-start.13 = (bf16[400,256]{1,0:T(8,128)(2,1)S(1)}, bf16[400,256]{1,0:T(8,128)(2,1)S(1)}, u32[]{:S(2)}, u32[]{:S(2)}) collective-permute-start(bf16[400,256]{1,0:T(8,128)(2,1)S(1)} %get-tuple-element.88), channel_id=1, source_target_pairs={{0,12},{1,13},{2,14},{3,15},{4,0},{5,1},{6,2},{7,3},{8,4},{9,5},{1... | collective-permute-start | bytes 614408 | tf_op jit(solution)/shard_map/ppermute | solution.py:43
  80.2 20.0 %collective-permute-start.14 = (bf16[400,256]{1,0:T(8,128)(2,1)S(1)}, bf16[400,256]{1,0:T(8,128)(2,1)S(1)}, u32[]{:S(2)}, u32[]{:S(2)}) collective-permute-start(bf16[400,256]{1,0:T(8,128)(2,1)S(1)} %get-tuple-element.89), channel_id=1, source_target_pairs={{0,8},{1,9},{2,10},{3,11},{4,12},{5,13},{6,14},{7,15},{8,0},{9,1},... | collective-permute-start | bytes 614408 | tf_op jit(solution)/shard_map/ppermute | solution.py:43
  85.2 4.8 %collective-permute-start.10 = (bf16[224,256]{1,0:T(8,128)(2,1)S(1)}, bf16[224,256]{1,0:T(8,128)(2,1)S(1)}, u32[]{:S(2)}, u32[]{:S(2)}) collective-permute-start(bf16[224,256]{1,0:T(8,128)(2,1)S(1)} %get-tuple-element.81), channel_id=1, source_target_pairs={{0,3},{1,0},{2,1},{3,2},{4,7},{5,4},{6,5},{7,6},{8,11},{9,8},{10,9... | collective-permute-start | bytes 344072 | tf_op jit(solution)/shard_map/ppermute | solution.py:43
  86.1 6.0 %collective-permute-start.9 = (bf16[224,256]{1,0:T(8,128)(2,1)S(1)}, bf16[224,256]{1,0:T(8,128)(2,1)S(1)}, u32[]{:S(2)}, u32[]{:S(2)}) collective-permute-start(bf16[224,256]{1,0:T(8,128)(2,1)S(1)} %get-tuple-element.79), channel_id=1, source_target_pairs={{0,1},{1,2},{2,3},{3,0},{4,5},{5,6},{6,7},{7,4},{8,9},{9,10},{10,1... | collective-permute-start | bytes 344072 | tf_op jit(solution)/shard_map/ppermute | solution.py:43
  103.4 18.0 %all-to-all-start.1 = ((f32[16,8,128]{2,1,0:T(8,128)}), f32[16,8,128]{2,1,0:T(8,128)S(1)}, u32[]{:S(2)}, u32[]{:S(2)}) async-start(f32[16,8,128]{2,1,0:T(8,128)} %tile.9), calls=%async_computation.1 | async-start | bytes 131072 | tf_op jit(solution)/shard_map/all_to_all | solution.py:356
  111.4 11.1 %copy-start.1 = (bf16[1024,256]{1,0:T(8,128)(2,1)}, bf16[1024,256]{1,0:T(8,128)(2,1)S(1)}, u32[]{:S(2)}) copy-start(bf16[1024,256]{1,0:T(8,128)(2,1)S(1)} %constant_dynamic-update-slice_fusion) | copy-start | bytes 1572868

commit v3 on v2

--- a/solution.py
+++ b/solution.py
@@ -18,7 +18,7 @@
 WIDE = 256
 MASK_FILL = -1e30
 EPSILON = 1e-06
-PLAN = {"B": (0, 400, "x", 1, True), "A": (400, 224, "z", 1, False), "C": (624, 400, "x", -1, False)}
+PLAN = {"B": (0, 384, "x", 1, True), "A": (384, 256, "z", 0, False), "C": (640, 384, "x", -1, False)}
 ORDER = ("1B", "1A", "1C", "2B", "2A", "2C", "3B", "3A", "3C", "FB", "FA", "FC")
 GATES = {("C", 1, "back"): "2C", ("A", 2, 1): "3C", ("A", 2, 2): "3C", ("A", 2, 3): "3C"}
 COST = pl.CostEstimate(flops=1, bytes_accessed=1, transcendentals=0)
@@ -73,6 +73,13 @@
 
 
 def columns_of(where_ref, axis, way, block):
+    if way == 0:
+        half = X * WIDE // 2
+        wanted = {FAR: ((2, 0), (1, 1)), BACK: ((2, 1), (3, 0)), NEAR: ((1, 0), (3, 1)), OWN: ((0, 0), (0, 1))}[block]
+        return [
+            (pl.multiple_of(lax.rem(where_ref[2] + step, Z) * (X * WIDE) + side * half, half), half, i * half)
+            for i, (step, side) in enumerate(wanted)
+        ]
     size = X if axis == "x" else Z
     steps = block if way > 0 else (size - block) % size
     place = lax.rem(where_ref[3 if axis == "x" else 2] + steps, size)
@@ -213,6 +220,62 @@
     )
 
 
+def both_kernel(where_ref, token_ref, w_ref, attn_ref, up_ref, down_ref, next_up, next_down, own_ref, token_out):
+    token_out[...] = jnp.zeros_like(token_out)
+    half = up_ref.shape[1] // 2
+    for block in (NEAR, OWN):
+        for i, (start, size, offset) in enumerate(columns_of(where_ref, "z", 0, block)):
+            total = jnp.dot(attn_ref[...], w_ref[:, pl.ds(start, size)], preferred_element_type=jnp.float32)
+            if block == NEAR:
+                ref = (up_ref, down_ref)[i]
+                (next_up, next_down)[i][...] = (total + ref[:, :half].astype(jnp.float32)).astype(jnp.bfloat16)
+            else:
+                ref = (down_ref, up_ref)[i]
+                own_ref[:, offset : offset + size] = total + ref[:, half:].astype(jnp.float32)
+
+
+def near_both(cost, where, out_weight, attn, up, down, token):
+    rows, cols = up.shape
+    halves = [jax.ShapeDtypeStruct((rows, cols // 2), jnp.bfloat16)] * 2
+    return call(
+        both_kernel,
+        "near_both",
+        cost,
+        OTHER_VMEM,
+        where,
+        (token, pltpu.with_memory_space_constraint(out_weight, pltpu.VMEM), attn, up, down),
+        [ANY, pl.BlockSpec(memory_space=pltpu.VMEM), full(attn.shape), full(up.shape), full(down.shape)],
+        halves + [jax.ShapeDtypeStruct((rows, cols), jnp.float32), TOKEN],
+    )
+
+
+def merge_both_kernel(where_ref, token_ref, own_ref, up_ref, down_ref, *rest):
+    outs, total_ref = rest[:-1], rest[-1]
+    outs[-1][...] = jnp.zeros_like(outs[-1])
+    half = up_ref.shape[1]
+    total_ref[:, :half] = own_ref[:, :half] + up_ref[...].astype(jnp.float32)
+    total_ref[:, half:] = own_ref[:, half:] + down_ref[...].astype(jnp.float32)
+    for step in range(4):
+        place = lax.rem(where_ref[3] + step, 4)
+        cols = pl.ds(pl.multiple_of(place * WIDE, WIDE), WIDE)
+        outs[step][...] = total_ref[:, cols].astype(jnp.bfloat16)
+
+
+def merge_both(cost, where, own, up, down, token):
+    rows = own.shape[0]
+    return call(
+        merge_both_kernel,
+        "merge_both",
+        cost,
+        OTHER_VMEM,
+        where,
+        (token, own, up, down),
+        [ANY] + [full(a.shape) for a in (own, up, down)],
+        [jax.ShapeDtypeStruct((rows, WIDE), jnp.bfloat16)] * 4 + [TOKEN],
+        [pltpu.VMEM(own.shape, jnp.float32)],
+    )
+
+
 def merge_kernel(axis, together, where_ref, token_ref, own_ref, ahead_ref, behind_ref, *outs):
     outs[-1][...] = jnp.zeros_like(outs[-1])
     for step in range(4):
@@ -270,7 +333,7 @@
         COST,
         OTHER_VMEM,
         where,
-        (token, pltpu.with_memory_space_constraint(residual, pltpu.HBM), parts, *others),
+        (token, residual, parts, *others),
         [ANY, pl.BlockSpec((pl.Element(rows), pl.Element(cols)), lambda i, s: (first, 0))]
         + [full(a.shape) for a in (parts, *others)],
         [jax.ShapeDtypeStruct((rows, cols), jnp.bfloat16), jax.ShapeDtypeStruct((rows, 1), jnp.float32), TOKEN],
@@ -321,19 +384,30 @@
             attn, far, back, token = attend(
                 first, rows, axis, way, inside, where, doc_ids, query, key_value, out_weight, token
             )
-            sender.send((chunk, 1, "far"), far, axis, way)
-            sender.send((chunk, 1, "back"), back, axis, -way)
+            sender.send((chunk, 1, "far"), far, axis, way or 1)
+            sender.send((chunk, 1, "back"), back, axis, -way or -1)
             state[chunk] = attn
         elif step == "2":
             attn = state[chunk]
             if chunk == "B":
                 attn, _ = lax.optimization_barrier((attn, *sender.take((chunk, 1, "back"))))
+            if way == 0:
+                passed = sender.take((chunk, 1, "far"), (chunk, 1, "back"))
+                up, down, state[chunk], token = near_both(cost, where, out_weight, attn, *passed, token)
+                sender.send((chunk, 1, "up"), up, axis, 1)
+                sender.send((chunk, 1, "down"), down, axis, -1)
+                sender.passed(step + chunk, token)
+                continue
             passed = sender.take((chunk, 1, "far"))
             summed, state[chunk], token = near(axis, way, cost, where, out_weight, attn, *passed, token)
             sender.send((chunk, 1, "near"), summed, axis, way)
         elif step == "3":
-            others = sender.take((chunk, 1, "near"), (chunk, 1, "back"))
-            *blocks, token = merge(axis, together, cost, where, state[chunk], *others, token)
+            if way == 0:
+                others = sender.take((chunk, 1, "up"), (chunk, 1, "down"))
+                *blocks, token = merge_both(cost, where, state[chunk], *others, token)
+            else:
+                others = sender.take((chunk, 1, "near"), (chunk, 1, "back"))
+                *blocks, token = merge(axis, together, cost, where, state[chunk], *others, token)
             if together:
                 sender.send((chunk, 2, 0), blocks[0], other, 0)
             else:

time: 123 us -> 118 us (0.959)
  starting transfers between devices: 52 us -> 42.3 us
  waiting for transfers between devices: 30.2 us -> 37.3 us
  Pallas kernels: 36.5 us -> 32.6 us
    ppermute x15 -> x16, waiting for transfers between devices: 20.2 us -> 27.3 us  [shift(): return lax.ppermute(value, 'tensor', ring_pairs(axis, step))]
    ppermute x15 -> x16, starting transfers between devices: 37.8 us -> 32.4 us  [shift(): return lax.ppermute(value, 'tensor', ring_pairs(axis, step))]
    pallas_call x12, Pallas kernels: 36.5 us -> 32.6 us  [call(): pl.pallas_call(kernel, out_shape=out_shapes, grid_spec=pltpu.PrefetchScal...]
    all_to_all x1, starting transfers between devices: 7.87 us -> 5.12 us  [body(): lax.all_to_all(spread, 'tensor', split_axis=0, concat_axis=0, tiled=True)]
    all_to_all x1, starting transfers between devices: 6.41 us -> 4.8 us  [swap(): lax.all_to_all(value, 'tensor', split_axis=0, concat_axis=0, axis_index_g...]
  transfers between devices with their start and end apart: 17 -> 18, of which waited for: 9 -> 8; matrix products, arithmetic and copies ran while one was open for 1% -> 1% of each run, Pallas kernels for 24% -> 22%
where the time goes in v3:
time: 118 us; the launch traced here: 117 us
  starting transfers between devices  42.3 us (36%)
  waiting for transfers between devices  37.3 us (32%)
  Pallas kernels  32.6 us (28%)
  local copies, waits for them, and re-layouts  2.22 us (2%)
  other arithmetic  1.87 us (2%)
    pallas_call x12, Pallas kernels, call(): pl.pallas_call(kernel, out_shape=out_shapes, grid_spec=pltpu.PrefetchScal...  32.6 us
    ppermute x16, starting transfers between devices, shift(): return lax.ppermute(value, 'tensor', ring_pairs(axis, step))  32.4 us
    ppermute x16, waiting for transfers between devices, shift(): return lax.ppermute(value, 'tensor', ring_pairs(axis, step))  27.3 us
    all_to_all x1, waiting for transfers between devices, body(): lax.all_to_all(spread, 'tensor', split_axis=0, concat_axis=0, tiled=True)  10 us
    all_to_all x1, starting transfers between devices, body(): lax.all_to_all(spread, 'tensor', split_axis=0, concat_axis=0, tiled=True)  5.12 us
    all_to_all x1, starting transfers between devices, swap(): lax.all_to_all(value, 'tensor', split_axis=0, concat_axis=0, axis_index_g...  4.8 us
  transfers between devices with their start and end apart: 18, of which 8 were waited for; matrix products, arithmetic and copies ran while one was open for 1% of the time, Pallas kernels for 22%

profile of v3, /device:TPU:16, one launch (start us, length us, event | category | flops | bytes accessed | tf_op | source)
XLA Modules:
  0.0 117.1 jit_solution(8264076152862705324)
XLA Ops:
  0.7 5.1 %attend_0.1 = (bf16[384,512]{1,0:T(8,128)(2,1)S(1)}, bf16[384,1024]{1,0:T(8,128)(2,1)S(1)}, bf16[384,1024]{1,0:T(8,128)(2,1)S(1)}, f32[8,128]{1,0:T(8,128)S(1)}) custom-call(s32[4]{0:T(128)S(1)} %pad_add_fusion.where_ref.token_ref, s32[4]{0:T(128)S(1)} %pad_add_fusion.where_ref.token_ref, s32[16,1024]{1,0:T(8,128)} %docs_hbm.5, bf16[1024,512]{1,0:T(8,128)(2,1)} %q_hbm.5, ...), custom_call_target="tpu_custom_call" | custom-call | flops 1 | bytes 1 | tf_op jit(solution)/shard_map/attend_0/pallas_call | solution.py:59
  5.8 2.8 %collective-permute-start = (bf16[384,1024]{1,0:T(8,128)(2,1)S(1)}, bf16[384,1024]{1,0:T(8,128)(2,1)S(1)}, u32[]{:S(2)}, u32[]{:S(2)}) collective-permute-start(bf16[384,1024]{1,0:T(8,128)(2,1)S(1)} %get-tuple-element.53), channel_id=1, source_target_pairs={{0,3},{1,0},{2,1},{3,2},{4,7},{5,4},{6,5},{7,6},{8,11},{9,8},{10,9... | collective-permute-start | bytes 2359304 | tf_op jit(solution)/shard_map/ppermute | solution.py:43
  8.7 4.0 %attend_384.1 = (bf16[256,512]{1,0:T(8,128)(2,1)S(1)}, bf16[256,1024]{1,0:T(8,128)(2,1)S(1)}, bf16[256,1024]{1,0:T(8,128)(2,1)S(1)}, f32[8,128]{1,0:T(8,128)S(1)}) custom-call(s32[4]{0:T(128)S(1)} %pad_add_fusion.where_ref.token_ref, f32[8,128]{1,0:T(8,128)S(1)} %get-tuple-element.49.token_ref, s32[16,1024]{1,0:T(8,128)} %docs_hbm.5, ...), custom_call_target="tpu_custom_call" | custom-call | flops 1 | bytes 1 | tf_op jit(solution)/shard_map/attend_384/pallas_call | solution.py:59
  12.7 3.3 %collective-permute-start.2 = (bf16[256,1024]{1,0:T(8,128)(2,1)S(1)}, bf16[256,1024]{1,0:T(8,128)(2,1)S(1)}, u32[]{:S(2)}, u32[]{:S(2)}) collective-permute-start(bf16[256,1024]{1,0:T(8,128)(2,1)S(1)} %get-tuple-element.58), channel_id=1, source_target_pairs={{0,4},{1,5},{2,6},{3,7},{4,8},{5,9},{6,10},{7,11},{8,12},{9,13},{1... | collective-permute-start | bytes 1572872 | tf_op jit(solution)/shard_map/ppermute | solution.py:43
  16.0 3.1 %collective-permute-start.3 = (bf16[256,1024]{1,0:T(8,128)(2,1)S(1)}, bf16[256,1024]{1,0:T(8,128)(2,1)S(1)}, u32[]{:S(2)}, u32[]{:S(2)}) collective-permute-start(bf16[256,1024]{1,0:T(8,128)(2,1)S(1)} %get-tuple-element.59), channel_id=1, source_target_pairs={{0,12},{1,13},{2,14},{3,15},{4,0},{5,1},{6,2},{7,3},{8,4},{9,5},{1... | collective-permute-start | bytes 1572872 | tf_op jit(solution)/shard_map/ppermute | solution.py:43
  19.2 7.1 %attend_640.1 = (bf16[384,512]{1,0:T(8,128)(2,1)S(1)}, bf16[384,1024]{1,0:T(8,128)(2,1)}, bf16[384,1024]{1,0:T(8,128)(2,1)}, f32[8,128]{1,0:T(8,128)S(1)}) custom-call(s32[4]{0:T(128)S(1)} %pad_add_fusion.where_ref.token_ref, f32[8,128]{1,0:T(8,128)S(1)} %get-tuple-element.50.token_ref, s32[16,1024]{1,0:T(8,128)} %docs_hbm.5, bf16[1024,512]{1,0:T(8,128)(2,1)} %q_hbm.5, ...), custom_call_target="tpu_custom_call" | custom-call | flops 1 | bytes 1 | tf_op jit(solution)/shard_map/attend_640/pallas_call | solution.py:59
  26.3 3.5 %collective-permute-start.4 = (bf16[384,1024]{1,0:T(8,128)(2,1)}, bf16[384,1024]{1,0:T(8,128)(2,1)}, u32[]{:S(2)}, u32[]{:S(2)}) collective-permute-start(bf16[384,1024]{1,0:T(8,128)(2,1)} %get-tuple-element.62), channel_id=1, source_target_pairs={{0,3},{1,0},{2,1},{3,2},{4,7},{5,4},{6,5},{7,6},{8,11},{9,8},{10,9... | collective-permute-start | bytes 2359304 | tf_op jit(solution)/shard_map/ppermute | solution.py:43
  29.8 2.1 %near.2 = (bf16[384,1024]{1,0:T(8,128)(2,1)}, bf16[384,1024]{1,0:T(8,128)(2,1)S(1)}, f32[8,128]{1,0:T(8,128)S(1)}) custom-call(s32[4]{0:T(128)S(1)} %pad_add_fusion.where_ref.token_ref, f32[8,128]{1,0:T(8,128)S(1)} %get-tuple-element.51.token_ref, bf16[512,4096]{1,0:T(8,128)(2,1)S(1)} %copy-done, bf16[384,512]{1,0:T(8,128)(2,1)S(1)} %get-tuple-element.54.attn_ref, ...), custom_call_target="tpu_custom_call" | custom-call | flops 1 | bytes 1 | tf_op jit(solution)/shard_map/near/pallas_call | solution.py:59
  31.9 3.2 %collective-permute-done.2.up_ref = bf16[256,1024]{1,0:T(8,128)(2,1)S(1)} collective-permute-done((bf16[256,1024]{1,0:T(8,128)(2,1)S(1)}, bf16[256,1024]{1,0:T(8,128)(2,1)S(1)}, u32[]{:S(2)}, u32[]{:S(2)}) %collective-permute-start.2) | collective-permute-done | bytes 524320 | tf_op jit(solution)/shard_map/ppermute | solution.py:43
  35.1 8.0 %collective-permute-done.3.down_ref = bf16[256,1024]{1,0:T(8,128)(2,1)S(1)} collective-permute-done((bf16[256,1024]{1,0:T(8,128)(2,1)S(1)}, bf16[256,1024]{1,0:T(8,128)(2,1)S(1)}, u32[]{:S(2)}, u32[]{:S(2)}) %collective-permute-start.3) | collective-permute-done | bytes 524320 | tf_op jit(solution)/shard_map/ppermute | solution.py:43
  43.1 1.3 %near_both.1 = (bf16[256,512]{1,0:T(8,128)(2,1)S(1)}, bf16[256,512]{1,0:T(8,128)(2,1)S(1)}, f32[256,1024]{1,0:T(8,128)S(1)}, f32[8,128]{1,0:T(8,128)S(1)}) custom-call(s32[4]{0:T(128)S(1)} %pad_add_fusion.where_ref.token_ref, f32[8,128]{1,0:T(8,128)S(1)} %get-tuple-element.56.token_ref, bf16[512,4096]{1,0:T(8,128)(2,1)S(1)} %copy-done, ...), custom_call_target="tpu_custom_call" | custom-call | flops 199999995904 | bytes 1 | tf_op jit(solution)/shard_map/near_both/pallas_call | solution.py:59
  44.4 3.9 %collective-permute-start.6 = (bf16[256,512]{1,0:T(8,128)(2,1)S(1)}, bf16[256,512]{1,0:T(8,128)(2,1)S(1)}, u32[]{:S(2)}, u32[]{:S(2)}) collective-permute-start(bf16[256,512]{1,0:T(8,128)(2,1)S(1)} %get-tuple-element.68), channel_id=1, source_target_pairs={{0,4},{1,5},{2,6},{3,7},{4,8},{5,9},{6,10},{7,11},{8,12},{9,13},{1... | collective-permute-start | bytes 786440 | tf_op jit(solution)/shard_map/ppermute | solution.py:43
  48.7 3.2 %near.3 = (bf16[384,1024]{1,0:T(8,128)(2,1)}, bf16[384,1024]{1,0:T(8,128)(2,1)S(1)}, f32[8,128]{1,0:T(8,128)S(1)}) custom-call(s32[4]{0:T(128)S(1)} %pad_add_fusion.where_ref.token_ref, f32[8,128]{1,0:T(8,128)S(1)} %get-tuple-element.60.token_ref, bf16[512,4096]{1,0:T(8,128)(2,1)S(1)} %copy-done, bf16[384,512]{1,0:T(8,128)(2,1)S(1)} %get-tuple-element.61.attn_ref, ...), custom_call_target="tpu_custom_call" | custom-call | flops 1 | bytes 1 | tf_op jit(solution)/shard_map/near/pallas_call | solution.py:59
  52.3 2.8 %collective-permute-start.8 = (bf16[384,1024]{1,0:T(8,128)(2,1)}, bf16[384,1024]{1,0:T(8,128)(2,1)}, u32[]{:S(2)}, u32[]{:S(2)}) collective-permute-start(bf16[384,1024]{1,0:T(8,128)(2,1)} %get-tuple-element.72), channel_id=1, source_target_pairs={{0,3},{1,0},{2,1},{3,2},{4,7},{5,4},{6,5},{7,6},{8,11},{9,8},{10,9... | collective-permute-start | bytes 2359304 | tf_op jit(solution)/shard_map/ppermute | solution.py:43
  55.1 2.9 %merge.2 = (bf16[4,384,256]{2,1,0:T(8,128)(2,1)}, f32[8,128]{1,0:T(8,128)S(1)}) custom-call(s32[4]{0:T(128)S(1)} %pad_add_fusion.where_ref.token_ref, f32[8,128]{1,0:T(8,128)S(1)} %get-tuple-element.63.token_ref, bf16[384,1024]{1,0:T(8,128)(2,1)S(1)} %get-tuple-element.64.own_ref, bf16[384,1024]{1,0:T(8,128)(2,1)} %collective-permute-done.5.ahead_ref, ...), custom_call_target="tpu_custom_call" | custom-call | flops 1 | bytes 1 | tf_op jit(solution)/shard_map/merge/pallas_call | solution.py:59
  58.0 4.8 %all-to-all-start = ((bf16[4,384,256]{2,1,0:T(8,128)(2,1)}), bf16[4,384,256]{2,1,0:T(8,128)(2,1)}, u32[]{:S(2)}, u32[]{:S(2)}) async-start(bf16[4,384,256]{2,1,0:T(8,128)(2,1)} %get-tuple-element.76), calls=%async_computation | async-start | bytes 1572864 | tf_op jit(solution)/shard_map/all_to_all | solution.py:51
  62.8 1.2 %copy-done.3 = f32[256,1024]{1,0:T(8,128)S(1)} copy-done((f32[256,1024]{1,0:T(8,128)S(1)}, f32[256,1024]{1,0:T(8,128)}, u32[]{:S(2)}) %copy-start.3) | copy-done | bytes 1048600
  64.8 7.1 %collective-permute-done.9.behind_ref = bf16[384,1024]{1,0:T(8,128)(2,1)} collective-permute-done((bf16[384,1024]{1,0:T(8,128)(2,1)}, bf16[384,1024]{1,0:T(8,128)(2,1)}, u32[]{:S(2)}, u32[]{:S(2)}) %collective-permute-start.9) | collective-permute-done | bytes 786464 | tf_op jit(solution)/shard_map/ppermute | solution.py:43
  71.9 2.2 %merge.3 = (bf16[384,256]{1,0:T(8,128)(2,1)S(1)}, bf16[384,256]{1,0:T(8,128)(2,1)S(1)}, bf16[384,256]{1,0:T(8,128)(2,1)S(1)}, bf16[384,256]{1,0:T(8,128)(2,1)S(1)}, f32[8,128]{1,0:T(8,128)S(1)}) custom-call(s32[4]{0:T(128)S(1)} %pad_add_fusion.where_ref.token_ref, f32[8,128]{1,0:T(8,128)S(1)} %get-tuple-element.70.token_ref, ...), custom_call_target="tpu_custom_call" | custom-call | flops 1 | bytes 1 | tf_op jit(solution)/shard_map/merge/pallas_call | solution.py:59
  74.1 3.0 %collective-permute-start.12 = (bf16[256,256]{1,0:T(8,128)(2,1)S(1)}, bf16[256,256]{1,0:T(8,128)(2,1)S(1)}, u32[]{:S(2)}, u32[]{:S(2)}) collective-permute-start(bf16[256,256]{1,0:T(8,128)(2,1)S(1)} %get-tuple-element.85), channel_id=1, source_target_pairs={{0,2},{1,3},{2,0},{3,1},{4,6},{5,7},{6,4},{7,5},{8,10},{9,11},{10,... | collective-permute-start | bytes 393224 | tf_op jit(solution)/shard_map/ppermute | solution.py:43
  77.1 1.7 %collective-permute-start.13 = (bf16[384,256]{1,0:T(8,128)(2,1)S(1)}, bf16[384,256]{1,0:T(8,128)(2,1)S(1)}, u32[]{:S(2)}, u32[]{:S(2)}) collective-permute-start(bf16[384,256]{1,0:T(8,128)(2,1)S(1)} %get-tuple-element.89), channel_id=1, source_target_pairs={{0,4},{1,5},{2,6},{3,7},{4,8},{5,9},{6,10},{7,11},{8,12},{9,13},{1... | collective-permute-start | bytes 589832 | tf_op jit(solution)/shard_map/ppermute | solution.py:43
  78.8 2.4 %collective-permute-start.14 = (bf16[384,256]{1,0:T(8,128)(2,1)S(1)}, bf16[384,256]{1,0:T(8,128)(2,1)S(1)}, u32[]{:S(2)}, u32[]{:S(2)}) collective-permute-start(bf16[384,256]{1,0:T(8,128)(2,1)S(1)} %get-tuple-element.90), channel_id=1, source_target_pairs={{0,12},{1,13},{2,14},{3,15},{4,0},{5,1},{6,2},{7,3},{8,4},{9,5},{1... | collective-permute-start | bytes 589832 | tf_op jit(solution)/shard_map/ppermute | solution.py:43
  81.2 3.0 %collective-permute-start.15 = (bf16[384,256]{1,0:T(8,128)(2,1)S(1)}, bf16[384,256]{1,0:T(8,128)(2,1)S(1)}, u32[]{:S(2)}, u32[]{:S(2)}) collective-permute-start(bf16[384,256]{1,0:T(8,128)(2,1)S(1)} %get-tuple-element.91), channel_id=1, source_target_pairs={{0,8},{1,9},{2,10},{3,11},{4,12},{5,13},{6,14},{7,15},{8,0},{9,1},... | collective-permute-start | bytes 589832 | tf_op jit(solution)/shard_map/ppermute | solution.py:43
  85.1 1.1 collective-permute-start.10
  87.0 1.9 %final.3 = (bf16[384,256]{1,0:T(8,128)(2,1)S(1)}, f32[384,1]{1,0:T(8,128)S(1)}, f32[8,128]{1,0:T(8,128)S(1)}) custom-call(s32[4]{0:T(128)S(1)} %pad_add_fusion.where_ref.token_ref, f32[8,128]{1,0:T(8,128)S(1)} %get-tuple-element.75.token_ref, bf16[1024,256]{1,0:T(8,128)(2,1)S(1)} %copy-done.1, bf16[4,384,256]{2,1,0:T(8,128)(2,1)} %all-to-all-done.parts_ref), custom_call_target="tpu_custom_call" | custom-call | flops 1 | bytes 1 | tf_op jit(solution)/shard_map/final/pallas_call | solution.py:59
  89.2 2.1 %collective-permute-done.10.rest_0_ = bf16[256,256]{1,0:T(8,128)(2,1)S(1)} collective-permute-done((bf16[256,256]{1,0:T(8,128)(2,1)S(1)}, bf16[256,256]{1,0:T(8,128)(2,1)S(1)}, u32[]{:S(2)}, u32[]{:S(2)}) %collective-permute-start.10) | collective-permute-done | bytes 131104 | tf_op jit(solution)/shard_map/ppermute | solution.py:43
  92.0 1.0 collective-permute-done.13.rest_0_
  93.0 5.6 %collective-permute-done.15.rest_2_ = bf16[384,256]{1,0:T(8,128)(2,1)S(1)} collective-permute-done((bf16[384,256]{1,0:T(8,128)(2,1)S(1)}, bf16[384,256]{1,0:T(8,128)(2,1)S(1)}, u32[]{:S(2)}, u32[]{:S(2)}) %collective-permute-start.15) | collective-permute-done | bytes 196640 | tf_op jit(solution)/shard_map/ppermute | solution.py:43
  98.6 1.3 %final.5 = (bf16[384,256]{1,0:T(8,128)(2,1)S(1)}, f32[384,1]{1,0:T(8,128)S(1)}, f32[8,128]{1,0:T(8,128)}) custom-call(s32[4]{0:T(128)S(1)} %pad_add_fusion.where_ref.token_ref, f32[8,128]{1,0:T(8,128)S(1)} %get-tuple-element.87.token_ref, bf16[1024,256]{1,0:T(8,128)(2,1)S(1)} %copy-done.1, bf16[384,256]{1,0:T(8,128)(2,1)S(1)} %get-tuple-element.88.parts_ref, ...), custom_call_target="tpu_custom_call" | custom-call | flops 1 | bytes 1 | tf_op jit(solution)/shard_map/final/pallas_call | solution.py:59
  100.9 5.1 %all-to-all-start.1 = ((f32[16,8,128]{2,1,0:T(8,128)}), f32[16,8,128]{2,1,0:T(8,128)S(1)}, u32[]{:S(2)}, u32[]{:S(2)}) async-start(f32[16,8,128]{2,1,0:T(8,128)} %tile.9), calls=%async_computation.1 | async-start | bytes 131072 | tf_op jit(solution)/shard_map/all_to_all | solution.py:430
  106.1 10.0 %all-to-all-done.1 = f32[16,8,128]{2,1,0:T(8,128)S(1)} async-done(((f32[16,8,128]{2,1,0:T(8,128)}), f32[16,8,128]{2,1,0:T(8,128)S(1)}, u32[]{:S(2)}, u32[]{:S(2)}) %all-to-all-start.1) | async-done | bytes 65568 | tf_op jit(solution)/shard_map/all_to_all | solution.py:430
  116.1 1.0 multiply_convert_fusion
  (39 shorter events, 5.2 us)
Async XLA Ops:
  0.7 7.9 %copy-start = (bf16[512,4096]{1,0:T(8,128)(2,1)S(1)}, bf16[512,4096]{1,0:T(8,128)(2,1)}, u32[]{:S(2)}) copy-start(bf16[512,4096]{1,0:T(8,128)(2,1)} %w_ref.5) | copy-start | bytes 12582916
  5.8 23.9 %collective-permute-start = (bf16[384,1024]{1,0:T(8,128)(2,1)S(1)}, bf16[384,1024]{1,0:T(8,128)(2,1)S(1)}, u32[]{:S(2)}, u32[]{:S(2)}) collective-permute-start(bf16[384,1024]{1,0:T(8,128)(2,1)S(1)} %get-tuple-element.53), channel_id=1, source_target_pairs={{0,3},{1,0},{2,1},{3,2},{4,7},{5,4},{6,5},{7,6},{8,11},{9,8},{10,9... | collective-permute-start | bytes 2359304 | tf_op jit(solution)/shard_map/ppermute | solution.py:43
  8.7 21.1 %collective-permute-start.1 = (bf16[384,1024]{1,0:T(8,128)(2,1)S(1)}, bf16[384,1024]{1,0:T(8,128)(2,1)S(1)}, u32[]{:S(2)}, u32[]{:S(2)}) collective-permute-start(bf16[384,1024]{1,0:T(8,128)(2,1)S(1)} %get-tuple-element.55), channel_id=1, source_target_pairs={{0,1},{1,2},{2,3},{3,0},{4,5},{5,6},{6,7},{7,4},{8,9},{9,10},{10,1... | collective-permute-start | bytes 2359304 | tf_op jit(solution)/shard_map/ppermute | solution.py:43
  12.7 22.4 %collective-permute-start.2 = (bf16[256,1024]{1,0:T(8,128)(2,1)S(1)}, bf16[256,1024]{1,0:T(8,128)(2,1)S(1)}, u32[]{:S(2)}, u32[]{:S(2)}) collective-permute-start(bf16[256,1024]{1,0:T(8,128)(2,1)S(1)} %get-tuple-element.58), channel_id=1, source_target_pairs={{0,4},{1,5},{2,6},{3,7},{4,8},{5,9},{6,10},{7,11},{8,12},{9,13},{1... | collective-permute-start | bytes 1572872 | tf_op jit(solution)/shard_map/ppermute | solution.py:43
  16.0 27.1 %collective-permute-start.3 = (bf16[256,1024]{1,0:T(8,128)(2,1)S(1)}, bf16[256,1024]{1,0:T(8,128)(2,1)S(1)}, u32[]{:S(2)}, u32[]{:S(2)}) collective-permute-start(bf16[256,1024]{1,0:T(8,128)(2,1)S(1)} %get-tuple-element.59), channel_id=1, source_target_pairs={{0,12},{1,13},{2,14},{3,15},{4,0},{5,1},{6,2},{7,3},{8,4},{9,5},{1... | collective-permute-start | bytes 1572872 | tf_op jit(solution)/shard_map/ppermute | solution.py:43
  26.3 22.4 %collective-permute-start.4 = (bf16[384,1024]{1,0:T(8,128)(2,1)}, bf16[384,1024]{1,0:T(8,128)(2,1)}, u32[]{:S(2)}, u32[]{:S(2)}) collective-permute-start(bf16[384,1024]{1,0:T(8,128)(2,1)} %get-tuple-element.62), channel_id=1, source_target_pairs={{0,3},{1,0},{2,1},{3,2},{4,7},{5,4},{6,5},{7,6},{8,11},{9,8},{10,9... | collective-permute-start | bytes 2359304 | tf_op jit(solution)/shard_map/ppermute | solution.py:43
  31.9 23.2 %collective-permute-start.5 = (bf16[384,1024]{1,0:T(8,128)(2,1)}, bf16[384,1024]{1,0:T(8,128)(2,1)}, u32[]{:S(2)}, u32[]{:S(2)}) collective-permute-start(bf16[384,1024]{1,0:T(8,128)(2,1)} %get-tuple-element.65), channel_id=1, source_target_pairs={{0,1},{1,2},{2,3},{3,0},{4,5},{5,6},{6,7},{7,4},{8,9},{9,10},{10,1... | collective-permute-start | bytes 2359304 | tf_op jit(solution)/shard_map/ppermute | solution.py:43
  44.4 13.6 %copy-start.2 = (f32[256,1024]{1,0:T(8,128)}, f32[256,1024]{1,0:T(8,128)S(1)}, u32[]{:S(2)}) copy-start(f32[256,1024]{1,0:T(8,128)S(1)} %get-tuple-element.67.own_ref) | copy-start | bytes 3145732
  44.4 18.4 %collective-permute-start.6 = (bf16[256,512]{1,0:T(8,128)(2,1)S(1)}, bf16[256,512]{1,0:T(8,128)(2,1)S(1)}, u32[]{:S(2)}, u32[]{:S(2)}) collective-permute-start(bf16[256,512]{1,0:T(8,128)(2,1)S(1)} %get-tuple-element.68), channel_id=1, source_target_pairs={{0,4},{1,5},{2,6},{3,7},{4,8},{5,9},{6,10},{7,11},{8,12},{9,13},{1... | collective-permute-start | bytes 786440 | tf_op jit(solution)/shard_map/ppermute | solution.py:43
  48.4 14.5 %collective-permute-start.7 = (bf16[256,512]{1,0:T(8,128)(2,1)S(1)}, bf16[256,512]{1,0:T(8,128)(2,1)S(1)}, u32[]{:S(2)}, u32[]{:S(2)}) collective-permute-start(bf16[256,512]{1,0:T(8,128)(2,1)S(1)} %get-tuple-element.69), channel_id=1, source_target_pairs={{0,12},{1,13},{2,14},{3,15},{4,0},{5,1},{6,2},{7,3},{8,4},{9,5},{1... | collective-permute-start | bytes 786440 | tf_op jit(solution)/shard_map/ppermute | solution.py:43
  51.9 20.0 %collective-permute-start.9 = (bf16[384,1024]{1,0:T(8,128)(2,1)}, bf16[384,1024]{1,0:T(8,128)(2,1)}, u32[]{:S(2)}, u32[]{:S(2)}) collective-permute-start(bf16[384,1024]{1,0:T(8,128)(2,1)} %get-tuple-element.74), channel_id=1, source_target_pairs={{0,1},{1,2},{2,3},{3,0},{4,5},{5,6},{6,7},{7,4},{8,9},{9,10},{10,1... | collective-permute-start | bytes 2359304 | tf_op jit(solution)/shard_map/ppermute | solution.py:43
  52.3 19.6 %collective-permute-start.8 = (bf16[384,1024]{1,0:T(8,128)(2,1)}, bf16[384,1024]{1,0:T(8,128)(2,1)}, u32[]{:S(2)}, u32[]{:S(2)}) collective-permute-start(bf16[384,1024]{1,0:T(8,128)(2,1)} %get-tuple-element.72), channel_id=1, source_target_pairs={{0,3},{1,0},{2,1},{3,2},{4,7},{5,4},{6,5},{7,6},{8,11},{9,8},{10,9... | collective-permute-start | bytes 2359304 | tf_op jit(solution)/shard_map/ppermute | solution.py:43
  58.0 29.0 %all-to-all-start = ((bf16[4,384,256]{2,1,0:T(8,128)(2,1)}), bf16[4,384,256]{2,1,0:T(8,128)(2,1)}, u32[]{:S(2)}, u32[]{:S(2)}) async-start(bf16[4,384,256]{2,1,0:T(8,128)(2,1)} %get-tuple-element.76), calls=%async_computation | async-start | bytes 1572864 | tf_op jit(solution)/shard_map/all_to_all | solution.py:51
  62.8 1.2 %copy-start.3 = (f32[256,1024]{1,0:T(8,128)S(1)}, f32[256,1024]{1,0:T(8,128)}, u32[]{:S(2)}) copy-start(f32[256,1024]{1,0:T(8,128)} %copy-done.2) | copy-start | bytes 3145732
  64.1 23.0 %copy-start.1 = (bf16[1024,256]{1,0:T(8,128)(2,1)S(1)}, bf16[1024,256]{1,0:T(8,128)(2,1)}, u32[]{:S(2)}) copy-start(bf16[1024,256]{1,0:T(8,128)(2,1)} %residual_ref.5) | copy-start | bytes 1572868
  74.1 11.0 %collective-permute-start.12 = (bf16[256,256]{1,0:T(8,128)(2,1)S(1)}, bf16[256,256]{1,0:T(8,128)(2,1)S(1)}, u32[]{:S(2)}, u32[]{:S(2)}) collective-permute-start(bf16[256,256]{1,0:T(8,128)(2,1)S(1)} %get-tuple-element.85), channel_id=1, source_target_pairs={{0,2},{1,3},{2,0},{3,1},{4,6},{5,7},{6,4},{7,5},{8,10},{9,11},{10,... | collective-permute-start | bytes 393224 | tf_op jit(solution)/shard_map/ppermute | solution.py:43
  77.1 15.9 %collective-permute-start.13 = (bf16[384,256]{1,0:T(8,128)(2,1)S(1)}, bf16[384,256]{1,0:T(8,128)(2,1)S(1)}, u32[]{:S(2)}, u32[]{:S(2)}) collective-permute-start(bf16[384,256]{1,0:T(8,128)(2,1)S(1)} %get-tuple-element.89), channel_id=1, source_target_pairs={{0,4},{1,5},{2,6},{3,7},{4,8},{5,9},{6,10},{7,11},{8,12},{9,13},{1... | collective-permute-start | bytes 589832 | tf_op jit(solution)/shard_map/ppermute | solution.py:43
  78.8 14.2 %collective-permute-start.14 = (bf16[384,256]{1,0:T(8,128)(2,1)S(1)}, bf16[384,256]{1,0:T(8,128)(2,1)S(1)}, u32[]{:S(2)}, u32[]{:S(2)}) collective-permute-start(bf16[384,256]{1,0:T(8,128)(2,1)S(1)} %get-tuple-element.90), channel_id=1, source_target_pairs={{0,12},{1,13},{2,14},{3,15},{4,0},{5,1},{6,2},{7,3},{8,4},{9,5},{1... | collective-permute-start | bytes 589832 | tf_op jit(solution)/shard_map/ppermute | solution.py:43
  81.2 17.4 %collective-permute-start.15 = (bf16[384,256]{1,0:T(8,128)(2,1)S(1)}, bf16[384,256]{1,0:T(8,128)(2,1)S(1)}, u32[]{:S(2)}, u32[]{:S(2)}) collective-permute-start(bf16[384,256]{1,0:T(8,128)(2,1)S(1)} %get-tuple-element.91), channel_id=1, source_target_pairs={{0,8},{1,9},{2,10},{3,11},{4,12},{5,13},{6,14},{7,15},{8,0},{9,1},... | collective-permute-start | bytes 589832 | tf_op jit(solution)/shard_map/ppermute | solution.py:43
  84.2 5.0 %collective-permute-start.11 = (bf16[256,256]{1,0:T(8,128)(2,1)S(1)}, bf16[256,256]{1,0:T(8,128)(2,1)S(1)}, u32[]{:S(2)}, u32[]{:S(2)}) collective-permute-start(bf16[256,256]{1,0:T(8,128)(2,1)S(1)} %get-tuple-element.83), channel_id=1, source_target_pairs={{0,3},{1,0},{2,1},{3,2},{4,7},{5,4},{6,5},{7,6},{8,11},{9,8},{10,9... | collective-permute-start | bytes 393224 | tf_op jit(solution)/shard_map/ppermute | solution.py:43
  85.1 6.2 %collective-permute-start.10 = (bf16[256,256]{1,0:T(8,128)(2,1)S(1)}, bf16[256,256]{1,0:T(8,128)(2,1)S(1)}, u32[]{:S(2)}, u32[]{:S(2)}) collective-permute-start(bf16[256,256]{1,0:T(8,128)(2,1)S(1)} %get-tuple-element.81), channel_id=1, source_target_pairs={{0,1},{1,2},{2,3},{3,0},{4,5},{5,6},{6,7},{7,4},{8,9},{9,10},{10,1... | collective-permute-start | bytes 393224 | tf_op jit(solution)/shard_map/ppermute | solution.py:43
  100.9 15.2 %all-to-all-start.1 = ((f32[16,8,128]{2,1,0:T(8,128)}), f32[16,8,128]{2,1,0:T(8,128)S(1)}, u32[]{:S(2)}, u32[]{:S(2)}) async-start(f32[16,8,128]{2,1,0:T(8,128)} %tile.9), calls=%async_computation.1 | async-start | bytes 131072 | tf_op jit(solution)/shard_map/all_to_all | solution.py:430
  106.1 11.1 %copy-start.4 = (bf16[1024,256]{1,0:T(8,128)(2,1)}, bf16[1024,256]{1,0:T(8,128)(2,1)S(1)}, u32[]{:S(2)}) copy-start(bf16[1024,256]{1,0:T(8,128)(2,1)S(1)} %constant_dynamic-update-slice_fusion) | copy-start | bytes 1572868

commit v4 on v3

--- a/solution.py
+++ b/solution.py
@@ -18,7 +18,7 @@
 WIDE = 256
 MASK_FILL = -1e30
 EPSILON = 1e-06
-PLAN = {"B": (0, 384, "x", 1, True), "A": (384, 256, "z", 0, False), "C": (640, 384, "x", -1, False)}
+PLAN = {"B": (0, 384, "x", 1, False), "A": (384, 256, "z", 0, False), "C": (640, 384, "x", -1, False)}
 ORDER = ("1B", "1A", "1C", "2B", "2A", "2C", "3B", "3A", "3C", "FB", "FA", "FC")
 GATES = {("C", 1, "back"): "2C", ("A", 2, 1): "3C", ("A", 2, 2): "3C", ("A", 2, 3): "3C"}
 COST = pl.CostEstimate(flops=1, bytes_accessed=1, transcendentals=0)

time: 118 us -> 117 us (level)
  waiting for transfers between devices: 37.3 us -> 32.7 us
  starting transfers between devices: 42.3 us -> 46.3 us
  local copies, waits for them, and re-layouts: 2.22 us -> 0.99 us
    ppermute x16 -> x19, starting transfers between devices: 32.4 us -> 41.1 us  [shift(): return lax.ppermute(value, 'tensor', ring_pairs(axis, step))]
    all_to_all x1 -> x0, starting transfers between devices: 4.8 us -> none  [swap(): lax.all_to_all(value, 'tensor', split_axis=0, concat_axis=0, axis_index_g...]
    ppermute x16 -> x19, waiting for transfers between devices: 27.3 us -> 22.7 us  [shift(): return lax.ppermute(value, 'tensor', ring_pairs(axis, step))]
    unnamed x12 -> x8, local copies, waits for them, and re-layouts: 1.26 us -> 0.04 us
  transfers between devices with their start and end apart: 18 -> 20, of which waited for: 8 -> 8; matrix products, arithmetic and copies ran while one was open for 1% -> 1% of each run, Pallas kernels for 22% -> 23%
where the time goes in v4:
time: 117 us; the launch traced here: 116 us
  starting transfers between devices  46.3 us (40%)
  Pallas kernels  33 us (28%)
  waiting for transfers between devices  32.7 us (28%)
  other arithmetic  1.87 us (2%)
    ppermute x19, starting transfers between devices, shift(): return lax.ppermute(value, 'tensor', ring_pairs(axis, step))  41.1 us
    pallas_call x12, Pallas kernels, call(): pl.pallas_call(kernel, out_shape=out_shapes, grid_spec=pltpu.PrefetchScal...  33 us
    ppermute x19, waiting for transfers between devices, shift(): return lax.ppermute(value, 'tensor', ring_pairs(axis, step))  22.7 us
    all_to_all x1, waiting for transfers between devices, body(): lax.all_to_all(spread, 'tensor', split_axis=0, concat_axis=0, tiled=True)  10 us
    all_to_all x1, starting transfers between devices, body(): lax.all_to_all(spread, 'tensor', split_axis=0, concat_axis=0, tiled=True)  5.29 us
  transfers between devices with their start and end apart: 20, of which 8 were waited for; matrix products, arithmetic and copies ran while one was open for 1% of the time, Pallas kernels for 23%

profile of v4, /device:TPU:16, one launch (start us, length us, event | category | flops | bytes accessed | tf_op | source)
XLA Modules:
  0.0 115.7 jit_solution(10383109159162955387)
XLA Ops:
  0.7 5.1 %attend_0.1 = (bf16[384,512]{1,0:T(8,128)(2,1)S(1)}, bf16[384,1024]{1,0:T(8,128)(2,1)S(1)}, bf16[384,1024]{1,0:T(8,128)(2,1)S(1)}, f32[8,128]{1,0:T(8,128)S(1)}) custom-call(s32[4]{0:T(128)S(1)} %pad_add_fusion.where_ref.token_ref, s32[4]{0:T(128)S(1)} %pad_add_fusion.where_ref.token_ref, s32[16,1024]{1,0:T(8,128)} %docs_hbm.5, bf16[1024,512]{1,0:T(8,128)(2,1)} %q_hbm.5, ...), custom_call_target="tpu_custom_call" | custom-call | flops 1 | bytes 1 | tf_op jit(solution)/shard_map/attend_0/pallas_call | solution.py:59
  5.8 2.8 %collective-permute-start = (bf16[384,1024]{1,0:T(8,128)(2,1)S(1)}, bf16[384,1024]{1,0:T(8,128)(2,1)S(1)}, u32[]{:S(2)}, u32[]{:S(2)}) collective-permute-start(bf16[384,1024]{1,0:T(8,128)(2,1)S(1)} %get-tuple-element.56), channel_id=1, source_target_pairs={{0,3},{1,0},{2,1},{3,2},{4,7},{5,4},{6,5},{7,6},{8,11},{9,8},{10,9... | collective-permute-start | bytes 2359304 | tf_op jit(solution)/shard_map/ppermute | solution.py:43
  8.7 4.0 %attend_384.1 = (bf16[256,512]{1,0:T(8,128)(2,1)S(1)}, bf16[256,1024]{1,0:T(8,128)(2,1)S(1)}, bf16[256,1024]{1,0:T(8,128)(2,1)S(1)}, f32[8,128]{1,0:T(8,128)S(1)}) custom-call(s32[4]{0:T(128)S(1)} %pad_add_fusion.where_ref.token_ref, f32[8,128]{1,0:T(8,128)S(1)} %get-tuple-element.52.token_ref, s32[16,1024]{1,0:T(8,128)} %docs_hbm.5, ...), custom_call_target="tpu_custom_call" | custom-call | flops 1 | bytes 1 | tf_op jit(solution)/shard_map/attend_384/pallas_call | solution.py:59
  12.7 3.3 %collective-permute-start.2 = (bf16[256,1024]{1,0:T(8,128)(2,1)S(1)}, bf16[256,1024]{1,0:T(8,128)(2,1)S(1)}, u32[]{:S(2)}, u32[]{:S(2)}) collective-permute-start(bf16[256,1024]{1,0:T(8,128)(2,1)S(1)} %get-tuple-element.61), channel_id=1, source_target_pairs={{0,4},{1,5},{2,6},{3,7},{4,8},{5,9},{6,10},{7,11},{8,12},{9,13},{1... | collective-permute-start | bytes 1572872 | tf_op jit(solution)/shard_map/ppermute | solution.py:43
  16.0 3.1 %collective-permute-start.3 = (bf16[256,1024]{1,0:T(8,128)(2,1)S(1)}, bf16[256,1024]{1,0:T(8,128)(2,1)S(1)}, u32[]{:S(2)}, u32[]{:S(2)}) collective-permute-start(bf16[256,1024]{1,0:T(8,128)(2,1)S(1)} %get-tuple-element.62), channel_id=1, source_target_pairs={{0,12},{1,13},{2,14},{3,15},{4,0},{5,1},{6,2},{7,3},{8,4},{9,5},{1... | collective-permute-start | bytes 1572872 | tf_op jit(solution)/shard_map/ppermute | solution.py:43
  19.2 7.1 %attend_640.1 = (bf16[384,512]{1,0:T(8,128)(2,1)S(1)}, bf16[384,1024]{1,0:T(8,128)(2,1)}, bf16[384,1024]{1,0:T(8,128)(2,1)}, f32[8,128]{1,0:T(8,128)S(1)}) custom-call(s32[4]{0:T(128)S(1)} %pad_add_fusion.where_ref.token_ref, f32[8,128]{1,0:T(8,128)S(1)} %get-tuple-element.53.token_ref, s32[16,1024]{1,0:T(8,128)} %docs_hbm.5, bf16[1024,512]{1,0:T(8,128)(2,1)} %q_hbm.5, ...), custom_call_target="tpu_custom_call" | custom-call | flops 1 | bytes 1 | tf_op jit(solution)/shard_map/attend_640/pallas_call | solution.py:59
  26.2 3.5 %collective-permute-start.4 = (bf16[384,1024]{1,0:T(8,128)(2,1)}, bf16[384,1024]{1,0:T(8,128)(2,1)}, u32[]{:S(2)}, u32[]{:S(2)}) collective-permute-start(bf16[384,1024]{1,0:T(8,128)(2,1)} %get-tuple-element.65), channel_id=1, source_target_pairs={{0,3},{1,0},{2,1},{3,2},{4,7},{5,4},{6,5},{7,6},{8,11},{9,8},{10,9... | collective-permute-start | bytes 2359304 | tf_op jit(solution)/shard_map/ppermute | solution.py:43
  29.8 2.1 %near.2 = (bf16[384,1024]{1,0:T(8,128)(2,1)}, bf16[384,1024]{1,0:T(8,128)(2,1)S(1)}, f32[8,128]{1,0:T(8,128)S(1)}) custom-call(s32[4]{0:T(128)S(1)} %pad_add_fusion.where_ref.token_ref, f32[8,128]{1,0:T(8,128)S(1)} %get-tuple-element.54.token_ref, bf16[512,4096]{1,0:T(8,128)(2,1)S(1)} %copy-done, bf16[384,512]{1,0:T(8,128)(2,1)S(1)} %get-tuple-element.57.attn_ref, ...), custom_call_target="tpu_custom_call" | custom-call | flops 1 | bytes 1 | tf_op jit(solution)/shard_map/near/pallas_call | solution.py:59
  31.8 3.3 %collective-permute-done.2.up_ref = bf16[256,1024]{1,0:T(8,128)(2,1)S(1)} collective-permute-done((bf16[256,1024]{1,0:T(8,128)(2,1)S(1)}, bf16[256,1024]{1,0:T(8,128)(2,1)S(1)}, u32[]{:S(2)}, u32[]{:S(2)}) %collective-permute-start.2) | collective-permute-done | bytes 524320 | tf_op jit(solution)/shard_map/ppermute | solution.py:43
  35.2 8.0 %collective-permute-done.3.down_ref = bf16[256,1024]{1,0:T(8,128)(2,1)S(1)} collective-permute-done((bf16[256,1024]{1,0:T(8,128)(2,1)S(1)}, bf16[256,1024]{1,0:T(8,128)(2,1)S(1)}, u32[]{:S(2)}, u32[]{:S(2)}) %collective-permute-start.3) | collective-permute-done | bytes 524320 | tf_op jit(solution)/shard_map/ppermute | solution.py:43
  43.1 1.3 %near_both.1 = (bf16[256,512]{1,0:T(8,128)(2,1)S(1)}, bf16[256,512]{1,0:T(8,128)(2,1)S(1)}, f32[256,1024]{1,0:T(8,128)S(1)}, f32[8,128]{1,0:T(8,128)S(1)}) custom-call(s32[4]{0:T(128)S(1)} %pad_add_fusion.where_ref.token_ref, f32[8,128]{1,0:T(8,128)S(1)} %get-tuple-element.59.token_ref, bf16[512,4096]{1,0:T(8,128)(2,1)S(1)} %copy-done, ...), custom_call_target="tpu_custom_call" | custom-call | flops 199999995904 | bytes 1 | tf_op jit(solution)/shard_map/near_both/pallas_call | solution.py:59
  44.4 3.9 %collective-permute-start.6 = (bf16[256,512]{1,0:T(8,128)(2,1)S(1)}, bf16[256,512]{1,0:T(8,128)(2,1)S(1)}, u32[]{:S(2)}, u32[]{:S(2)}) collective-permute-start(bf16[256,512]{1,0:T(8,128)(2,1)S(1)} %get-tuple-element.71), channel_id=1, source_target_pairs={{0,4},{1,5},{2,6},{3,7},{4,8},{5,9},{6,10},{7,11},{8,12},{9,13},{1... | collective-permute-start | bytes 786440 | tf_op jit(solution)/shard_map/ppermute | solution.py:43
  48.7 3.3 %near.3 = (bf16[384,1024]{1,0:T(8,128)(2,1)}, bf16[384,1024]{1,0:T(8,128)(2,1)S(1)}, f32[8,128]{1,0:T(8,128)S(1)}) custom-call(s32[4]{0:T(128)S(1)} %pad_add_fusion.where_ref.token_ref, f32[8,128]{1,0:T(8,128)S(1)} %get-tuple-element.63.token_ref, bf16[512,4096]{1,0:T(8,128)(2,1)S(1)} %copy-done, bf16[384,512]{1,0:T(8,128)(2,1)S(1)} %get-tuple-element.64.attn_ref, ...), custom_call_target="tpu_custom_call" | custom-call | flops 1 | bytes 1 | tf_op jit(solution)/shard_map/near/pallas_call | solution.py:59
  52.3 2.8 %collective-permute-start.8 = (bf16[384,1024]{1,0:T(8,128)(2,1)}, bf16[384,1024]{1,0:T(8,128)(2,1)}, u32[]{:S(2)}, u32[]{:S(2)}) collective-permute-start(bf16[384,1024]{1,0:T(8,128)(2,1)} %get-tuple-element.75), channel_id=1, source_target_pairs={{0,3},{1,0},{2,1},{3,2},{4,7},{5,4},{6,5},{7,6},{8,11},{9,8},{10,9... | collective-permute-start | bytes 2359304 | tf_op jit(solution)/shard_map/ppermute | solution.py:43
  55.2 2.6 %merge.2 = (bf16[384,256]{1,0:T(8,128)(2,1)S(1)}, bf16[384,256]{1,0:T(8,128)(2,1)}, bf16[384,256]{1,0:T(8,128)(2,1)}, bf16[384,256]{1,0:T(8,128)(2,1)}, f32[8,128]{1,0:T(8,128)S(1)}) custom-call(s32[4]{0:T(128)S(1)} %pad_add_fusion.where_ref.token_ref, f32[8,128]{1,0:T(8,128)S(1)} %get-tuple-element.66.token_ref, ...), custom_call_target="tpu_custom_call" | custom-call | flops 1 | bytes 1 | tf_op jit(solution)/shard_map/merge/pallas_call | solution.py:59
  57.8 2.6 %collective-permute-start.10 = (bf16[384,256]{1,0:T(8,128)(2,1)}, bf16[384,256]{1,0:T(8,128)(2,1)}, u32[]{:S(2)}, u32[]{:S(2)}) collective-permute-start(bf16[384,256]{1,0:T(8,128)(2,1)} %get-tuple-element.80), channel_id=1, source_target_pairs={{0,4},{1,5},{2,6},{3,7},{4,8},{5,9},{6,10},{7,11},{8,12},{9,13},{1... | collective-permute-start | bytes 589832 | tf_op jit(solution)/shard_map/ppermute | solution.py:43
  60.4 1.5 %collective-permute-start.11 = (bf16[384,256]{1,0:T(8,128)(2,1)}, bf16[384,256]{1,0:T(8,128)(2,1)}, u32[]{:S(2)}, u32[]{:S(2)}) collective-permute-start(bf16[384,256]{1,0:T(8,128)(2,1)} %get-tuple-element.81), channel_id=1, source_target_pairs={{0,12},{1,13},{2,14},{3,15},{4,0},{5,1},{6,2},{7,3},{8,4},{9,5},{1... | collective-permute-start | bytes 589832 | tf_op jit(solution)/shard_map/ppermute | solution.py:43
  61.9 3.5 %collective-permute-start.12 = (bf16[384,256]{1,0:T(8,128)(2,1)}, bf16[384,256]{1,0:T(8,128)(2,1)}, u32[]{:S(2)}, u32[]{:S(2)}) collective-permute-start(bf16[384,256]{1,0:T(8,128)(2,1)} %get-tuple-element.82), channel_id=1, source_target_pairs={{0,8},{1,9},{2,10},{3,11},{4,12},{5,13},{6,14},{7,15},{8,0},{9,1},... | collective-permute-start | bytes 589832 | tf_op jit(solution)/shard_map/ppermute | solution.py:43
  65.5 1.4 %merge_both.1 = (bf16[256,256]{1,0:T(8,128)(2,1)S(1)}, bf16[256,256]{1,0:T(8,128)(2,1)S(1)}, bf16[256,256]{1,0:T(8,128)(2,1)S(1)}, bf16[256,256]{1,0:T(8,128)(2,1)}, f32[8,128]{1,0:T(8,128)S(1)}) custom-call(s32[4]{0:T(128)S(1)} %pad_add_fusion.where_ref.token_ref, f32[8,128]{1,0:T(8,128)S(1)} %get-tuple-element.69.token_ref, ...), custom_call_target="tpu_custom_call" | custom-call | flops 199999995904 | bytes 1 | tf_op jit(solution)/shard_map/merge_both/pallas_call | solution.py:59
  66.8 5.1 %collective-permute-done.9.behind_ref = bf16[384,1024]{1,0:T(8,128)(2,1)} collective-permute-done((bf16[384,1024]{1,0:T(8,128)(2,1)}, bf16[384,1024]{1,0:T(8,128)(2,1)}, u32[]{:S(2)}, u32[]{:S(2)}) %collective-permute-start.9) | collective-permute-done | bytes 786464 | tf_op jit(solution)/shard_map/ppermute | solution.py:43
  71.9 2.2 %merge.3 = (bf16[384,256]{1,0:T(8,128)(2,1)S(1)}, bf16[384,256]{1,0:T(8,128)(2,1)S(1)}, bf16[384,256]{1,0:T(8,128)(2,1)S(1)}, bf16[384,256]{1,0:T(8,128)(2,1)S(1)}, f32[8,128]{1,0:T(8,128)S(1)}) custom-call(s32[4]{0:T(128)S(1)} %pad_add_fusion.where_ref.token_ref, f32[8,128]{1,0:T(8,128)S(1)} %get-tuple-element.73.token_ref, ...), custom_call_target="tpu_custom_call" | custom-call | flops 1 | bytes 1 | tf_op jit(solution)/shard_map/merge/pallas_call | solution.py:59
  74.2 3.0 %collective-permute-start.15 = (bf16[256,256]{1,0:T(8,128)(2,1)S(1)}, bf16[256,256]{1,0:T(8,128)(2,1)S(1)}, u32[]{:S(2)}, u32[]{:S(2)}) collective-permute-start(bf16[256,256]{1,0:T(8,128)(2,1)S(1)} %get-tuple-element.91), channel_id=1, source_target_pairs={{0,2},{1,3},{2,0},{3,1},{4,6},{5,7},{6,4},{7,5},{8,10},{9,11},{10,... | collective-permute-start | bytes 393224 | tf_op jit(solution)/shard_map/ppermute | solution.py:43
  77.1 1.7 %collective-permute-start.16 = (bf16[384,256]{1,0:T(8,128)(2,1)S(1)}, bf16[384,256]{1,0:T(8,128)(2,1)S(1)}, u32[]{:S(2)}, u32[]{:S(2)}) collective-permute-start(bf16[384,256]{1,0:T(8,128)(2,1)S(1)} %get-tuple-element.95), channel_id=1, source_target_pairs={{0,4},{1,5},{2,6},{3,7},{4,8},{5,9},{6,10},{7,11},{8,12},{9,13},{1... | collective-permute-start | bytes 589832 | tf_op jit(solution)/shard_map/ppermute | solution.py:43
  78.9 1.8 %collective-permute-done.15.rest_2_ = bf16[256,256]{1,0:T(8,128)(2,1)S(1)} collective-permute-done((bf16[256,256]{1,0:T(8,128)(2,1)S(1)}, bf16[256,256]{1,0:T(8,128)(2,1)S(1)}, u32[]{:S(2)}, u32[]{:S(2)}) %collective-permute-start.15) | collective-permute-done | bytes 131104 | tf_op jit(solution)/shard_map/ppermute | solution.py:43
  80.7 1.8 %collective-permute-start.17 = (bf16[384,256]{1,0:T(8,128)(2,1)S(1)}, bf16[384,256]{1,0:T(8,128)(2,1)S(1)}, u32[]{:S(2)}, u32[]{:S(2)}) collective-permute-start(bf16[384,256]{1,0:T(8,128)(2,1)S(1)} %get-tuple-element.96), channel_id=1, source_target_pairs={{0,12},{1,13},{2,14},{3,15},{4,0},{5,1},{6,2},{7,3},{8,4},{9,5},{1... | collective-permute-start | bytes 589832 | tf_op jit(solution)/shard_map/ppermute | solution.py:43
  82.5 3.7 %collective-permute-start.18 = (bf16[384,256]{1,0:T(8,128)(2,1)S(1)}, bf16[384,256]{1,0:T(8,128)(2,1)S(1)}, u32[]{:S(2)}, u32[]{:S(2)}) collective-permute-start(bf16[384,256]{1,0:T(8,128)(2,1)S(1)} %get-tuple-element.97), channel_id=1, source_target_pairs={{0,8},{1,9},{2,10},{3,11},{4,12},{5,13},{6,14},{7,15},{8,0},{9,1},... | collective-permute-start | bytes 589832 | tf_op jit(solution)/shard_map/ppermute | solution.py:43
  86.2 3.0 %collective-permute-start.14 = (bf16[256,256]{1,0:T(8,128)(2,1)}, bf16[256,256]{1,0:T(8,128)(2,1)S(1)}, u32[]{:S(2)}, u32[]{:S(2)}) collective-permute-start(bf16[256,256]{1,0:T(8,128)(2,1)} %get-tuple-element.89), channel_id=1, source_target_pairs={{0,3},{1,0},{2,1},{3,2},{4,7},{5,4},{6,5},{7,6},{8,11},{9,8},{10,9... | collective-permute-start | bytes 393224 | tf_op jit(solution)/shard_map/ppermute | solution.py:43
  89.9 1.9 %final.3 = (bf16[384,256]{1,0:T(8,128)(2,1)S(1)}, f32[384,1]{1,0:T(8,128)S(1)}, f32[8,128]{1,0:T(8,128)S(1)}) custom-call(s32[4]{0:T(128)S(1)} %pad_add_fusion.where_ref.token_ref, f32[8,128]{1,0:T(8,128)S(1)} %get-tuple-element.78.token_ref, bf16[1024,256]{1,0:T(8,128)(2,1)S(1)} %copy-done.1, bf16[384,256]{1,0:T(8,128)(2,1)S(1)} %get-tuple-element.79.parts_ref, ...), custom_call_target="tpu_custom_call" | custom-call | flops 1 | bytes 1 | tf_op jit(solution)/shard_map/final/pallas_call | solution.py:59
  92.0 3.3 %collective-permute-done.13.rest_0_ = bf16[256,256]{1,0:T(8,128)(2,1)S(1)} collective-permute-done((bf16[256,256]{1,0:T(8,128)(2,1)S(1)}, bf16[256,256]{1,0:T(8,128)(2,1)S(1)}, u32[]{:S(2)}, u32[]{:S(2)}) %collective-permute-start.13) | collective-permute-done | bytes 131104 | tf_op jit(solution)/shard_map/ppermute | solution.py:43
  97.0 1.3 %final.5 = (bf16[384,256]{1,0:T(8,128)(2,1)S(1)}, f32[384,1]{1,0:T(8,128)S(1)}, f32[8,128]{1,0:T(8,128)}) custom-call(s32[4]{0:T(128)S(1)} %pad_add_fusion.where_ref.token_ref, f32[8,128]{1,0:T(8,128)S(1)} %get-tuple-element.93.token_ref, bf16[1024,256]{1,0:T(8,128)(2,1)S(1)} %copy-done.1, bf16[384,256]{1,0:T(8,128)(2,1)S(1)} %get-tuple-element.94.parts_ref, ...), custom_call_target="tpu_custom_call" | custom-call | flops 1 | bytes 1 | tf_op jit(solution)/shard_map/final/pallas_call | solution.py:59
  99.2 5.3 %all-to-all-start = ((f32[16,8,128]{2,1,0:T(8,128)}), f32[16,8,128]{2,1,0:T(8,128)S(1)}, u32[]{:S(2)}, u32[]{:S(2)}) async-start(f32[16,8,128]{2,1,0:T(8,128)} %tile.9), calls=%async_computation | async-start | bytes 131072 | tf_op jit(solution)/shard_map/all_to_all | solution.py:430
  104.6 10.0 %all-to-all-done = f32[16,8,128]{2,1,0:T(8,128)S(1)} async-done(((f32[16,8,128]{2,1,0:T(8,128)}), f32[16,8,128]{2,1,0:T(8,128)S(1)}, u32[]{:S(2)}, u32[]{:S(2)}) %all-to-all-start) | async-done | bytes 65568 | tf_op jit(solution)/shard_map/all_to_all | solution.py:430
  (39 shorter events, 5.5 us)
Async XLA Ops:
  0.7 7.9 %copy-start = (bf16[512,4096]{1,0:T(8,128)(2,1)S(1)}, bf16[512,4096]{1,0:T(8,128)(2,1)}, u32[]{:S(2)}) copy-start(bf16[512,4096]{1,0:T(8,128)(2,1)} %w_ref.5) | copy-start | bytes 12582916
  5.8 23.9 %collective-permute-start = (bf16[384,1024]{1,0:T(8,128)(2,1)S(1)}, bf16[384,1024]{1,0:T(8,128)(2,1)S(1)}, u32[]{:S(2)}, u32[]{:S(2)}) collective-permute-start(bf16[384,1024]{1,0:T(8,128)(2,1)S(1)} %get-tuple-element.56), channel_id=1, source_target_pairs={{0,3},{1,0},{2,1},{3,2},{4,7},{5,4},{6,5},{7,6},{8,11},{9,8},{10,9... | collective-permute-start | bytes 2359304 | tf_op jit(solution)/shard_map/ppermute | solution.py:43
  8.7 21.1 %collective-permute-start.1 = (bf16[384,1024]{1,0:T(8,128)(2,1)S(1)}, bf16[384,1024]{1,0:T(8,128)(2,1)S(1)}, u32[]{:S(2)}, u32[]{:S(2)}) collective-permute-start(bf16[384,1024]{1,0:T(8,128)(2,1)S(1)} %get-tuple-element.58), channel_id=1, source_target_pairs={{0,1},{1,2},{2,3},{3,0},{4,5},{5,6},{6,7},{7,4},{8,9},{9,10},{10,1... | collective-permute-start | bytes 2359304 | tf_op jit(solution)/shard_map/ppermute | solution.py:43
  12.7 22.5 %collective-permute-start.2 = (bf16[256,1024]{1,0:T(8,128)(2,1)S(1)}, bf16[256,1024]{1,0:T(8,128)(2,1)S(1)}, u32[]{:S(2)}, u32[]{:S(2)}) collective-permute-start(bf16[256,1024]{1,0:T(8,128)(2,1)S(1)} %get-tuple-element.61), channel_id=1, source_target_pairs={{0,4},{1,5},{2,6},{3,7},{4,8},{5,9},{6,10},{7,11},{8,12},{9,13},{1... | collective-permute-start | bytes 1572872 | tf_op jit(solution)/shard_map/ppermute | solution.py:43
  16.0 27.1 %collective-permute-start.3 = (bf16[256,1024]{1,0:T(8,128)(2,1)S(1)}, bf16[256,1024]{1,0:T(8,128)(2,1)S(1)}, u32[]{:S(2)}, u32[]{:S(2)}) collective-permute-start(bf16[256,1024]{1,0:T(8,128)(2,1)S(1)} %get-tuple-element.62), channel_id=1, source_target_pairs={{0,12},{1,13},{2,14},{3,15},{4,0},{5,1},{6,2},{7,3},{8,4},{9,5},{1... | collective-permute-start | bytes 1572872 | tf_op jit(solution)/shard_map/ppermute | solution.py:43
  26.2 22.4 %collective-permute-start.4 = (bf16[384,1024]{1,0:T(8,128)(2,1)}, bf16[384,1024]{1,0:T(8,128)(2,1)}, u32[]{:S(2)}, u32[]{:S(2)}) collective-permute-start(bf16[384,1024]{1,0:T(8,128)(2,1)} %get-tuple-element.65), channel_id=1, source_target_pairs={{0,3},{1,0},{2,1},{3,2},{4,7},{5,4},{6,5},{7,6},{8,11},{9,8},{10,9... | collective-permute-start | bytes 2359304 | tf_op jit(solution)/shard_map/ppermute | solution.py:43
  31.8 23.3 %collective-permute-start.5 = (bf16[384,1024]{1,0:T(8,128)(2,1)}, bf16[384,1024]{1,0:T(8,128)(2,1)}, u32[]{:S(2)}, u32[]{:S(2)}) collective-permute-start(bf16[384,1024]{1,0:T(8,128)(2,1)} %get-tuple-element.68), channel_id=1, source_target_pairs={{0,1},{1,2},{2,3},{3,0},{4,5},{5,6},{6,7},{7,4},{8,9},{9,10},{10,1... | collective-permute-start | bytes 2359304 | tf_op jit(solution)/shard_map/ppermute | solution.py:43
  44.4 16.0 %collective-permute-start.6 = (bf16[256,512]{1,0:T(8,128)(2,1)S(1)}, bf16[256,512]{1,0:T(8,128)(2,1)S(1)}, u32[]{:S(2)}, u32[]{:S(2)}) collective-permute-start(bf16[256,512]{1,0:T(8,128)(2,1)S(1)} %get-tuple-element.71), channel_id=1, source_target_pairs={{0,4},{1,5},{2,6},{3,7},{4,8},{5,9},{6,10},{7,11},{8,12},{9,13},{1... | collective-permute-start | bytes 786440 | tf_op jit(solution)/shard_map/ppermute | solution.py:43
  48.4 13.6 %collective-permute-start.7 = (bf16[256,512]{1,0:T(8,128)(2,1)S(1)}, bf16[256,512]{1,0:T(8,128)(2,1)S(1)}, u32[]{:S(2)}, u32[]{:S(2)}) collective-permute-start(bf16[256,512]{1,0:T(8,128)(2,1)S(1)} %get-tuple-element.72), channel_id=1, source_target_pairs={{0,12},{1,13},{2,14},{3,15},{4,0},{5,1},{6,2},{7,3},{8,4},{9,5},{1... | collective-permute-start | bytes 786440 | tf_op jit(solution)/shard_map/ppermute | solution.py:43
  51.9 20.0 %collective-permute-start.9 = (bf16[384,1024]{1,0:T(8,128)(2,1)}, bf16[384,1024]{1,0:T(8,128)(2,1)}, u32[]{:S(2)}, u32[]{:S(2)}) collective-permute-start(bf16[384,1024]{1,0:T(8,128)(2,1)} %get-tuple-element.77), channel_id=1, source_target_pairs={{0,1},{1,2},{2,3},{3,0},{4,5},{5,6},{6,7},{7,4},{8,9},{9,10},{10,1... | collective-permute-start | bytes 2359304 | tf_op jit(solution)/shard_map/ppermute | solution.py:43
  52.3 19.6 %collective-permute-start.8 = (bf16[384,1024]{1,0:T(8,128)(2,1)}, bf16[384,1024]{1,0:T(8,128)(2,1)}, u32[]{:S(2)}, u32[]{:S(2)}) collective-permute-start(bf16[384,1024]{1,0:T(8,128)(2,1)} %get-tuple-element.75), channel_id=1, source_target_pairs={{0,3},{1,0},{2,1},{3,2},{4,7},{5,4},{6,5},{7,6},{8,11},{9,8},{10,9... | collective-permute-start | bytes 2359304 | tf_op jit(solution)/shard_map/ppermute | solution.py:43
  57.8 24.7 %collective-permute-start.10 = (bf16[384,256]{1,0:T(8,128)(2,1)}, bf16[384,256]{1,0:T(8,128)(2,1)}, u32[]{:S(2)}, u32[]{:S(2)}) collective-permute-start(bf16[384,256]{1,0:T(8,128)(2,1)} %get-tuple-element.80), channel_id=1, source_target_pairs={{0,4},{1,5},{2,6},{3,7},{4,8},{5,9},{6,10},{7,11},{8,12},{9,13},{1... | collective-permute-start | bytes 589832 | tf_op jit(solution)/shard_map/ppermute | solution.py:43
  60.4 25.7 %collective-permute-start.11 = (bf16[384,256]{1,0:T(8,128)(2,1)}, bf16[384,256]{1,0:T(8,128)(2,1)}, u32[]{:S(2)}, u32[]{:S(2)}) collective-permute-start(bf16[384,256]{1,0:T(8,128)(2,1)} %get-tuple-element.81), channel_id=1, source_target_pairs={{0,12},{1,13},{2,14},{3,15},{4,0},{5,1},{6,2},{7,3},{8,4},{9,5},{1... | collective-permute-start | bytes 589832 | tf_op jit(solution)/shard_map/ppermute | solution.py:43
  61.9 27.2 %collective-permute-start.12 = (bf16[384,256]{1,0:T(8,128)(2,1)}, bf16[384,256]{1,0:T(8,128)(2,1)}, u32[]{:S(2)}, u32[]{:S(2)}) collective-permute-start(bf16[384,256]{1,0:T(8,128)(2,1)} %get-tuple-element.82), channel_id=1, source_target_pairs={{0,8},{1,9},{2,10},{3,11},{4,12},{5,13},{6,14},{7,15},{8,0},{9,1},... | collective-permute-start | bytes 589832 | tf_op jit(solution)/shard_map/ppermute | solution.py:43
  65.5 24.4 %copy-start.1 = (bf16[1024,256]{1,0:T(8,128)(2,1)S(1)}, bf16[1024,256]{1,0:T(8,128)(2,1)}, u32[]{:S(2)}) copy-start(bf16[1024,256]{1,0:T(8,128)(2,1)} %residual_ref.5) | copy-start | bytes 1572868
  74.2 6.6 %collective-permute-start.15 = (bf16[256,256]{1,0:T(8,128)(2,1)S(1)}, bf16[256,256]{1,0:T(8,128)(2,1)S(1)}, u32[]{:S(2)}, u32[]{:S(2)}) collective-permute-start(bf16[256,256]{1,0:T(8,128)(2,1)S(1)} %get-tuple-element.91), channel_id=1, source_target_pairs={{0,2},{1,3},{2,0},{3,1},{4,6},{5,7},{6,4},{7,5},{8,10},{9,11},{10,... | collective-permute-start | bytes 393224 | tf_op jit(solution)/shard_map/ppermute | solution.py:43
  77.1 18.9 %collective-permute-start.16 = (bf16[384,256]{1,0:T(8,128)(2,1)S(1)}, bf16[384,256]{1,0:T(8,128)(2,1)S(1)}, u32[]{:S(2)}, u32[]{:S(2)}) collective-permute-start(bf16[384,256]{1,0:T(8,128)(2,1)S(1)} %get-tuple-element.95), channel_id=1, source_target_pairs={{0,4},{1,5},{2,6},{3,7},{4,8},{5,9},{6,10},{7,11},{8,12},{9,13},{1... | collective-permute-start | bytes 589832 | tf_op jit(solution)/shard_map/ppermute | solution.py:43
  80.7 15.3 %collective-permute-start.17 = (bf16[384,256]{1,0:T(8,128)(2,1)S(1)}, bf16[384,256]{1,0:T(8,128)(2,1)S(1)}, u32[]{:S(2)}, u32[]{:S(2)}) collective-permute-start(bf16[384,256]{1,0:T(8,128)(2,1)S(1)} %get-tuple-element.96), channel_id=1, source_target_pairs={{0,12},{1,13},{2,14},{3,15},{4,0},{5,1},{6,2},{7,3},{8,4},{9,5},{1... | collective-permute-start | bytes 589832 | tf_op jit(solution)/shard_map/ppermute | solution.py:43
  82.5 14.5 %collective-permute-start.18 = (bf16[384,256]{1,0:T(8,128)(2,1)S(1)}, bf16[384,256]{1,0:T(8,128)(2,1)S(1)}, u32[]{:S(2)}, u32[]{:S(2)}) collective-permute-start(bf16[384,256]{1,0:T(8,128)(2,1)S(1)} %get-tuple-element.97), channel_id=1, source_target_pairs={{0,8},{1,9},{2,10},{3,11},{4,12},{5,13},{6,14},{7,15},{8,0},{9,1},... | collective-permute-start | bytes 589832 | tf_op jit(solution)/shard_map/ppermute | solution.py:43
  86.2 5.8 %collective-permute-start.14 = (bf16[256,256]{1,0:T(8,128)(2,1)}, bf16[256,256]{1,0:T(8,128)(2,1)S(1)}, u32[]{:S(2)}, u32[]{:S(2)}) collective-permute-start(bf16[256,256]{1,0:T(8,128)(2,1)} %get-tuple-element.89), channel_id=1, source_target_pairs={{0,3},{1,0},{2,1},{3,2},{4,7},{5,4},{6,5},{7,6},{8,11},{9,8},{10,9... | collective-permute-start | bytes 393224 | tf_op jit(solution)/shard_map/ppermute | solution.py:43
  89.1 6.2 %collective-permute-start.13 = (bf16[256,256]{1,0:T(8,128)(2,1)S(1)}, bf16[256,256]{1,0:T(8,128)(2,1)S(1)}, u32[]{:S(2)}, u32[]{:S(2)}) collective-permute-start(bf16[256,256]{1,0:T(8,128)(2,1)S(1)} %get-tuple-element.87), channel_id=1, source_target_pairs={{0,1},{1,2},{2,3},{3,0},{4,5},{5,6},{6,7},{7,4},{8,9},{9,10},{10,1... | collective-permute-start | bytes 393224 | tf_op jit(solution)/shard_map/ppermute | solution.py:43
  99.2 15.4 %all-to-all-start = ((f32[16,8,128]{2,1,0:T(8,128)}), f32[16,8,128]{2,1,0:T(8,128)S(1)}, u32[]{:S(2)}, u32[]{:S(2)}) async-start(f32[16,8,128]{2,1,0:T(8,128)} %tile.9), calls=%async_computation | async-start | bytes 131072 | tf_op jit(solution)/shard_map/all_to_all | solution.py:430
  104.6 11.1 %copy-start.2 = (bf16[1024,256]{1,0:T(8,128)(2,1)}, bf16[1024,256]{1,0:T(8,128)(2,1)S(1)}, u32[]{:S(2)}) copy-start(bf16[1024,256]{1,0:T(8,128)(2,1)S(1)} %constant_dynamic-update-slice_fusion) | copy-start | bytes 1572868
